TPU v7x, 32 devices: a whole 2x2x4 slice. The times are simulated.
32 devices in a mesh: dp: 4 (over x, core), space: 8 (over z, y).
Axes of the slice: x: 2, y: 2, z: 4, core: 2. Of those that a mesh axis runs over, the one named last changes fastest.
Arguments:
- features: bfloat16 [4, 65536, 128], P('dp', 'space'), may hold values from -6 to 6
- child_parent: int32 [4, 65536], P('dp', 'space'), may hold values from 0 to 16383, as said below
- child_code: int32 [4, 65536], P('dp', 'space'), may hold values from 0 to 7
- weight: bfloat16 [8, 128, 128], replicated, may hold values from -0.25 to 0.25
- out_grad: bfloat16 [4, 16384, 128], P('dp', 'space'), may hold values from -6 to 6
Outputs:
- parent_out: bfloat16 [4, 16384, 128], P('dp', 'space')
- feature_grad: bfloat16 [4, 65536, 128], P('dp', 'space')
- weight_grad: float32 [8, 128, 128], replicated
Inputs may be any that keep to these rules, and one draw needn't show every extreme that they name: Within one window, child_parent is nondecreasing along the 8192 rows of one device of space. Parent p lies on device p // 2048 of space; at most 2048 rows of one device have their parent on one device, and on every device some device receives exactly 2048. No two fine octants of a window share both parent and child_code.
All inputs are finite; a program needn't handle non-finite values.
Results may differ from a plain program's by a relative error of at most 0.001.
Values may be sent and summed in bfloat16 or wider, within the bound.
No kernel may reach another device: no remote copies, remote signals or barrier semaphores. Data moves between devices by JAX's collectives and lax.ppermute only.
A program may use at most 128 MiB of HBM per device.

v0:
```python
import jax
import jax.numpy as jnp
from jax import lax
from jax.sharding import PartitionSpec as P


def gather_blocks(rows, starts, capacity):
    extended = jnp.concatenate([rows, jnp.zeros((capacity,) + rows.shape[1:], rows.dtype)], axis=0)

    def window(offset):
        return lax.dynamic_slice_in_dim(extended, offset, capacity, 0)

    return jax.vmap(window)(starts)


def spread_blocks(blocks, starts, row_count):
    capacity = blocks.shape[1]
    channels = blocks.shape[2]
    canvas = jnp.zeros((row_count + capacity, channels), blocks.dtype)
    numbers = lax.ScatterDimensionNumbers(
        update_window_dims=(1, 2), inserted_window_dims=(), scatter_dims_to_operand_dims=(0,)
    )
    placed = lax.scatter_add(canvas, starts[:, None], blocks, numbers)
    return placed[:row_count]


def per_device(features, child_parent, child_code, weight, out_grad):
    fine_rows = features[0]
    parents = child_parent[0]
    child_kinds = child_code[0]
    cotangent = out_grad[0]
    row_count = fine_rows.shape[0]
    par_rows = cotangent.shape[0]
    kinds_total = weight.shape[0]
    chan_in = weight.shape[1]
    chan_out = weight.shape[2]
    space_size = lax.axis_size("space")
    capacity = 2 * row_count // space_size
    owners = parents // par_rows
    local_slot = (parents - owners * par_rows) * kinds_total + child_kinds
    counts = jnp.sum((owners[:, None] == jnp.arange(space_size)[None, :]).astype(jnp.int32), axis=0)
    starts = jnp.cumsum(counts) - counts
    slot_lane = jnp.arange(capacity)
    live_mask = slot_lane[None, :] < counts[:, None]
    marker = kinds_total * par_rows
    slot_blocks = gather_blocks(local_slot[:, None], starts, capacity)[:, :, 0]
    send_slots = jnp.where(live_mask, slot_blocks, marker)
    weight_flat = weight.reshape(kinds_total * chan_in, chan_out)
    feat_blocks = gather_blocks(fine_rows, starts, capacity)
    send_feats = jnp.where(live_mask[:, :, None], feat_blocks, jnp.zeros((), jnp.bfloat16))
    recv_feats, recv_slots = (
        lax.all_to_all(send_feats, "space", split_axis=0, concat_axis=0, tiled=True),
        lax.all_to_all(send_slots, "space", split_axis=0, concat_axis=0, tiled=True),
    )
    slot_grid = (
        jnp.zeros((marker, chan_in), jnp.bfloat16)
        .at[recv_slots.reshape(-1)]
        .set(recv_feats.reshape(-1, chan_in), mode="drop")
    )
    slot_grid = slot_grid.reshape(par_rows, kinds_total * chan_in)
    result = jnp.dot(slot_grid, weight_flat, preferred_element_type=jnp.float32).astype(
        jnp.bfloat16
    )
    parent_grad = jnp.dot(cotangent, weight_flat.T, preferred_element_type=jnp.float32).astype(
        jnp.bfloat16
    )
    parent_grad = parent_grad.reshape(marker, chan_in)
    back_rows = jnp.take(parent_grad, recv_slots, axis=0, mode="fill", fill_value=0)
    returned = lax.all_to_all(back_rows, "space", split_axis=0, concat_axis=0, tiled=True)
    feature_grad = spread_blocks(returned, starts, row_count)
    weight_term = lax.dot_general(
        slot_grid, cotangent, (((0,), (0,)), ((), ())), preferred_element_type=jnp.float32
    )
    summed_terms = lax.psum(weight_term, ("dp", "space"))
    total_rows = row_count * space_size * lax.axis_size("dp")
    weight_grad = (summed_terms / jnp.sqrt(jnp.float32(total_rows))).reshape(
        kinds_total, chan_in, chan_out
    )
    return (result[None], feature_grad[None], weight_grad)


def solution(mesh):
    placed = (
        P("dp", "space", None),
        P("dp", "space"),
        P("dp", "space"),
        P(),
        P("dp", "space", None),
    )
    return jax.shard_map(
        per_device,
        mesh=mesh,
        in_specs=placed,
        out_specs=(P("dp", "space", None), P("dp", "space", None), P()),
        check_vma=False,
    )
```

profile of v0, /device:TPU:0, one launch (start us, length us, event | category | flops | bytes accessed | tf_op | source)
XLA Modules:
  0.0 361.1 jit_solution(6928677446499418560)
XLA Ops:
  7.2 0.8 add_select_fusion.1
  8.4 1.0 bitcast_add_fusion
  9.4 10.7 %while.6 = (s32[]{:T(128)}, s32[10240,1]{0,1:T(1,128)S(1)}, s32[8,2]{0,1:T(2,128)S(1)}, s32[8,2048,1]{1,2,0:T(1,128)S(1)}) while((s32[]{:T(128)}, s32[10240,1]{0,1:T(1,128)S(1)}, s32[8,2]{0,1:T(2,128)S(1)}, s32[8,2048,1]{1,2,0:T(1,128)S(1)}) %tuple.52), condition=%wide.while_cond.clone, body=%wide.while_body.sunk.clone | while | flops 2 | bytes 16473 | solution.py:11
  10.0 0.7 bitcast_dynamic-update-slice_fusion.6
  11.4 0.7 bitcast_dynamic-update-slice_fusion.6
  12.7 0.7 bitcast_dynamic-update-slice_fusion.6
  14.0 0.7 bitcast_dynamic-update-slice_fusion.6
  15.4 0.7 bitcast_dynamic-update-slice_fusion.6
  16.7 0.7 bitcast_dynamic-update-slice_fusion.6
  19.4 0.7 bitcast_dynamic-update-slice_fusion.6
  20.1 0.8 compare_select_fusion.2
  20.9 7.3 %all-to-all-start = ((s32[8,1,2048]{2,1,0:T(1,128)}), s32[8,1,2048]{2,1,0:T(1,128)S(1)}, u32[]{:S(2)}, u32[]{:S(2)}) async-start(s32[8,1,2048]{2,1,0:T(1,128)} %compare_select_fusion.2), calls=%async_computation | async-start | bytes 131072 | tf_op jit(solution)/shard_map/all_to_all | solution.py:53
  28.3 1.8 concatenate.12
  30.1 17.9 %while.7 = (s32[]{:T(128)}, bf16[10240,128]{1,0:T(8,128)(2,1)S(1)}, s32[8,2]{0,1:T(2,128)S(1)}, bf16[8,2048,128]{2,1,0:T(8,128)(2,1)}) while((s32[]{:T(128)}, bf16[10240,128]{1,0:T(8,128)(2,1)S(1)}, s32[8,2]{0,1:T(2,128)S(1)}, bf16[8,2048,128]{2,1,0:T(8,128)(2,1)}) %tuple.63), condition=%wide.while_cond.1.clone, body=%wide.while_body.1.sunk.clone | while | flops 2 | bytes 1049681 | solution.py:11
  30.8 1.6 bitcast_dynamic-update-slice_fusion.7
  33.0 1.6 bitcast_dynamic-update-slice_fusion.7
  35.2 1.6 bitcast_dynamic-update-slice_fusion.7
  37.5 1.6 bitcast_dynamic-update-slice_fusion.7
  39.7 1.6 bitcast_dynamic-update-slice_fusion.7
  41.9 1.6 bitcast_dynamic-update-slice_fusion.7
  44.1 1.6 bitcast_dynamic-update-slice_fusion.7
  46.4 1.6 bitcast_dynamic-update-slice_fusion.7
  48.0 7.7 %broadcast_select_fusion.1 = bf16[8,2048,128]{2,1,0:T(8,128)(2,1)} fusion(bf16[8,2048,128]{2,1,0:T(8,128)(2,1)} %get-tuple-element.18, pred[8,2048]{1,0:T(8,128)(4,1)S(1)} %iota_compare_fusion.1), kind=kLoop, calls=%fused_computation.9 | loop fusion | flops 2097152 | bytes 8404992 | tf_op jit(solution)/shard_map/jit(_where)/select_n | solution.py:50
  55.6 6.1 %all-to-all-start.1 = ((bf16[8,2048,128]{2,1,0:T(8,128)(2,1)}), bf16[8,2048,128]{2,1,0:T(8,128)(2,1)}, u32[]{:S(2)}, u32[]{:S(2)}) async-start(bf16[8,2048,128]{2,1,0:T(8,128)(2,1)} %broadcast_select_fusion.1), calls=%async_computation.1 | async-start | bytes 8388608 | tf_op jit(solution)/shard_map/all_to_all | solution.py:52
  61.8 3.2 convolution_convert_fusion
  65.0 7.3 %reshape.281 = bf16[16384,128]{1,0:T(8,128)(2,1)} reshape(bf16[2048,1024]{1,0:T(8,128)(2,1)} %convolution_convert_fusion) | data formatting | bytes 8388608 | tf_op jit(solution)/shard_map/reshape | solution.py:67
  72.4 58.1 %gather_fusion = bf16[16384,128]{1,0:T(8,128)(2,1)} fusion(bf16[16384,128]{1,0:T(8,128)(2,1)} %reshape.281, s32[16384]{0:T(1024)S(1)} %broadcast_clamp_fusion), kind=kCustom, calls=%fused_computation | custom fusion | bytes 8454144 | tf_op jit(solution)/shard_map/jit(_take)/gather | solution.py:68
  130.5 7.7 %broadcast_select_fusion = bf16[8,2048,128]{2,1,0:T(8,128)(2,1)} fusion(bf16[8,2048,128]{2,1,0:T(8,128)(2,1)} %bitcast.79, pred[8,2048]{1,0:T(8,128)(4,1)S(1)} %compare_and_fusion), kind=kLoop, calls=%fused_computation.8 | loop fusion | flops 2097152 | bytes 8404992 | tf_op jit(solution)/shard_map/jit(_take)/select_n | solution.py:68
  138.2 16.3 %all-to-all-done.1 = bf16[8,2048,128]{2,1,0:T(8,128)(2,1)} async-done(((bf16[8,2048,128]{2,1,0:T(8,128)(2,1)}), bf16[8,2048,128]{2,1,0:T(8,128)(2,1)}, u32[]{:S(2)}, u32[]{:S(2)}) %all-to-all-start.1) | async-done | bytes 4194336 | tf_op jit(solution)/shard_map/all_to_all | solution.py:52
  154.5 4.5 %all-to-all-start.2 = ((bf16[8,2048,128]{2,1,0:T(8,128)(2,1)}), bf16[8,2048,128]{2,1,0:T(8,128)(2,1)}, u32[]{:S(2)}, u32[]{:S(2)}) async-start(bf16[8,2048,128]{2,1,0:T(8,128)(2,1)} %broadcast_select_fusion), calls=%async_computation.2 | async-start | bytes 8388608 | tf_op jit(solution)/shard_map/all_to_all | solution.py:69
  159.2 44.0 %scatter_custom_fusion = bf16[16384,128]{1,0:T(8,128)(2,1)} fusion(s32[16384]{0:T(1024)S(1)} %bitcast.87, bf16[16384,128]{1,0:T(8,128)(2,1)} %bitcast.8, bf16[]{:T(256)} %constant.17.clone.1), kind=kCustom, calls=%fused_computation.14 | custom fusion | bytes 4194816 | tf_op jit(solution)/shard_map/scatter | solution.py:58
  203.2 7.3 %reshape.279 = bf16[2048,1024]{1,0:T(8,128)(2,1)} reshape(bf16[16384,128]{1,0:T(8,128)(2,1)} %scatter_custom_fusion) | data formatting | bytes 8388608 | tf_op jit(solution)/shard_map/reshape | solution.py:60
  210.6 4.3 %fusion.3 = f32[1024,128]{1,0:T(8,128)} fusion(bf16[2048,1024]{1,0:T(8,128)(2,1)} %reshape.279, bf16[1,2048,128]{2,1,0:T(8,128)(2,1)S(1)} %copy-done), kind=kOutput, calls=%fused_computation.16 | convolution fusion | flops 536870912 | bytes 5242880 | tf_op jit(solution)/shard_map/dot_general | solution.py:71
  214.9 4.2 %fusion = bf16[1,2048,128]{2,1,0:T(8,128)(2,1)} fusion(bf16[2048,1024]{1,0:T(8,128)(2,1)} %reshape.279, bf16[1024,128]{1,0:T(8,128)(2,1)S(1)} %bitcast.82), kind=kOutput, calls=%fused_computation.12 | convolution fusion | flops 537133056 | bytes 4980736 | tf_op jit(solution)/shard_map/dot_general | solution.py:61
  219.1 35.0 %all-to-all-done.2 = bf16[8,2048,128]{2,1,0:T(8,128)(2,1)} async-done(((bf16[8,2048,128]{2,1,0:T(8,128)(2,1)}), bf16[8,2048,128]{2,1,0:T(8,128)(2,1)}, u32[]{:S(2)}, u32[]{:S(2)}) %all-to-all-start.2) | async-done | bytes 4194336 | tf_op jit(solution)/shard_map/all_to_all | solution.py:69
  254.1 1.7 broadcast_in_dim.57
  255.8 71.9 %while.8 = (s32[]{:T(128)}, bf16[10240,128]{1,0:T(8,128)(2,1)}, s32[8]{0:T(128)S(1)}, bf16[8,2048,128]{2,1,0:T(8,128)(2,1)}, s32[2]{0:T(128)S(1)}, /*index=5*/s32[1]{0:T(128)}) while((s32[]{:T(128)}, bf16[10240,128]{1,0:T(8,128)(2,1)}, s32[8]{0:T(128)S(1)}, bf16[8,2048,128]{2,1,0:T(8,128)(2,1)}, s32[2]{0:T(128)S(1)}, ...), condition=%wide.while_cond.2.clone, body=%wide.while_body.2.sunk.clone | while | flops 1310731 | bytes 2621551 | solution.py:23
  256.4 1.3 and_reduce_fusion.3
  257.8 2.6 add_select_fusion.4
  260.4 4.4 %dynamic-update-slice.16 = bf16[10240,128]{1,0:T(8,128)(2,1)} dynamic-update-slice(bf16[10240,128]{1,0:T(8,128)(2,1)} %get-tuple-element.196, bf16[2048,128]{1,0:T(8,128)(2,1)S(1)} %add_select_fusion.4, s32[]{:T(128)} %bitcast.78, s32[]{:T(128)} %constant.22.clone.1..sunk.1) | dynamic-update-slice | bytes 1048580 | tf_op jit(solution)/shard_map/scatter-add
  265.4 1.3 and_reduce_fusion.3
  266.8 2.6 add_select_fusion.4
  269.4 4.4 %dynamic-update-slice.16 = bf16[10240,128]{1,0:T(8,128)(2,1)} dynamic-update-slice(bf16[10240,128]{1,0:T(8,128)(2,1)} %get-tuple-element.196, bf16[2048,128]{1,0:T(8,128)(2,1)S(1)} %add_select_fusion.4, s32[]{:T(128)} %bitcast.78, s32[]{:T(128)} %constant.22.clone.1..sunk.1) | dynamic-update-slice | bytes 1048580 | tf_op jit(solution)/shard_map/scatter-add
  274.4 1.3 and_reduce_fusion.3
  275.7 2.6 add_select_fusion.4
  278.4 4.5 %dynamic-update-slice.16 = bf16[10240,128]{1,0:T(8,128)(2,1)} dynamic-update-slice(bf16[10240,128]{1,0:T(8,128)(2,1)} %get-tuple-element.196, bf16[2048,128]{1,0:T(8,128)(2,1)S(1)} %add_select_fusion.4, s32[]{:T(128)} %bitcast.78, s32[]{:T(128)} %constant.22.clone.1..sunk.1) | dynamic-update-slice | bytes 1048580 | tf_op jit(solution)/shard_map/scatter-add
  283.4 1.3 and_reduce_fusion.3
  284.7 2.6 add_select_fusion.4
  287.4 4.4 %dynamic-update-slice.16 = bf16[10240,128]{1,0:T(8,128)(2,1)} dynamic-update-slice(bf16[10240,128]{1,0:T(8,128)(2,1)} %get-tuple-element.196, bf16[2048,128]{1,0:T(8,128)(2,1)S(1)} %add_select_fusion.4, s32[]{:T(128)} %bitcast.78, s32[]{:T(128)} %constant.22.clone.1..sunk.1) | dynamic-update-slice | bytes 1048580 | tf_op jit(solution)/shard_map/scatter-add
  292.4 1.3 and_reduce_fusion.3
  293.7 2.6 add_select_fusion.4
  296.4 4.4 %dynamic-update-slice.16 = bf16[10240,128]{1,0:T(8,128)(2,1)} dynamic-update-slice(bf16[10240,128]{1,0:T(8,128)(2,1)} %get-tuple-element.196, bf16[2048,128]{1,0:T(8,128)(2,1)S(1)} %add_select_fusion.4, s32[]{:T(128)} %bitcast.78, s32[]{:T(128)} %constant.22.clone.1..sunk.1) | dynamic-update-slice | bytes 1048580 | tf_op jit(solution)/shard_map/scatter-add
  301.4 1.3 and_reduce_fusion.3
  302.7 2.6 add_select_fusion.4
  305.3 4.4 %dynamic-update-slice.16 = bf16[10240,128]{1,0:T(8,128)(2,1)} dynamic-update-slice(bf16[10240,128]{1,0:T(8,128)(2,1)} %get-tuple-element.196, bf16[2048,128]{1,0:T(8,128)(2,1)S(1)} %add_select_fusion.4, s32[]{:T(128)} %bitcast.78, s32[]{:T(128)} %constant.22.clone.1..sunk.1) | dynamic-update-slice | bytes 1048580 | tf_op jit(solution)/shard_map/scatter-add
  310.4 1.3 and_reduce_fusion.3
  311.7 2.6 add_select_fusion.4
  314.3 4.4 %dynamic-update-slice.16 = bf16[10240,128]{1,0:T(8,128)(2,1)} dynamic-update-slice(bf16[10240,128]{1,0:T(8,128)(2,1)} %get-tuple-element.196, bf16[2048,128]{1,0:T(8,128)(2,1)S(1)} %add_select_fusion.4, s32[]{:T(128)} %bitcast.78, s32[]{:T(128)} %constant.22.clone.1..sunk.1) | dynamic-update-slice | bytes 1048580 | tf_op jit(solution)/shard_map/scatter-add
  319.4 1.3 and_reduce_fusion.3
  320.7 2.6 add_select_fusion.4
  323.3 4.4 %dynamic-update-slice.16 = bf16[10240,128]{1,0:T(8,128)(2,1)} dynamic-update-slice(bf16[10240,128]{1,0:T(8,128)(2,1)} %get-tuple-element.196, bf16[2048,128]{1,0:T(8,128)(2,1)S(1)} %add_select_fusion.4, s32[]{:T(128)} %bitcast.78, s32[]{:T(128)} %constant.22.clone.1..sunk.1) | dynamic-update-slice | bytes 1048580 | tf_op jit(solution)/shard_map/scatter-add
  327.7 3.1 slice_bitcast_fusion
  330.8 21.6 %all-reduce.5.cloned.1.call-done = f32[1024,128]{1,0:T(8,128)} async-done(((f32[1024,128]{1,0:T(8,128)}), f32[1024,128]{1,0:T(8,128)}) %all-reduce.5.cloned.1.call-update) | async-done | bytes 524304 | tf_op jit(solution)/shard_map/psum | solution.py:74
  352.4 1.9 broadcast_multiply_fusion
  (62 shorter events, 16.2 us)
Async XLA Ops:
  7.2 54.6 %copy-start = (bf16[1,2048,128]{2,1,0:T(8,128)(2,1)S(1)}, bf16[1,2048,128]{2,1,0:T(8,128)(2,1)}, u32[]{:S(2)}) copy-start(bf16[1,2048,128]{2,1,0:T(8,128)(2,1)} %param.9) | copy-start | bytes 1572868
  20.9 34.7 %all-to-all-start = ((s32[8,1,2048]{2,1,0:T(1,128)}), s32[8,1,2048]{2,1,0:T(1,128)S(1)}, u32[]{:S(2)}, u32[]{:S(2)}) async-start(s32[8,1,2048]{2,1,0:T(1,128)} %compare_select_fusion.2), calls=%async_computation | async-start | bytes 131072 | tf_op jit(solution)/shard_map/all_to_all | solution.py:53
  55.6 6.1 %copy-start.1 = (bf16[8,128,128]{2,1,0:T(8,128)(2,1)S(1)}, bf16[8,128,128]{2,1,0:T(8,128)(2,1)}, u32[]{:S(2)}) copy-start(bf16[8,128,128]{2,1,0:T(8,128)(2,1)} %param.8) | copy-start | bytes 786436
  55.6 98.9 %all-to-all-start.1 = ((bf16[8,2048,128]{2,1,0:T(8,128)(2,1)}), bf16[8,2048,128]{2,1,0:T(8,128)(2,1)}, u32[]{:S(2)}, u32[]{:S(2)}) async-start(bf16[8,2048,128]{2,1,0:T(8,128)(2,1)} %broadcast_select_fusion.1), calls=%async_computation.1 | async-start | bytes 8388608 | tf_op jit(solution)/shard_map/all_to_all | solution.py:52
  154.5 99.6 %all-to-all-start.2 = ((bf16[8,2048,128]{2,1,0:T(8,128)(2,1)}), bf16[8,2048,128]{2,1,0:T(8,128)(2,1)}, u32[]{:S(2)}, u32[]{:S(2)}) async-start(bf16[8,2048,128]{2,1,0:T(8,128)(2,1)} %broadcast_select_fusion), calls=%async_computation.2 | async-start | bytes 8388608 | tf_op jit(solution)/shard_map/all_to_all | solution.py:69
  159.1 193.4 %all-reduce.5.cloned.1.call-start = ((), (), s32[]{:S(2)}) async-start(), calls=%async_computation.3 | async-start | bytes 1048576 | tf_op jit(solution)/shard_map/psum | solution.py:74
  214.9 41.0 %copy-start.2 = (s32[2]{0:T(128)S(1)}, s32[2]{0:T(128)}, u32[]{:S(2)}) copy-start(s32[2]{0:T(128)} %constant.153) | copy-start | bytes 28
Sparse Core Ops, SparseCore 0:
  215.0 137.3 all-reduce.4
where the time goes:
time: 364 us; the launch traced here: 361 us
  local copies, waits for them, and re-layouts  192 us (53%)
  waiting for transfers between devices  73 us (20%)
  other arithmetic  52.1 us (14%)
  starting transfers between devices  18 us (5%)
  between operations  14.1 us (4%)
  matrix products  11.7 us (3%)
    gather x1, local copies, waits for them, and re-layouts, per_device(): jnp.take(parent_grad, recv_slots, axis=0, mode='fill', fill_value=0)  58.1 us
    scatter x1, local copies, waits for them, and re-layouts, per_device(): slot_grid = jnp.zeros((marker, chan_in), jnp.bfloat16).at[recv_slots.resh...  44 us
    scatter-add x16, local copies, waits for them, and re-layouts  40.2 us
    all_to_all x1, waiting for transfers between devices, per_device(): lax.all_to_all(back_rows, 'space', split_axis=0, concat_axis=0, tiled=True)  35 us
    scatter-add x16, other arithmetic  31.6 us
    gather x48, local copies, waits for them, and re-layouts  28.4 us
    psum x1, waiting for transfers between devices, per_device(): summed_terms = lax.psum(weight_term, ('dp', 'space'))  21.6 us
    all_to_all x1, waiting for transfers between devices, per_device(): lax.all_to_all(send_feats, 'space', split_axis=0, concat_axis=0, tiled=True)  16.3 us
  transfers between devices with their start and end apart: 4, of which 3 were waited for; matrix products, arithmetic and copies ran while one was open for 67% of the time, Pallas kernels for 0%

commit v1 on v0

v1 whole, which is shorter than its diff:
```python
import jax
import jax.numpy as jnp
from jax import lax
from jax.experimental import pallas as pl
from jax.experimental.pallas import tpu as pltpu
from jax.sharding import PartitionSpec as P

LANES = 128
ALIGN = 16
TILE = 256
META = 32
VMEM_LIMIT = 56 * 1024 * 1024


def column(row):
    return jnp.transpose(jnp.broadcast_to(row.astype(jnp.float32), (LANES, LANES))).astype(jnp.int32)


def pack_kernel(capacity, par_rows, count, dest_ref, parent_ref, code_ref, feats_ref, *rest):
    outs = rest[:count]
    parents, codes, meta, sems, meta_sems = rest[count:]
    lines = parent_ref.shape[0]
    fine_rows = lines * LANES
    tail = meta.shape[1]
    parents[...] = jnp.full(parents.shape, 1 << 20, jnp.int32)
    codes[...] = jnp.zeros(codes.shape, jnp.int32)
    parents[0:lines] = parent_ref[...]
    codes[0:lines] = code_ref[...]
    meta[...] = jnp.zeros(meta.shape, meta.dtype)
    copies = []
    offsets = []
    for m in range(count):
        base = dest_ref[m] * par_rows
        start = jnp.sum((parent_ref[...] < base).astype(jnp.int32))
        offset = jnp.minimum(start // ALIGN * ALIGN, fine_rows - capacity)
        offset = pl.multiple_of(offset, ALIGN)
        offsets.append(offset)
        copy = pltpu.make_async_copy(
            feats_ref.at[pl.ds(offset, capacity)], outs[m].at[pl.ds(0, capacity)], sems.at[m]
        )
        copy.start()
        copies.append(copy)
    lane = lax.broadcasted_iota(jnp.int32, (META, LANES), 1)
    for m in range(count):
        base = dest_ref[m] * par_rows
        line = offsets[m] // LANES
        shift = offsets[m] % LANES

        def window(ref):
            here = pltpu.roll(ref[pl.ds(line, META), :], (LANES - shift) % LANES, 1)
            after = pltpu.roll(ref[pl.ds(line + 1, META), :], (LANES - shift) % LANES, 1)
            return jnp.where(lane < LANES - shift, here, after)

        rel = window(parents) - base
        code = window(codes)
        high = jnp.clip(rel >> 4, -1, 256)
        low = (rel & 15) * 8 + code
        meta[m, 0:META] = high.astype(jnp.float32).astype(jnp.bfloat16)
        meta[m, META : 2 * META] = low.astype(jnp.float32).astype(jnp.bfloat16)
        copy = pltpu.make_async_copy(
            meta.at[m], outs[m].at[pl.ds(capacity, tail)], meta_sems.at[m]
        )
        copy.start()
        copies.append(copy)
    for copy in copies:
        copy.wait()


def pack(dests, parents, codes, feats, capacity, par_rows, total):
    count = dests.shape[0]
    lines = parents.shape[0]
    tail = total - capacity
    return pl.pallas_call(
        lambda *refs: pack_kernel(capacity, par_rows, count, *refs),
        out_shape=[jax.ShapeDtypeStruct((total, LANES), jnp.bfloat16)] * count,
        in_specs=[
            pl.BlockSpec(memory_space=pltpu.SMEM),
            pl.BlockSpec(memory_space=pltpu.VMEM),
            pl.BlockSpec(memory_space=pltpu.VMEM),
            pl.BlockSpec(memory_space=pltpu.VMEM),
        ],
        out_specs=[pl.BlockSpec(memory_space=pl.ANY)] * count,
        scratch_shapes=[
            pltpu.VMEM((lines + META + 8, LANES), jnp.int32),
            pltpu.VMEM((lines + META + 8, LANES), jnp.int32),
            pltpu.VMEM((count, tail, LANES), jnp.bfloat16),
            pltpu.SemaphoreType.DMA((count,)),
            pltpu.SemaphoreType.DMA((count,)),
        ],
        compiler_params=pltpu.CompilerParams(vmem_limit_bytes=VMEM_LIMIT),
        cost_estimate=pl.CostEstimate(flops=0, bytes_accessed=2 * count * total * 256, transcendentals=0),
        name="pack_windows",
    )(dests, parents, codes, feats)


def gather_children_kernel(capacity, par_rows, first, last, payload_ref, weight_ref, *rest):
    if first:
        out_ref, total_ref, hilo_ref = rest
    else:
        prior_ref, out_ref, total_ref, hilo_ref = rest
    total_rows = payload_ref.shape[0]
    lines = total_rows // LANES
    chan_out = weight_ref.shape[1] // 8
    high = payload_ref[capacity : capacity + META, :].astype(jnp.float32).astype(jnp.int32)
    low = payload_ref[capacity + META : capacity + 2 * META, :].astype(jnp.float32).astype(jnp.int32)
    rel = high * 16 + (low >> 3)
    code = low & 7
    tiles = par_rows // TILE
    if first:
        total_ref[...] = jnp.zeros(total_ref.shape, jnp.float32)
    else:
        total_ref[:, 0:chan_out] = prior_ref[...]
        total_ref[:, chan_out : 2 * chan_out] = jnp.zeros(prior_ref.shape, jnp.float32)

    def row_tile(row0, line0, span):
        rows = span * LANES
        feats = payload_ref[row0 : row0 + rows, :]
        products = jnp.dot(feats, weight_ref[...], preferred_element_type=jnp.float32)
        kinds = [column(code[line0 + i : line0 + i + 1, :]) for i in range(span)]
        kind = kinds[0] if span == 1 else jnp.concatenate(kinds, axis=0)
        picked = products[:, 0:chan_out]
        for k in range(1, 8):
            picked = jnp.where(kind == k, products[:, k * chan_out : (k + 1) * chan_out], picked)
        upper = picked.astype(jnp.bfloat16)
        lower = (picked - upper.astype(jnp.float32)).astype(jnp.bfloat16)
        both = jnp.concatenate([upper, lower], axis=1)
        spots = rel[line0 : line0 + span, :]
        valid = (spots >= 0) & (spots < par_rows)
        least = jnp.min(jnp.where(valid, spots, par_rows))
        most = jnp.max(jnp.where(valid, spots, -1))
        spot = jnp.concatenate([spots[i : i + 1, :] for i in range(span)], axis=1)
        rank = lax.broadcasted_iota(jnp.int32, (TILE, rows), 0)

        def body(tile, carry):
            base = pl.multiple_of(tile * TILE, TILE)
            hit = jnp.where(rank == spot - base, 1.0, 0.0).astype(jnp.bfloat16)
            total_ref[pl.ds(base, TILE), :] += jnp.dot(hit, both, preferred_element_type=jnp.float32)
            return carry

        lax.fori_loop(least // TILE, (most + TILE) // TILE, body, 0)

    for t in range(lines // 2):
        row_tile(t * TILE, 2 * t, 2)
    if lines % 2:
        row_tile((lines - 1) * LANES, lines - 1, 1)
    out_ref[...] = (total_ref[:, 0:chan_out] + total_ref[:, chan_out : 2 * chan_out]).astype(out_ref.dtype)


def gather_children(payload, weight_wide, prior, capacity, par_rows, last):
    first = prior is None
    chan_out = weight_wide.shape[1] // 8
    args = (payload, weight_wide) if first else (payload, weight_wide, prior)
    return pl.pallas_call(
        lambda *refs: gather_children_kernel(capacity, par_rows, first, last, *refs),
        out_shape=jax.ShapeDtypeStruct((par_rows, chan_out), jnp.bfloat16 if last else jnp.float32),
        in_specs=[pl.BlockSpec(memory_space=pltpu.VMEM)] * len(args),
        out_specs=pl.BlockSpec(memory_space=pltpu.VMEM),
        scratch_shapes=[
            pltpu.VMEM((par_rows, 2 * chan_out), jnp.float32),
            pltpu.VMEM((8, LANES), jnp.float32),
        ],
        compiler_params=pltpu.CompilerParams(vmem_limit_bytes=VMEM_LIMIT),
        cost_estimate=pl.CostEstimate(flops=0, bytes_accessed=27 << 20, transcendentals=0),
        name="gather_children",
    )(*args)


def backward_kernel(blocks, block_ids_ref, parent_ref, code_ref, feats_ref, weight_ref, *rest):
    cots = rest[:blocks]
    out_ref, kernel_ref, cot_ref, sems = rest[blocks:]
    par_rows, chan_out = cot_ref.shape[1:]
    lines = parent_ref.shape[0]
    copies = [
        pltpu.make_async_copy(cots[i], cot_ref.at[block_ids_ref[i]], sems.at[i]) for i in range(blocks)
    ]
    for copy in copies:
        copy.start()
    kernel_ref[...] = jnp.zeros(kernel_ref.shape, jnp.float32)
    for copy in copies:
        copy.wait()
    rank = lax.broadcasted_iota(jnp.int32, (LANES, TILE), 1)

    def row_tile(t, carry):
        lines_here = parent_ref[pl.ds(2 * t, 2), :]
        codes_here = code_ref[pl.ds(2 * t, 2), :]
        least = jnp.min(lines_here[0:1, :])
        most = jnp.max(lines_here[1:2, :])
        spots = [column(lines_here[i : i + 1, :]) for i in range(2)]
        kind = jnp.concatenate([column(codes_here[i : i + 1, :]) for i in range(2)], axis=0)
        wide = [jnp.concatenate([s, s], axis=1) for s in spots]

        def body(tile, rows):
            base = tile * TILE
            hit = jnp.concatenate(
                [jnp.where(rank + base == w, 1.0, 0.0).astype(jnp.bfloat16) for w in wide], axis=0
            )
            block = base // par_rows
            inner = pl.multiple_of(base % par_rows, TILE)
            return rows + jnp.dot(hit, cot_ref[block, pl.ds(inner, TILE), :], preferred_element_type=jnp.float32)

        rows = lax.fori_loop(
            least // TILE, most // TILE + 1, body, jnp.zeros((TILE, chan_out), jnp.float32)
        )
        spread = jnp.concatenate(
            [jnp.where(kind == k, rows, 0.0).astype(jnp.bfloat16) for k in range(8)], axis=1
        )
        here = pl.multiple_of(t * TILE, TILE)
        out_ref[pl.ds(here, TILE), :] = jnp.dot(
            spread, weight_ref[...], preferred_element_type=jnp.float32
        ).astype(out_ref.dtype)
        kernel_ref[...] += lax.dot_general(
            feats_ref[pl.ds(here, TILE), :],
            spread,
            (((0,), (0,)), ((), ())),
            preferred_element_type=jnp.float32,
        )
        return carry

    lax.fori_loop(0, lines // 2, row_tile, 0)


def backward(block_ids, parents, codes, feats, weight_tall, cots):
    blocks = len(cots)
    par_rows, chan_out = cots[0].shape
    chan_in = feats.shape[1]
    vmem = pl.BlockSpec(memory_space=pltpu.VMEM)
    return pl.pallas_call(
        lambda *refs: backward_kernel(blocks, *refs),
        out_shape=[
            jax.ShapeDtypeStruct(feats.shape, jnp.bfloat16),
            jax.ShapeDtypeStruct((chan_in, 8 * chan_out), jnp.float32),
        ],
        in_specs=[pl.BlockSpec(memory_space=pltpu.SMEM), vmem, vmem, vmem, vmem]
        + [pl.BlockSpec(memory_space=pl.ANY)] * blocks,
        out_specs=[vmem, vmem],
        scratch_shapes=[
            pltpu.VMEM((blocks, par_rows, chan_out), jnp.bfloat16),
            pltpu.SemaphoreType.DMA((blocks,)),
        ],
        compiler_params=pltpu.CompilerParams(vmem_limit_bytes=VMEM_LIMIT),
        cost_estimate=pl.CostEstimate(flops=0, bytes_accessed=150 << 20, transcendentals=0),
        name="fine_gradients",
    )(block_ids, parents, codes, feats, weight_tall, *cots)


def reduce_kernel_terms(terms):
    rows = terms.shape[0]
    parts = lax.axis_size("dp") * lax.axis_size("space")
    axes = ("dp", "space")
    pieces = lax.all_to_all(
        terms.reshape(parts, rows // parts, terms.shape[1]), axes, 0, 0, tiled=True
    )
    mine = jnp.sum(pieces, axis=0)
    back = lax.all_to_all(
        jnp.broadcast_to(mine[None], (parts,) + mine.shape), axes, 0, 0, tiled=True
    )
    return back.reshape(terms.shape)


def cycle_of(size):
    return list(range(0, size, 2)) + list(range(size - 1, 0, -2))


def collect_blocks(block, space_size):
    cycle = cycle_of(space_size)
    place = {d: i for i, d in enumerate(cycle)}
    me = lax.axis_index("space")
    spot = jnp.asarray([place[d] for d in range(space_size)], jnp.int32)[me]
    ring = jnp.asarray(cycle, jnp.int32)
    ahead = [(cycle[i], cycle[(i + 1) % space_size]) for i in range(space_size)]
    behind = [(b, a) for a, b in ahead]
    blocks, ids = [block], [me]
    right = left = block
    for step in range(1, space_size // 2 + 1):
        right = lax.ppermute(right, "space", ahead)
        blocks.append(right)
        ids.append(ring[(spot - step) % space_size])
        if step < space_size // 2:
            left = lax.ppermute(left, "space", behind)
            blocks.append(left)
            ids.append(ring[(spot + step) % space_size])
    return blocks, jnp.stack(ids).astype(jnp.int32)


def per_device(features, child_parent, child_code, weight, out_grad):
    fine_rows = features[0]
    row_count = fine_rows.shape[0]
    parents = child_parent[0].reshape(row_count // LANES, LANES)
    codes = child_code[0].reshape(row_count // LANES, LANES)
    cotangent = out_grad[0]
    par_rows = cotangent.shape[0]
    kinds_total, chan_in, chan_out = weight.shape
    space_size = lax.axis_size("space")
    me = lax.axis_index("space")
    capacity = 2 * row_count // space_size + ALIGN
    total = -(-(capacity + 2 * META) // LANES) * LANES
    weight_wide = jnp.transpose(weight, (1, 0, 2)).reshape(chan_in, kinds_total * chan_out)
    weight_tall = jnp.transpose(weight, (0, 2, 1)).reshape(kinds_total * chan_out, chan_in)
    dests = (me ^ jnp.arange(space_size)).astype(jnp.int32)

    payloads = pack(dests, parents, codes, fine_rows, capacity, par_rows, total)
    cotangent, *payloads = lax.optimization_barrier((cotangent, *payloads))
    blocks, ids = collect_blocks(cotangent, space_size)
    arrived = [
        lax.ppermute(payloads[m], "space", [(i, i ^ m) for i in range(space_size)])
        for m in range(1, space_size)
    ]
    feature_grad, term = backward(ids, parents, codes, fine_rows, weight_tall, blocks)
    summed = reduce_kernel_terms(term.reshape(chan_in * kinds_total, chan_out))
    acc = gather_children(payloads[0], weight_wide, None, capacity, par_rows, False)
    for m in range(1, space_size):
        acc = gather_children(
            arrived[m - 1], weight_wide, acc, capacity, par_rows, m == space_size - 1
        )
    total_rows = row_count * space_size * lax.axis_size("dp")
    weight_grad = summed.reshape(chan_in, kinds_total, chan_out).transpose(1, 0, 2) / jnp.sqrt(
        jnp.float32(total_rows)
    )
    return (acc[None], feature_grad[None], weight_grad)


def solution(mesh):
    placed = (
        P("dp", "space", None),
        P("dp", "space"),
        P("dp", "space"),
        P(),
        P("dp", "space", None),
    )
    return jax.shard_map(
        per_device,
        mesh=mesh,
        in_specs=placed,
        out_specs=(P("dp", "space", None), P("dp", "space", None), P()),
        check_vma=False,
    )
```

time: 364 us -> 252 us (0.69)
  local copies, waits for them, and re-layouts: 192 us -> 16.4 us
  Pallas kernels: 0 us -> 106 us
  other arithmetic: 52.1 us -> 0.6 us
  waiting for transfers between devices: 73 us -> 92.8 us
  starting transfers between devices: 18 us -> 30.1 us
  matrix products: 11.7 us -> 0 us
  between operations: 14.1 us -> 5.2 us
    pallas_call x0 -> x10, Pallas kernels: none -> 106 us  [the longest x8 60.6 us: gather_children(): pl.pallas_call(lambda *refs: gather_children_kernel(capacity, par_rows, f...]
    gather x49 -> x0, local copies, waits for them, and re-layouts: 86.5 us -> none  [the longest x1 58.1 us: per_device(): jnp.take(parent_grad, recv_slots, axis=0, mode='fill', fill_value=0)]
    ppermute x0 -> x14, waiting for transfers between devices: none -> 79.7 us  [the longest x7 46.6 us: per_device(): lax.ppermute(payloads[m], 'space', [(i, i ^ m) for i in range(space_size)])]
    scatter x1 -> x0, local copies, waits for them, and re-layouts: 44 us -> none  [per_device(): slot_grid = jnp.zeros((marker, chan_in), jnp.bfloat16).at[recv_slots.resh...]
    scatter-add x16 -> x0, local copies, waits for them, and re-layouts: 40.2 us -> none
    all_to_all x3 -> x2, waiting for transfers between devices: 51.3 us -> 13.1 us  [the longest x1 13.1 us: reduce_kernel_terms(): lax.all_to_all(terms.reshape(parts, rows // parts, terms.shape[1]), axes,...]
    scatter-add x16 -> x0, other arithmetic: 31.6 us -> none
    ppermute x0 -> x14, starting transfers between devices: none -> 22.3 us  [the longest x7 13.8 us: per_device(): lax.ppermute(payloads[m], 'space', [(i, i ^ m) for i in range(space_size)])]
  transfers between devices with their start and end apart: 4 -> 16, of which waited for: 3 -> 6; matrix products, arithmetic and copies ran while one was open for 67% -> 3% of each run, Pallas kernels for 0% -> 24%
where the time goes in v1:
time: 252 us; the launch traced here: 251 us
  Pallas kernels  106 us (42%)
  waiting for transfers between devices  92.8 us (37%)
  starting transfers between devices  30.1 us (12%)
  local copies, waits for them, and re-layouts  16.4 us (7%)
  between operations  5.2 us (2%)
    pallas_call x8, Pallas kernels, gather_children(): pl.pallas_call(lambda *refs: gather_children_kernel(capacity, par_rows, f...  60.6 us
    ppermute x7, waiting for transfers between devices, per_device(): lax.ppermute(payloads[m], 'space', [(i, i ^ m) for i in range(space_size)])  46.6 us
    pallas_call x1, Pallas kernels, backward(): pl.pallas_call(lambda *refs: backward_kernel(blocks, *refs), out_shape=[j...  41.2 us
    ppermute x4, waiting for transfers between devices, collect_blocks(): right = lax.ppermute(right, 'space', ahead)  33.1 us
    ppermute x7, starting transfers between devices, per_device(): lax.ppermute(payloads[m], 'space', [(i, i ^ m) for i in range(space_size)])  13.8 us
    all_to_all x1, waiting for transfers between devices, reduce_kernel_terms(): lax.all_to_all(terms.reshape(parts, rows // parts, terms.shape[1]), axes,...  13.1 us
    ppermute x4, starting transfers between devices, collect_blocks(): right = lax.ppermute(right, 'space', ahead)  7.73 us
    unnamed x39, local copies, waits for them, and re-layouts  5.72 us
  transfers between devices with their start and end apart: 16, of which 6 were waited for; matrix products, arithmetic and copies ran while one was open for 3% of the time, Pallas kernels for 24%

profile of v1, /device:TPU:0, one launch (start us, length us, event | category | flops | bytes accessed | tf_op | source)
XLA Modules:
  0.0 250.8 jit_solution(18354777488808256960)
XLA Ops:
  0.6 0.0 copy-start.18
  0.6 0.0 copy-start.15
  0.7 0.0 copy-start.8
  0.7 0.0 copy-start
  0.7 0.5 iota_xor_fusion.refs_0_
  1.2 4.0 %pack_windows.1 = (bf16[2176,128]{1,0:T(8,128)(2,1)}, bf16[2176,128]{1,0:T(8,128)(2,1)}, bf16[2176,128]{1,0:T(8,128)(2,1)}, bf16[2176,128]{1,0:T(8,128)(2,1)}, b...) custom-call(s32[8]{0:T(128)} %iota_xor_fusion.refs_0_, ...), custom_call_target="tpu_custom_call" | custom-call | bytes 8912896 | tf_op jit(solution)/shard_map/pack_windows/pallas_call | solution.py:73
  5.2 3.1 %collective-permute-start.7 = (bf16[2048,128]{1,0:T(8,128)(2,1)S(1)}, bf16[2048,128]{1,0:T(8,128)(2,1)S(1)}, u32[]{:S(2)}, u32[]{:S(2)}) collective-permute-start(bf16[2048,128]{1,0:T(8,128)(2,1)S(1)} %bitcast.32), channel_id=1, source_target_pairs={{0,2},{2,4},{4,6},{6,7},{7,5},{5,3},{3,1},{1,0},{8,10},{10,12},{12... | collective-permute-start | bytes 1572872 | tf_op jit(solution)/shard_map/ppermute | solution.py:275
  8.3 0.0 collective-permute-start.8
  8.3 11.9 %collective-permute-done.7.refs_6_ = bf16[2048,128]{1,0:T(8,128)(2,1)S(1)} collective-permute-done((bf16[2048,128]{1,0:T(8,128)(2,1)S(1)}, bf16[2048,128]{1,0:T(8,128)(2,1)S(1)}, u32[]{:S(2)}, u32[]{:S(2)}) %collective-permute-start.7) | collective-permute-done | bytes 524320 | tf_op jit(solution)/shard_map/ppermute | solution.py:275
  20.1 1.8 collective-permute-start.9
  21.9 0.0 collective-permute-done.8.refs_7_
  21.9 0.2 collective-permute-start.10
  22.2 11.1 %collective-permute-done.9.refs_8_ = bf16[2048,128]{1,0:T(8,128)(2,1)S(1)} collective-permute-done((bf16[2048,128]{1,0:T(8,128)(2,1)S(1)}, bf16[2048,128]{1,0:T(8,128)(2,1)S(1)}, u32[]{:S(2)}, u32[]{:S(2)}) %collective-permute-start.9) | collective-permute-done | bytes 524320 | tf_op jit(solution)/shard_map/ppermute | solution.py:275
  33.2 1.5 collective-permute-start.11
  34.7 0.0 collective-permute-done.10.refs_9_
  34.7 0.5 collective-permute-start.12
  35.3 10.2 %collective-permute-done.11.refs_10_ = bf16[2048,128]{1,0:T(8,128)(2,1)S(1)} collective-permute-done((bf16[2048,128]{1,0:T(8,128)(2,1)S(1)}, bf16[2048,128]{1,0:T(8,128)(2,1)S(1)}, u32[]{:S(2)}, u32[]{:S(2)}) %collective-permute-start.11) | collective-permute-done | bytes 524320 | tf_op jit(solution)/shard_map/ppermute | solution.py:275
  45.4 1.4 collective-permute-start.13
  46.8 0.6 dynamic_slice.24
  51.8 0.9 copy.13
  52.7 0.7 fusion
  53.3 5.0 %stack.7.refs_0_ = s32[8]{0:T(128)} concatenate(s32[1]{0:T(128)} %bitcast.6, s32[1]{0:T(128)} %get-tuple-element.49, s32[1]{0:T(128)} %get-tuple-element.48, s32[1]{0:T(128)} %get-tuple-element.47, s32[1]{0:T(128)} %get-tuple-element.46, s32[1]{0:T(128)} %get-tuple-element.45, s32[1]{0:T(128)} %get-tuple-element.50, s32[1]{0:T(128)} %get-tuple-element.44), dimensions={0} | concatenate | bytes 64 | tf_op jit(solution)/shard_map/stack | solution.py:282
  58.3 0.0 collective-permute-done.12.refs_11_
  58.3 0.0 collective-permute-done.13.refs_12_
  58.3 0.0 copy-done.9
  58.3 0.0 copy-done.10
  58.3 0.0 copy-done.11
  58.4 0.7 copy-done.14
  59.1 41.2 %fine_gradients.1 = (bf16[8192,128]{1,0:T(8,128)(2,1)}, f32[128,1024]{1,0:T(8,128)}) custom-call(s32[8]{0:T(128)} %stack.7.refs_0_, s32[64,128]{1,0:T(8,128)} %bitcast.35, s32[64,128]{1,0:T(8,128)} %bitcast.37, bf16[8192,128]{1,0:T(8,128)(2,1)} %bitcast.26, bf16[1024,128]{1,0:T(8,128)(2,1)} %bitcast.29, bf16[2048,128]{1,0:T(8,128)(2,1)} %bitcast.31, ...), custom_call_target="tpu_custom_call" | custom-call | bytes 157286400 | tf_op jit(solution)/shard_map/fine_gradients/pallas_call | solution.py:227
  100.3 2.0 reshape_reshape.4
  102.3 5.2 %all-to-all-start = ((f32[32,32,128]{2,1,0:T(8,128)}), f32[32,32,128]{2,1,0:T(8,128)S(1)}, u32[]{:S(2)}, u32[]{:S(2)}) async-start(f32[32,32,128]{2,1,0:T(8,128)} %reshape_reshape.4), calls=%async_computation | async-start | bytes 1048576 | tf_op jit(solution)/shard_map/all_to_all | solution.py:250
  107.5 1.8 collective-permute-start.5
  109.4 1.5 collective-permute-start.6
  110.8 13.1 %all-to-all-done = f32[32,32,128]{2,1,0:T(8,128)S(1)} async-done(((f32[32,32,128]{2,1,0:T(8,128)}), f32[32,32,128]{2,1,0:T(8,128)S(1)}, u32[]{:S(2)}, u32[]{:S(2)}) %all-to-all-start) | async-done | bytes 524320 | tf_op jit(solution)/shard_map/all_to_all | solution.py:250
  123.9 0.9 broadcast_in_dim.14
  124.8 2.6 %all-to-all-start.1 = ((f32[32,32,128]{2,1,0:T(8,128)}), f32[32,32,128]{2,1,0:T(8,128)S(1)}, u32[]{:S(2)}, u32[]{:S(2)}) async-start(f32[32,32,128]{2,1,0:T(8,128)} %broadcast_in_dim.14), calls=%async_computation.1 | async-start | bytes 1048576 | tf_op jit(solution)/shard_map/all_to_all | solution.py:254
  127.4 3.7 %collective-permute-start.2 = (bf16[2176,128]{1,0:T(8,128)(2,1)}, bf16[2176,128]{1,0:T(8,128)(2,1)S(1)}, u32[]{:S(2)}, u32[]{:S(2)}) collective-permute-start(bf16[2176,128]{1,0:T(8,128)(2,1)} %get-tuple-element.32), channel_id=1, source_target_pairs={{0,5},{1,4},{2,7},{3,6},{4,1},{5,0},{6,3},{7,2},{8,13},{9,12},{10,... | collective-permute-start | bytes 1671176 | tf_op jit(solution)/shard_map/ppermute | solution.py:305
  131.0 1.5 collective-permute-start.4
  132.5 0.4 collective-permute-start.3
  133.0 0.0 collective-permute-done.5.refs_0_
  133.0 2.5 collective-permute-start.1
  135.5 0.0 collective-permute-done.6.refs_0_
  135.5 2.4 collective-permute-start
  137.9 0.7 copy_bitcast_fusion.refs_1_
  138.6 7.6 %gather_children.8.refs_2_ = f32[2048,128]{1,0:T(8,128)} custom-call(bf16[2176,128]{1,0:T(8,128)(2,1)} %get-tuple-element.37.refs_0_, bf16[128,1024]{1,0:T(8,128)(2,1)} %copy_bitcast_fusion.refs_1_), custom_call_target="tpu_custom_call" | custom-call | bytes 28311552 | tf_op jit(solution)/shard_map/gather_children/pallas_call | solution.py:153
  146.2 6.9 %gather_children.9.refs_2_ = f32[2048,128]{1,0:T(8,128)} custom-call(bf16[2176,128]{1,0:T(8,128)(2,1)} %copy-done.3, bf16[128,1024]{1,0:T(8,128)(2,1)} %copy_bitcast_fusion.refs_1_, f32[2048,128]{1,0:T(8,128)} %gather_children.8.refs_2_), custom_call_target="tpu_custom_call" | custom-call | bytes 28311552 | tf_op jit(solution)/shard_map/gather_children/pallas_call | solution.py:153
  153.1 8.0 %gather_children.10.refs_2_ = f32[2048,128]{1,0:T(8,128)} custom-call(bf16[2176,128]{1,0:T(8,128)(2,1)} %copy-done.1, bf16[128,1024]{1,0:T(8,128)(2,1)} %copy_bitcast_fusion.refs_1_, f32[2048,128]{1,0:T(8,128)} %gather_children.9.refs_2_), custom_call_target="tpu_custom_call" | custom-call | bytes 28311552 | tf_op jit(solution)/shard_map/gather_children/pallas_call | solution.py:153
  161.0 2.9 %collective-permute-done.4.refs_0_ = bf16[2176,128]{1,0:T(8,128)(2,1)S(1)} collective-permute-done((bf16[2176,128]{1,0:T(8,128)(2,1)}, bf16[2176,128]{1,0:T(8,128)(2,1)S(1)}, u32[]{:S(2)}, u32[]{:S(2)}) %collective-permute-start.4) | collective-permute-done | bytes 557088 | tf_op jit(solution)/shard_map/ppermute | solution.py:305
  164.0 0.8 copy-done.7
  164.8 7.4 %gather_children.11.refs_2_ = f32[2048,128]{1,0:T(8,128)} custom-call(bf16[2176,128]{1,0:T(8,128)(2,1)} %copy-done.7, bf16[128,1024]{1,0:T(8,128)(2,1)} %copy_bitcast_fusion.refs_1_, f32[2048,128]{1,0:T(8,128)} %gather_children.10.refs_2_), custom_call_target="tpu_custom_call" | custom-call | bytes 28311552 | tf_op jit(solution)/shard_map/gather_children/pallas_call | solution.py:153
  172.1 43.7 %collective-permute-done.3.refs_0_ = bf16[2176,128]{1,0:T(8,128)(2,1)S(1)} collective-permute-done((bf16[2176,128]{1,0:T(8,128)(2,1)}, bf16[2176,128]{1,0:T(8,128)(2,1)S(1)}, u32[]{:S(2)}, u32[]{:S(2)}) %collective-permute-start.3) | collective-permute-done | bytes 557088 | tf_op jit(solution)/shard_map/ppermute | solution.py:305
  215.8 0.8 copy-done.6
  216.6 8.2 %gather_children.12.refs_2_ = f32[2048,128]{1,0:T(8,128)} custom-call(bf16[2176,128]{1,0:T(8,128)(2,1)} %copy-done.6, bf16[128,1024]{1,0:T(8,128)(2,1)} %copy_bitcast_fusion.refs_1_, f32[2048,128]{1,0:T(8,128)} %gather_children.11.refs_2_), custom_call_target="tpu_custom_call" | custom-call | bytes 28311552 | tf_op jit(solution)/shard_map/gather_children/pallas_call | solution.py:153
  224.8 0.0 collective-permute-done.2.refs_0_
  224.8 0.8 copy-done.2
  225.6 7.0 %gather_children.13.refs_2_ = f32[2048,128]{1,0:T(8,128)} custom-call(bf16[2176,128]{1,0:T(8,128)(2,1)} %copy-done.2, bf16[128,1024]{1,0:T(8,128)(2,1)} %copy_bitcast_fusion.refs_1_, f32[2048,128]{1,0:T(8,128)} %gather_children.12.refs_2_), custom_call_target="tpu_custom_call" | custom-call | bytes 28311552 | tf_op jit(solution)/shard_map/gather_children/pallas_call | solution.py:153
  232.6 0.0 collective-permute-done.1.refs_0_
  232.6 0.8 copy-done.4
  233.4 7.6 %gather_children.14.refs_2_ = f32[2048,128]{1,0:T(8,128)} custom-call(bf16[2176,128]{1,0:T(8,128)(2,1)} %copy-done.4, bf16[128,1024]{1,0:T(8,128)(2,1)} %copy_bitcast_fusion.refs_1_, f32[2048,128]{1,0:T(8,128)} %gather_children.13.refs_2_), custom_call_target="tpu_custom_call" | custom-call | bytes 28311552 | tf_op jit(solution)/shard_map/gather_children/pallas_call | solution.py:153
  241.1 0.0 collective-permute-done.refs_0_
  241.1 0.8 copy-done.5
  241.9 8.0 %gather_children.15 = bf16[2048,128]{1,0:T(8,128)(2,1)} custom-call(bf16[2176,128]{1,0:T(8,128)(2,1)} %copy-done.5, bf16[128,1024]{1,0:T(8,128)(2,1)} %copy_bitcast_fusion.refs_1_, f32[2048,128]{1,0:T(8,128)} %gather_children.14.refs_2_), custom_call_target="tpu_custom_call" | custom-call | bytes 28311552 | tf_op jit(solution)/shard_map/gather_children/pallas_call | solution.py:153
  249.8 0.0 all-to-all-done.1
  249.9 0.9 copy.14
  (27 shorter events, 0.1 us)
Async XLA Ops:
  0.6 46.2 %copy-start.18 = (s32[8]{0:T(128)S(1)}, s32[8]{0:T(128)}, u32[]{:S(2)}) copy-start(s32[8]{0:T(128)} %constant.73.clone) | copy-start | bytes 100
  0.6 52.0 %copy-start.15 = (s32[8]{0:T(128)S(1)}, s32[8]{0:T(128)}, u32[]{:S(2)}) copy-start(s32[8]{0:T(128)} %constant.74.clone) | copy-start | bytes 100
  0.7 4.5 %copy-start.8 = (bf16[1,2048,128]{2,1,0:T(8,128)(2,1)S(1)}, bf16[1,2048,128]{2,1,0:T(8,128)(2,1)}, u32[]{:S(2)}) copy-start(bf16[1,2048,128]{2,1,0:T(8,128)(2,1)} %param.11) | copy-start | bytes 1572868
  0.7 51.1 %copy-start = (bf16[8,128,128]{2,1,0:T(8,128)(2,1)S(1)}, bf16[8,128,128]{2,1,0:T(8,128)(2,1)}, u32[]{:S(2)}) copy-start(bf16[8,128,128]{2,1,0:T(8,128)(2,1)} %param.10) | copy-start | bytes 786436
  5.2 14.9 %collective-permute-start.7 = (bf16[2048,128]{1,0:T(8,128)(2,1)S(1)}, bf16[2048,128]{1,0:T(8,128)(2,1)S(1)}, u32[]{:S(2)}, u32[]{:S(2)}) collective-permute-start(bf16[2048,128]{1,0:T(8,128)(2,1)S(1)} %bitcast.32), channel_id=1, source_target_pairs={{0,2},{2,4},{4,6},{6,7},{7,5},{5,3},{3,1},{1,0},{8,10},{10,12},{12... | collective-permute-start | bytes 1572872 | tf_op jit(solution)/shard_map/ppermute | solution.py:275
  8.3 13.7 %collective-permute-start.8 = (bf16[2048,128]{1,0:T(8,128)(2,1)S(1)}, bf16[2048,128]{1,0:T(8,128)(2,1)S(1)}, u32[]{:S(2)}, u32[]{:S(2)}) collective-permute-start(bf16[2048,128]{1,0:T(8,128)(2,1)S(1)} %bitcast.33), channel_id=1, source_target_pairs={{2,0},{4,2},{6,4},{7,6},{5,7},{3,5},{1,3},{0,1},{10,8},{12,10},{14... | collective-permute-start | bytes 1572872 | tf_op jit(solution)/shard_map/ppermute | solution.py:279
  20.1 38.2 %copy-start.9 = (bf16[2048,128]{1,0:T(8,128)(2,1)}, bf16[2048,128]{1,0:T(8,128)(2,1)S(1)}, u32[]{:S(2)}) copy-start(bf16[2048,128]{1,0:T(8,128)(2,1)S(1)} %collective-permute-done.7.refs_6_) | copy-start | bytes 1572868
  20.1 13.1 %collective-permute-start.9 = (bf16[2048,128]{1,0:T(8,128)(2,1)S(1)}, bf16[2048,128]{1,0:T(8,128)(2,1)S(1)}, u32[]{:S(2)}, u32[]{:S(2)}) collective-permute-start(bf16[2048,128]{1,0:T(8,128)(2,1)S(1)} %collective-permute-done.7.refs_6_), channel_id=1, source_target_pairs={{0,2},{2,4},{4,6},{6,7},{7,5},{5,3},{3,1},{1,0},{8,10},{10,12},{12... | collective-permute-start | bytes 1572872 | tf_op jit(solution)/shard_map/ppermute | solution.py:275
  21.9 36.4 %copy-start.10 = (bf16[2048,128]{1,0:T(8,128)(2,1)}, bf16[2048,128]{1,0:T(8,128)(2,1)S(1)}, u32[]{:S(2)}) copy-start(bf16[2048,128]{1,0:T(8,128)(2,1)S(1)} %collective-permute-done.8.refs_7_) | copy-start | bytes 1572868
  21.9 12.8 %collective-permute-start.10 = (bf16[2048,128]{1,0:T(8,128)(2,1)S(1)}, bf16[2048,128]{1,0:T(8,128)(2,1)S(1)}, u32[]{:S(2)}, u32[]{:S(2)}) collective-permute-start(bf16[2048,128]{1,0:T(8,128)(2,1)S(1)} %collective-permute-done.8.refs_7_), channel_id=1, source_target_pairs={{2,0},{4,2},{6,4},{7,6},{5,7},{3,5},{1,3},{0,1},{10,8},{12,10},{14... | collective-permute-start | bytes 1572872 | tf_op jit(solution)/shard_map/ppermute | solution.py:279
  33.2 25.1 %copy-start.11 = (bf16[2048,128]{1,0:T(8,128)(2,1)}, bf16[2048,128]{1,0:T(8,128)(2,1)S(1)}, u32[]{:S(2)}) copy-start(bf16[2048,128]{1,0:T(8,128)(2,1)S(1)} %collective-permute-done.9.refs_8_) | copy-start | bytes 1572868
  33.2 12.2 %collective-permute-start.11 = (bf16[2048,128]{1,0:T(8,128)(2,1)S(1)}, bf16[2048,128]{1,0:T(8,128)(2,1)S(1)}, u32[]{:S(2)}, u32[]{:S(2)}) collective-permute-start(bf16[2048,128]{1,0:T(8,128)(2,1)S(1)} %collective-permute-done.9.refs_8_), channel_id=1, source_target_pairs={{0,2},{2,4},{4,6},{6,7},{7,5},{5,3},{3,1},{1,0},{8,10},{10,12},{12... | collective-permute-start | bytes 1572872 | tf_op jit(solution)/shard_map/ppermute | solution.py:275
  34.7 23.6 %copy-start.12 = (bf16[2048,128]{1,0:T(8,128)(2,1)}, bf16[2048,128]{1,0:T(8,128)(2,1)S(1)}, u32[]{:S(2)}) copy-start(bf16[2048,128]{1,0:T(8,128)(2,1)S(1)} %collective-permute-done.10.refs_9_) | copy-start | bytes 1572868
  34.7 23.6 %collective-permute-start.12 = (bf16[2048,128]{1,0:T(8,128)(2,1)S(1)}, bf16[2048,128]{1,0:T(8,128)(2,1)S(1)}, u32[]{:S(2)}, u32[]{:S(2)}) collective-permute-start(bf16[2048,128]{1,0:T(8,128)(2,1)S(1)} %collective-permute-done.10.refs_9_), channel_id=1, source_target_pairs={{2,0},{4,2},{6,4},{7,6},{5,7},{3,5},{1,3},{0,1},{10,8},{12,10},{14... | collective-permute-start | bytes 1572872 | tf_op jit(solution)/shard_map/ppermute | solution.py:279
  45.4 12.9 %copy-start.13 = (bf16[2048,128]{1,0:T(8,128)(2,1)}, bf16[2048,128]{1,0:T(8,128)(2,1)S(1)}, u32[]{:S(2)}) copy-start(bf16[2048,128]{1,0:T(8,128)(2,1)S(1)} %collective-permute-done.11.refs_10_) | copy-start | bytes 1572868
  45.4 12.9 %collective-permute-start.13 = (bf16[2048,128]{1,0:T(8,128)(2,1)S(1)}, bf16[2048,128]{1,0:T(8,128)(2,1)}, u32[]{:S(2)}, u32[]{:S(2)}) collective-permute-start(bf16[2048,128]{1,0:T(8,128)(2,1)S(1)} %collective-permute-done.11.refs_10_), channel_id=1, source_target_pairs={{0,2},{2,4},{4,6},{6,7},{7,5},{5,3},{3,1},{1,0},{8,10},{10,12},{12... | collective-permute-start | bytes 1572872 | tf_op jit(solution)/shard_map/ppermute | solution.py:275
  58.3 0.8 copy-start.14
  100.3 32.7 %copy-start.17 = (bf16[2176,128]{1,0:T(8,128)(2,1)S(1)}, bf16[2176,128]{1,0:T(8,128)(2,1)}, u32[]{:S(2)}) copy-start(bf16[2176,128]{1,0:T(8,128)(2,1)} %get-tuple-element.31) | copy-start | bytes 1671172
  100.3 35.2 %copy-start.16 = (bf16[2176,128]{1,0:T(8,128)(2,1)S(1)}, bf16[2176,128]{1,0:T(8,128)(2,1)}, u32[]{:S(2)}) copy-start(bf16[2176,128]{1,0:T(8,128)(2,1)} %get-tuple-element.30) | copy-start | bytes 1671172
  102.3 21.6 %all-to-all-start = ((f32[32,32,128]{2,1,0:T(8,128)}), f32[32,32,128]{2,1,0:T(8,128)S(1)}, u32[]{:S(2)}, u32[]{:S(2)}) async-start(f32[32,32,128]{2,1,0:T(8,128)} %reshape_reshape.4), calls=%async_computation | async-start | bytes 1048576 | tf_op jit(solution)/shard_map/all_to_all | solution.py:250
  107.5 25.5 %collective-permute-start.5 = (bf16[2176,128]{1,0:T(8,128)(2,1)}, bf16[2176,128]{1,0:T(8,128)(2,1)S(1)}, u32[]{:S(2)}, u32[]{:S(2)}) collective-permute-start(bf16[2176,128]{1,0:T(8,128)(2,1)} %get-tuple-element.35), channel_id=1, source_target_pairs={{0,2},{1,3},{2,0},{3,1},{4,6},{5,7},{6,4},{7,5},{8,10},{9,11},{10,... | collective-permute-start | bytes 1671176 | tf_op jit(solution)/shard_map/ppermute | solution.py:305
  109.4 26.1 %collective-permute-start.6 = (bf16[2176,128]{1,0:T(8,128)(2,1)}, bf16[2176,128]{1,0:T(8,128)(2,1)S(1)}, u32[]{:S(2)}, u32[]{:S(2)}) collective-permute-start(bf16[2176,128]{1,0:T(8,128)(2,1)} %get-tuple-element.36), channel_id=1, source_target_pairs={{0,1},{1,0},{2,3},{3,2},{4,5},{5,4},{6,7},{7,6},{8,9},{9,8},{10,11... | collective-permute-start | bytes 1671176 | tf_op jit(solution)/shard_map/ppermute | solution.py:305
  124.8 125.1 %all-to-all-start.1 = ((f32[32,32,128]{2,1,0:T(8,128)}), f32[32,32,128]{2,1,0:T(8,128)S(1)}, u32[]{:S(2)}, u32[]{:S(2)}) async-start(f32[32,32,128]{2,1,0:T(8,128)} %broadcast_in_dim.14), calls=%async_computation.1 | async-start | bytes 1048576 | tf_op jit(solution)/shard_map/all_to_all | solution.py:254
  127.4 97.4 %collective-permute-start.2 = (bf16[2176,128]{1,0:T(8,128)(2,1)}, bf16[2176,128]{1,0:T(8,128)(2,1)S(1)}, u32[]{:S(2)}, u32[]{:S(2)}) collective-permute-start(bf16[2176,128]{1,0:T(8,128)(2,1)} %get-tuple-element.32), channel_id=1, source_target_pairs={{0,5},{1,4},{2,7},{3,6},{4,1},{5,0},{6,3},{7,2},{8,13},{9,12},{10,... | collective-permute-start | bytes 1671176 | tf_op jit(solution)/shard_map/ppermute | solution.py:305
  131.0 32.9 %collective-permute-start.4 = (bf16[2176,128]{1,0:T(8,128)(2,1)}, bf16[2176,128]{1,0:T(8,128)(2,1)S(1)}, u32[]{:S(2)}, u32[]{:S(2)}) collective-permute-start(bf16[2176,128]{1,0:T(8,128)(2,1)} %get-tuple-element.34), channel_id=1, source_target_pairs={{0,3},{1,2},{2,1},{3,0},{4,7},{5,6},{6,5},{7,4},{8,11},{9,10},{10,... | collective-permute-start | bytes 1671176 | tf_op jit(solution)/shard_map/ppermute | solution.py:305
  132.5 83.3 %collective-permute-start.3 = (bf16[2176,128]{1,0:T(8,128)(2,1)}, bf16[2176,128]{1,0:T(8,128)(2,1)S(1)}, u32[]{:S(2)}, u32[]{:S(2)}) collective-permute-start(bf16[2176,128]{1,0:T(8,128)(2,1)} %get-tuple-element.33), channel_id=1, source_target_pairs={{0,4},{1,5},{2,6},{3,7},{4,0},{5,1},{6,2},{7,3},{8,12},{9,13},{10,... | collective-permute-start | bytes 1671176 | tf_op jit(solution)/shard_map/ppermute | solution.py:305
  133.0 20.1 %copy-start.1 = (bf16[2176,128]{1,0:T(8,128)(2,1)}, bf16[2176,128]{1,0:T(8,128)(2,1)S(1)}, u32[]{:S(2)}) copy-start(bf16[2176,128]{1,0:T(8,128)(2,1)S(1)} %collective-permute-done.5.refs_0_) | copy-start | bytes 1671172
  133.0 99.7 %collective-permute-start.1 = (bf16[2176,128]{1,0:T(8,128)(2,1)S(1)}, bf16[2176,128]{1,0:T(8,128)(2,1)S(1)}, u32[]{:S(2)}, u32[]{:S(2)}) collective-permute-start(bf16[2176,128]{1,0:T(8,128)(2,1)S(1)} %copy-done.17), channel_id=1, source_target_pairs={{0,6},{1,7},{2,4},{3,5},{4,2},{5,3},{6,0},{7,1},{8,14},{9,15},{10,... | collective-permute-start | bytes 1671176 | tf_op jit(solution)/shard_map/ppermute | solution.py:305
  135.5 10.7 %copy-start.3 = (bf16[2176,128]{1,0:T(8,128)(2,1)}, bf16[2176,128]{1,0:T(8,128)(2,1)S(1)}, u32[]{:S(2)}) copy-start(bf16[2176,128]{1,0:T(8,128)(2,1)S(1)} %collective-permute-done.6.refs_0_) | copy-start | bytes 1671172
  135.5 105.6 %collective-permute-start = (bf16[2176,128]{1,0:T(8,128)(2,1)S(1)}, bf16[2176,128]{1,0:T(8,128)(2,1)S(1)}, u32[]{:S(2)}, u32[]{:S(2)}) collective-permute-start(bf16[2176,128]{1,0:T(8,128)(2,1)S(1)} %copy-done.16), channel_id=1, source_target_pairs={{0,7},{1,6},{2,5},{3,4},{4,3},{5,2},{6,1},{7,0},{8,15},{9,14},{10,... | collective-permute-start | bytes 1671176 | tf_op jit(solution)/shard_map/ppermute | solution.py:305
  164.0 0.8 copy-start.7
  215.8 0.8 copy-start.6
  224.8 0.8 copy-start.2
  232.6 0.8 copy-start.4
  241.1 0.8 copy-start.5

commit v2 on v0

v2 whole, which is shorter than its diff:
```python
import jax
import jax.numpy as jnp
from jax import lax
from jax.experimental import pallas as pl
from jax.experimental.pallas import tpu as pltpu
from jax.sharding import PartitionSpec as P

LANES = 128
ALIGN = 16
TILE = 256
VMEM_LIMIT = 60 * 1024 * 1024


def column(row):
    return jnp.transpose(jnp.broadcast_to(row.astype(jnp.float32), (LANES, LANES))).astype(jnp.int32)


def pack_kernel(half, par_rows, parent_ref, code_ref, feats_ref, early_ref, late_ref, wide, parents, codes, stage_ref, sems):
    lines = parent_ref.shape[0]
    count = early_ref.shape[0]
    fine_rows = lines * LANES
    half_lines = half // LANES
    parents[...] = jnp.full(parents.shape, 1 << 20, jnp.int32)
    codes[...] = jnp.zeros(codes.shape, jnp.int32)
    parents[0:lines] = parent_ref[...]
    codes[0:lines] = code_ref[...]
    wide[0:fine_rows] = feats_ref[...].astype(jnp.float32)
    wide[fine_rows:] = jnp.zeros((wide.shape[0] - fine_rows, wide.shape[1]), jnp.float32)
    lane = lax.broadcasted_iota(jnp.int32, (8, LANES), 1)
    copies = []
    for m in range(count):
        base = m * par_rows
        start = jnp.sum((parent_ref[...] < base).astype(jnp.int32))
        for part, out in enumerate((early_ref, late_ref)):
            here = start + part * half
            line = here // LANES
            shift = here % LANES

            def window(ref):
                now = pltpu.roll(ref[pl.ds(line, 8), :], (LANES - shift) % LANES, 1)
                after = pltpu.roll(ref[pl.ds(line + 1, 8), :], (LANES - shift) % LANES, 1)
                return jnp.where(lane < LANES - shift, now, after)

            rel = window(parents) - base
            high = jnp.clip(rel >> 4, -1, 256)
            low = (rel & 15) * 8 + window(codes)
            both = jnp.concatenate([high, low], axis=0).astype(jnp.float32)
            stage_ref[m, part, 0:half] = wide[pl.ds(here, half), :].astype(jnp.bfloat16)
            stage_ref[m, part, half : half + ALIGN] = both.astype(jnp.bfloat16)
            copy = pltpu.make_async_copy(stage_ref.at[m, part], out.at[m], sems.at[m, part])
            copy.start()
            copies.append(copy)
    for copy in copies:
        copy.wait()


def pack(parents, codes, feats, count, half, par_rows):
    lines = parents.shape[0]
    rows = half + ALIGN
    vmem = pl.BlockSpec(memory_space=pltpu.VMEM)
    return pl.pallas_call(
        lambda *refs: pack_kernel(half, par_rows, *refs),
        out_shape=[jax.ShapeDtypeStruct((count, rows, LANES), jnp.bfloat16)] * 2,
        in_specs=[vmem] * 3,
        out_specs=[pl.BlockSpec(memory_space=pl.ANY)] * 2,
        scratch_shapes=[
            pltpu.VMEM((feats.shape[0] + 2 * half + 8, LANES), jnp.float32),
            pltpu.VMEM((lines + half // LANES + 16, LANES), jnp.int32),
            pltpu.VMEM((lines + half // LANES + 16, LANES), jnp.int32),
            pltpu.VMEM((count, 2, rows, LANES), jnp.bfloat16),
            pltpu.SemaphoreType.DMA((count, 2)),
        ],
        compiler_params=pltpu.CompilerParams(vmem_limit_bytes=VMEM_LIMIT),
        name="pack_windows",
    )(parents, codes, feats)


def spread_kinds(kind, rows, kinds_total):
    zero = jnp.zeros((), rows.dtype)
    tag = kind.astype(jnp.float32).astype(rows.dtype)
    return jnp.concatenate(
        [jnp.where(tag == jnp.asarray(k, rows.dtype), rows, zero) for k in range(kinds_total)], axis=1
    )


def place_children_kernel(half, first, payload_ref, weight_ref, *rest):
    if first:
        out_ref, total_ref, rel_ref, code_ref, ends_vmem, ends_ref, sem = rest
    else:
        prior_ref, out_ref, total_ref, rel_ref, code_ref, ends_vmem, ends_ref, sem = rest
    par_rows, chan_out = out_ref.shape
    sources = payload_ref.shape[0]
    kinds_total = weight_ref.shape[0] // payload_ref.shape[2]
    lines = half // LANES
    size = min(2 * TILE, half)
    parts = size // TILE
    per = TILE // LANES
    window = min(5 * TILE // 2, par_rows)
    meta = payload_ref[:, half : half + ALIGN, :].astype(jnp.float32).astype(jnp.int32)
    rel = meta[:, 0:8] * 16 + (meta[:, 8:16] >> 3)
    line = lax.broadcasted_iota(jnp.int32, rel.shape, 1)
    rel = jnp.where(line < lines, rel, par_rows).reshape(8 * sources, LANES)
    rel_ref[...] = rel
    code_ref[...] = (meta[:, 8:16] & 7).reshape(8 * sources, LANES)
    least = jnp.min(jnp.maximum(rel, 0), axis=1, keepdims=True)
    most = jnp.max(jnp.where(rel < par_rows, rel, -1), axis=1, keepdims=True)
    ends_vmem[0] = jnp.broadcast_to(least, rel.shape)
    ends_vmem[1] = jnp.broadcast_to(most, rel.shape)
    copy = pltpu.make_async_copy(ends_vmem, ends_ref, sem)
    copy.start()
    total_ref[...] = jnp.zeros(total_ref.shape, jnp.float32)
    if not first:
        total_ref[:, 0:chan_out] = prior_ref[...]
    copy.wait()
    chunks = half // size

    def chunk(step, carry):
        s = step // chunks
        c = step % chunks
        line0 = 8 * s + c * (size // LANES)
        mosts = [
            jnp.maximum(ends_ref[1, line0 + per * p, 0], ends_ref[1, line0 + per * p + per - 1, 0])
            for p in range(parts)
        ]
        starts = [
            pl.multiple_of(jnp.minimum(ends_ref[0, line0 + per * p, 0] // 8 * 8, par_rows - window), 8)
            for p in range(parts)
        ]
        slow = mosts[0] >= starts[0] + window
        live = mosts[0] >= 0
        for p in range(1, parts):
            slow = slow | (mosts[p] >= starts[p] + window)
            live = live | (mosts[p] >= 0)

        def work(extra):
            feats = payload_ref[s, pl.ds(pl.multiple_of(c * size, size), size), :]
            kinds = [column(code_ref[pl.ds(line0 + i, 1), :]) for i in range(size // LANES)]
            spread = spread_kinds(jnp.concatenate(kinds, axis=0), feats, kinds_total)
            product = jnp.dot(spread, weight_ref[...], preferred_element_type=jnp.float32)
            upper = product.astype(jnp.bfloat16)
            lower = (product - upper.astype(jnp.float32)).astype(jnp.bfloat16)
            both = jnp.concatenate([upper, lower], axis=1)
            for p in range(parts):
                count = TILE // LANES
                spots = [rel_ref[pl.ds(line0 + p * count + i, 1), :] for i in range(count)]
                spot = jnp.concatenate(spots, axis=1)
                mine = both[p * TILE : (p + 1) * TILE]

                def add(start, width, floor):
                    rank = lax.broadcasted_iota(jnp.int32, (width, TILE), 0) + start
                    hit = rank == spot
                    if floor is not None:
                        hit = hit & (rank >= floor)
                    total_ref[pl.ds(start, width), :] += jnp.dot(
                        jnp.where(hit, 1.0, 0.0).astype(jnp.bfloat16),
                        mine,
                        preferred_element_type=jnp.float32,
                    )

                add(starts[p], window, None)
                if extra:

                    def body(i, carry):
                        floor = starts[p] + window + i * TILE
                        add(pl.multiple_of(jnp.minimum(floor, par_rows - TILE), 8), TILE, floor)
                        return carry

                    lax.fori_loop(0, (mosts[p] + TILE - starts[p] - window) // TILE, body, 0)

        pl.when(live & slow)(lambda: work(True))
        pl.when(live & jnp.logical_not(slow))(lambda: work(False))
        return carry

    lax.fori_loop(0, sources * chunks, chunk, 0)
    out_ref[...] = (total_ref[:, 0:chan_out] + total_ref[:, chan_out : 2 * chan_out]).astype(out_ref.dtype)


def place_children(payload, weight_flat, prior, par_rows, last):
    first = prior is None
    chan_out = weight_flat.shape[1]
    sources = payload.shape[0]
    args = (payload, weight_flat) if first else (payload, weight_flat, prior)
    return pl.pallas_call(
        lambda *refs: place_children_kernel(payload.shape[1] - ALIGN, first, *refs),
        out_shape=jax.ShapeDtypeStruct((par_rows, chan_out), jnp.bfloat16 if last else jnp.float32),
        in_specs=[pl.BlockSpec(memory_space=pltpu.VMEM)] * len(args),
        out_specs=pl.BlockSpec(memory_space=pltpu.VMEM),
        scratch_shapes=[
            pltpu.VMEM((par_rows, 2 * chan_out), jnp.float32),
            pltpu.VMEM((8 * sources, LANES), jnp.int32),
            pltpu.VMEM((8 * sources, LANES), jnp.int32),
            pltpu.VMEM((2, 8 * sources, LANES), jnp.int32),
            pltpu.SMEM((2, 8 * sources, LANES), jnp.int32),
            pltpu.SemaphoreType.DMA(()),
        ],
        compiler_params=pltpu.CompilerParams(vmem_limit_bytes=VMEM_LIMIT),
        name="place_children",
    )(*args)


def stage_kernel(blocks, priors, shares, offset, table_ref, ends_ref, parent_ref, code_ref, feats_ref, weight_ref, *rest):
    cots = rest[:blocks]
    prior_refs = rest[blocks : blocks + priors]
    outs = rest[blocks + priors : 2 * blocks + priors]
    rest = rest[2 * blocks + priors :]
    terms_ref = rest[-1]
    kinds_total, chan_in, chan_out = terms_ref.shape
    size = 2 * TILE
    lines = size // LANES
    if priors:
        total = prior_refs[0][...]
        for prior_ref in prior_refs[1:]:
            total = total + prior_ref[...]
        terms_ref[...] = total
    else:
        terms_ref[...] = jnp.zeros(terms_ref.shape, jnp.float32)
    parents = parent_ref[...]
    for i, cot_ref in enumerate(cots):
        base = table_ref[offset + i]
        span = cot_ref.shape[0]
        window = min(3 * TILE, span)
        first = jnp.sum((parents < base).astype(jnp.int32)) // size
        last = (jnp.sum((parents < base + span).astype(jnp.int32)) + size - 1) // size

        def chunk(c, carry):
            starts, mosts = [], []
            for part in range(2):
                least = jnp.clip(ends_ref[0, 2 * c + part] - base, 0, span - 1)
                mosts.append(jnp.minimum(ends_ref[1, 2 * c + part] - base, span - 1))
                starts.append(pl.multiple_of(jnp.minimum(least // 16 * 16, span - window), 16))
            slow = (mosts[0] >= starts[0] + window) | (mosts[1] >= starts[1] + window)

            def work(extra):
                slots = (parent_ref[pl.ds(c * lines, lines), :] - base) * 8 + code_ref[
                    pl.ds(c * lines, lines), :
                ]
                slot = [column(slots[j : j + 1, :]) for j in range(lines)]
                kind = jnp.concatenate(slot, axis=0) & 7
                picked = []
                for part in range(2):
                    spot = jnp.concatenate(slot[2 * part : 2 * part + 2], axis=0) >> 3

                    def pull(start, width, floor):
                        lane = lax.broadcasted_iota(jnp.int32, (TILE, LANES), 1) + start
                        hits = []
                        for off in range(0, width, LANES):
                            hit = lane + off == spot
                            if floor is not None:
                                hit = hit & (lane + off >= floor)
                            hits.append(jnp.where(hit, 1.0, 0.0).astype(jnp.bfloat16))
                        return jnp.dot(
                            jnp.concatenate(hits, axis=1),
                            cot_ref[pl.ds(start, width), :],
                            preferred_element_type=jnp.float32,
                        )

                    rows = pull(starts[part], window, None)
                    if extra:

                        def body(n, rows):
                            floor = starts[part] + window + n * TILE
                            at = pl.multiple_of(jnp.minimum(floor, span - TILE), 16)
                            return rows + pull(at, TILE, floor)

                        count = (mosts[part] + TILE - starts[part] - window) // TILE
                        rows = lax.fori_loop(0, count, body, rows)
                    picked.append(rows.astype(jnp.bfloat16))
                spread = spread_kinds(kind, jnp.concatenate(picked, axis=0), kinds_total)
                there = pl.ds(pl.multiple_of((c - first) * size, size), size)
                outs[i][there, :] = jnp.dot(
                    spread, weight_ref[...], preferred_element_type=jnp.float32
                ).astype(jnp.bfloat16)
                part = lax.dot_general(
                    feats_ref[pl.ds(pl.multiple_of(c * size, size), size), :],
                    spread,
                    (((0,), (0,)), ((), ())),
                    preferred_element_type=jnp.float32,
                )
                for k in range(kinds_total):
                    terms_ref[k] += part[:, k * chan_out : (k + 1) * chan_out]

            pl.when(slow)(lambda: work(True))
            pl.when(jnp.logical_not(slow))(lambda: work(False))
            return carry

        lax.fori_loop(first, last, chunk, 0)
    if shares:
        per = kinds_total // shares
        for m in range(shares):
            owner = table_ref[offset + blocks + m]
            rest[m][...] = terms_ref[pl.ds(owner * per, per)].reshape(rest[m].shape)


def stage(table, offset, ends, parents, codes, feats, weight_tall, cots, priors, shares, rows):
    blocks = len(cots)
    chan_out = cots[0].shape[1]
    chan_in = feats.shape[1]
    kinds_total = weight_tall.shape[0] // chan_out
    smem = pl.BlockSpec(memory_space=pltpu.SMEM)
    vmem = pl.BlockSpec(memory_space=pltpu.VMEM)
    args = (table, ends, parents, codes, feats, weight_tall, *cots, *priors)
    outs = [jax.ShapeDtypeStruct((rows, chan_in), jnp.bfloat16)] * blocks
    scratch = []
    terms_shape = (kinds_total, chan_in, chan_out)
    if shares:
        outs += [jax.ShapeDtypeStruct((kinds_total * chan_in // shares, chan_out), jnp.float32)] * shares
        scratch = [pltpu.VMEM(terms_shape, jnp.float32)]
    else:
        outs += [jax.ShapeDtypeStruct(terms_shape, jnp.float32)]
    return pl.pallas_call(
        lambda *refs: stage_kernel(blocks, len(priors), shares, offset, *refs),
        out_shape=outs,
        in_specs=[smem, smem] + [vmem] * (len(args) - 2),
        out_specs=[vmem] * len(outs),
        scratch_shapes=scratch,
        compiler_params=pltpu.CompilerParams(vmem_limit_bytes=VMEM_LIMIT),
        name="fine_gradients",
    )(*args)


def merge_kernel(spans, offset, table_ref, parent_ref, *rest):
    out_ref = rest[-1]
    size = 2 * TILE
    out_ref[...] = jnp.zeros(out_ref.shape, out_ref.dtype)
    parents = parent_ref[...]
    for i, span in enumerate(spans):
        base = table_ref[offset + i]
        first = jnp.sum((parents < base).astype(jnp.int32)) // size
        last = (jnp.sum((parents < base + span).astype(jnp.int32)) + size - 1) // size

        def chunk(c, carry):
            here = pl.ds(pl.multiple_of(c * size, size), size)
            there = pl.ds(pl.multiple_of((c - first) * size, size), size)
            out_ref[here, :] = (
                out_ref[here, :].astype(jnp.float32) + rest[i][there, :].astype(jnp.float32)
            ).astype(out_ref.dtype)
            return carry

        lax.fori_loop(first, last, chunk, 0)


def merge(table, offset, parents, spans, parts, shape):
    vmem = pl.BlockSpec(memory_space=pltpu.VMEM)
    return pl.pallas_call(
        lambda *refs: merge_kernel(spans, offset, *refs),
        out_shape=jax.ShapeDtypeStruct(shape, jnp.bfloat16),
        in_specs=[pl.BlockSpec(memory_space=pltpu.SMEM)] + [vmem] * (1 + len(parts)),
        out_specs=vmem,
        compiler_params=pltpu.CompilerParams(vmem_limit_bytes=VMEM_LIMIT),
        name="merge_gradients",
    )(table, parents, *parts)

GATE_EARLY = 3


def after(value, *marks):
    return lax.optimization_barrier((value, *marks))[0]


def swap(value, mask, axis):
    size = lax.axis_size(axis)
    return lax.ppermute(value, axis, [(i, i ^ mask) for i in range(size)])


def pick(parts, index):
    return lax.dynamic_index_in_dim(parts, index, 0, keepdims=False)


def sum_terms(keep, send, mark):
    space_size = lax.axis_size("space")
    dp_size = lax.axis_size("dp")
    total = keep + swap(send, 1, "dp")
    trail = [("dp", 1)]
    steps = [("dp", 1 << b) for b in range(1, dp_size.bit_length() - 1)] + [("space", 1)]
    for axis, bit in steps:
        total = mark(("down", axis, bit), total)
        mine = lax.axis_index(axis) // bit % 2
        parts = total.reshape(2, total.shape[0] // 2, total.shape[1])
        total = pick(parts, mine) + swap(pick(parts, 1 - mine), bit, axis)
        trail.append((axis, bit))
    total = mark("across", total)
    if space_size == 8:
        total = (total + swap(total, 2, "space")) + (swap(total, 4, "space") + swap(total, 6, "space"))
    else:
        bit = 2
        while bit < space_size:
            total = total + swap(total, bit, "space")
            bit *= 2
    spot = lax.axis_index("dp") // 2 * 2 + lax.axis_index("space") % 2
    if dp_size == 4:
        total = mark("up", total)
        pairs = [(d * space_size + s, (d ^ 2) * space_size + (s ^ 1)) for d in range(4) for s in range(space_size)]
        by = [total, swap(total, 1, "space"), swap(total, 2, "dp"), lax.ppermute(total, ("dp", "space"), pairs)]
        wide = []
        for place in range(4):
            piece = by[0]
            for k in range(1, 4):
                piece = jnp.where(spot ^ k == place, by[k], piece)
            wide.append(piece)
        total = jnp.concatenate(wide, axis=0)
        trail = trail[:1]
    for axis, bit in trail[::-1]:
        total = mark(("up", axis, bit), total)
        mine = lax.axis_index(axis) // bit % 2
        other = swap(total, bit, axis)
        total = jnp.where(
            mine == 0, jnp.concatenate([total, other]), jnp.concatenate([other, total])
        )
    return total


def table_row(place, bit, cycle, par_rows):
    size = len(cycle)
    spot = cycle.index(place)
    row = [place * par_rows]
    for step in range(1, size // 2):
        row += [cycle[(spot - step) % size] * par_rows, cycle[(spot + step) % size] * par_rows]
    far = cycle[(spot + size // 2) % size] * par_rows
    return row + [far, far + par_rows // 2, bit, 1 - bit]


def per_device(features, child_parent, child_code, weight, out_grad):
    fine_rows = features[0]
    row_count = fine_rows.shape[0]
    parents = child_parent[0].reshape(row_count // LANES, LANES)
    codes = child_code[0].reshape(row_count // LANES, LANES)
    cotangent = out_grad[0]
    par_rows = cotangent.shape[0]
    kinds_total, chan_in, chan_out = weight.shape
    space_size = lax.axis_size("space")
    dp_size = lax.axis_size("dp")
    me = lax.axis_index("space")
    capacity = 2 * row_count // space_size
    weight_flat = weight.reshape(kinds_total * chan_in, chan_out)
    weight_tall = jnp.transpose(weight, (0, 2, 1)).reshape(kinds_total * chan_out, chan_in)
    steps = space_size // 2
    half = par_rows // 2
    cycle = list(range(0, space_size, 2)) + list(range(space_size - 1, 0, -2))
    ahead = [(cycle[i], cycle[(i + 1) % space_size]) for i in range(space_size)]
    behind = [(b, a) for a, b in ahead]
    dp_bit = lax.axis_index("dp") % 2
    table = jnp.asarray(
        [table_row(d, b, cycle, par_rows) for d in range(space_size) for b in range(2)], jnp.int32
    )
    table = lax.dynamic_index_in_dim(table, 2 * me + dp_bit, 0, keepdims=False)
    early, late = pack(parents, codes, fine_rows, space_size, capacity // 2, par_rows)

    tiles = child_parent[0].reshape(row_count // TILE, TILE)
    ends = jnp.stack([tiles[:, 0], tiles[:, TILE - 1]])
    size = 2 * TILE
    window_rows = (-(-(2 * row_count // space_size) // size) + 1) * size
    grads, spans, terms_parts = [], [], []

    def advance(step, blocks, shares=0):
        *parts, = stage(
            table, max(2 * step - 1, 0), ends, parents, codes, fine_rows, weight_tall, blocks,
            terms_parts if shares else (), shares, window_rows,
        )
        grads.extend(parts[: len(blocks)])
        spans.extend(block.shape[0] for block in blocks)
        return parts[len(blocks) :]

    def exchange(windows, mark):
        return lax.all_to_all(after(windows, mark), "space", 0, 0, tiled=True)

    right = left = cotangent
    blocks = (cotangent,)
    for step in range(1, steps + 1):
        if step == steps:
            right, left = right[:half], left[half:]
        right = lax.ppermute(right, "space", ahead)
        left = lax.ppermute(left, "space", behind)
        terms_parts += advance(step - 1, blocks)
        blocks = (right, left)
        if step < steps:
            right, left = lax.optimization_barrier((right, left, terms_parts[-1]))[:2]
        if step == GATE_EARLY:
            early = exchange(early, right)
    blocks = (blocks[0], after(blocks[1], terms_parts[-1]))
    keep, give = advance(steps, blocks, 2)
    late = lax.all_to_all(after(late, *blocks), "space", 0, 0, tiled=True)
    placed = place_children(after(early, keep), weight_flat, None, par_rows, False)
    acc = place_children(late, weight_flat, placed, par_rows, True)

    feature_grad = merge(table, 0, parents, spans, grads, fine_rows.shape)

    def mark(name, value):
        if name == ("down", "dp", 2):
            return after(value, placed)
        if name == ("up", "dp", 1):
            return after(value, acc)
        return after(value, feature_grad) if name == "across" else value

    terms = sum_terms(keep, give, mark)
    total_rows = row_count * space_size * dp_size
    summed = terms.reshape(kinds_total, chan_in, chan_out)
    weight_grad = summed / jnp.sqrt(jnp.float32(total_rows))
    return (acc[None], feature_grad[None], weight_grad)


def solution(mesh):
    placed = (
        P("dp", "space", None),
        P("dp", "space"),
        P("dp", "space"),
        P(),
        P("dp", "space", None),
    )
    return jax.shard_map(
        per_device,
        mesh=mesh,
        in_specs=placed,
        out_specs=(P("dp", "space", None), P("dp", "space", None), P()),
        check_vma=False,
    )
```

time: 364 us -> 186 us (0.51)
  local copies, waits for them, and re-layouts: 192 us -> 3.91 us
  Pallas kernels: 0 us -> 85.7 us
  other arithmetic: 52.1 us -> 3.94 us
  waiting for transfers between devices: 73 us -> 53.6 us
  starting transfers between devices: 18 us -> 36.6 us
  between operations: 14.1 us -> 0.83 us
  matrix products: 11.7 us -> 0 us
    gather x49 -> x0, local copies, waits for them, and re-layouts: 86.5 us -> none  [the longest x1 58.1 us: per_device(): jnp.take(parent_grad, recv_slots, axis=0, mode='fill', fill_value=0)]
    pallas_call x0 -> x9, Pallas kernels: none -> 85.7 us  [the longest x5 41.9 us: stage(): pl.pallas_call(lambda *refs: stage_kernel(blocks, len(priors), shares, of...]
    scatter x1 -> x0, local copies, waits for them, and re-layouts: 44 us -> none  [per_device(): slot_grid = jnp.zeros((marker, chan_in), jnp.bfloat16).at[recv_slots.resh...]
    ppermute x0 -> x18, waiting for transfers between devices: none -> 42.5 us  [the longest x4 21.7 us: per_device(): left = lax.ppermute(left, 'space', behind)]
    all_to_all x3 -> x2, waiting for transfers between devices: 51.3 us -> 11.1 us  [the longest x1 11.1 us: exchange(): return lax.all_to_all(after(windows, mark), 'space', 0, 0, tiled=True)]
    scatter-add x16 -> x0, local copies, waits for them, and re-layouts: 40.2 us -> none
    scatter-add x16 -> x0, other arithmetic: 31.6 us -> none
    ppermute x0 -> x18, starting transfers between devices: none -> 25 us  [the longest x9 15.2 us: swap(): return lax.ppermute(value, axis, [(i, i ^ mask) for i in range(size)])]
  transfers between devices with their start and end apart: 4 -> 20, of which waited for: 3 -> 12; matrix products, arithmetic and copies ran while one was open for 67% -> 4% of each run, Pallas kernels for 0% -> 46%
where the time goes in v2:
time: 186 us; the launch traced here: 185 us
  Pallas kernels  85.7 us (46%)
  waiting for transfers between devices  53.6 us (29%)
  starting transfers between devices  36.6 us (20%)
  other arithmetic  3.94 us (2%)
  local copies, waits for them, and re-layouts  3.91 us (2%)
    pallas_call x5, Pallas kernels, stage(): pl.pallas_call(lambda *refs: stage_kernel(blocks, len(priors), shares, of...  41.9 us
    pallas_call x2, Pallas kernels, place_children(): pl.pallas_call(lambda *refs: place_children_kernel(payload.shape[1] - ALI...  33.1 us
    ppermute x4, waiting for transfers between devices, per_device(): left = lax.ppermute(left, 'space', behind)  21.7 us
    ppermute x9, starting transfers between devices, swap(): return lax.ppermute(value, axis, [(i, i ^ mask) for i in range(size)])  15.2 us
    ppermute x9, waiting for transfers between devices, swap(): return lax.ppermute(value, axis, [(i, i ^ mask) for i in range(size)])  11.4 us
    all_to_all x1, waiting for transfers between devices, exchange(): return lax.all_to_all(after(windows, mark), 'space', 0, 0, tiled=True)  11.1 us
    ppermute x4, waiting for transfers between devices, per_device(): right = lax.ppermute(right, 'space', ahead)  9.33 us
    ppermute x4, starting transfers between devices, per_device(): left = lax.ppermute(left, 'space', behind)  7.29 us
  transfers between devices with their start and end apart: 20, of which 12 were waited for; matrix products, arithmetic and copies ran while one was open for 4% of the time, Pallas kernels for 46%

profile of v2, /device:TPU:0, one launch (start us, length us, event | category | flops | bytes accessed | tf_op | source)
XLA Modules:
  0.0 184.5 jit_solution(8949123058284864747)
XLA Ops:
  0.6 3.0 %collective-permute-start.1 = (bf16[2048,128]{1,0:T(8,128)(2,1)}, bf16[2048,128]{1,0:T(8,128)(2,1)S(1)}, u32[]{:S(2)}, u32[]{:S(2)}) collective-permute-start(bf16[2048,128]{1,0:T(8,128)(2,1)} %bitcast.58), channel_id=1, source_target_pairs={{2,0},{4,2},{6,4},{7,6},{5,7},{3,5},{1,3},{0,1},{10,8},{12,10},{14... | collective-permute-start | bytes 1572872 | tf_op jit(solution)/shard_map/ppermute | solution.py:472
  3.6 0.1 collective-permute-start
  3.8 0.5 broadcast.17
  4.3 1.5 reduce.3
  5.8 0.1 fusion.2
  5.9 0.1 copy.12
  5.9 0.1 copy.13
  6.0 1.8 copy.11
  7.8 1.3 fusion.1.refs_0_
  9.1 0.5 pad_add_fusion.refs_1_
  9.6 5.5 %fine_gradients.5 = (bf16[2560,128]{1,0:T(8,128)(2,1)}, f32[8,128,128]{2,1,0:T(8,128)}) custom-call(s32[11]{0:T(128)} %fusion.1.refs_0_, s32[2,32]{1,0:T(2,128)} %pad_add_fusion.refs_1_, s32[64,128]{1,0:T(8,128)} %bitcast.38, s32[64,128]{1,0:T(8,128)} %bitcast.46, bf16[8192,128]{1,0:T(8,128)(2,1)} %bitcast.24, bf16[1024,128]{1,0:T(8,128)(2,1)} %bitcast.30, ...), custom_call_target="tpu_custom_call" | custom-call | tf_op jit(solution)/shard_map/fine_gradients/pallas_call | solution.py:310
  15.1 0.8 collective-permute-done.1.refs_7_
  15.8 1.4 collective-permute-done.refs_6_
  17.2 0.4 collective-permute-start.2
  17.6 1.6 collective-permute-start.3
  19.3 0.0 copy-done.3
  19.3 0.0 copy-done.4
  19.3 10.2 %fine_gradients.6 = (bf16[2560,128]{1,0:T(8,128)(2,1)}, bf16[2560,128]{1,0:T(8,128)(2,1)}, f32[8,128,128]{2,1,0:T(8,128)}) custom-call(s32[11]{0:T(128)} %fusion.1.refs_0_, s32[2,32]{1,0:T(2,128)} %pad_add_fusion.refs_1_, s32[64,128]{1,0:T(8,128)} %bitcast.39, s32[64,128]{1,0:T(8,128)} %bitcast.47, bf16[8192,128]{1,0:T(8,128)(2,1)} %bitcast.25, ...), custom_call_target="tpu_custom_call" | custom-call | tf_op jit(solution)/shard_map/fine_gradients/pallas_call | solution.py:310
  29.5 0.3 collective-permute-done.2.refs_6_
  29.7 1.2 collective-permute-done.3.refs_7_
  31.0 1.4 collective-permute-start.4
  32.4 0.6 collective-permute-start.5
  33.0 4.4 %pack_windows.1 = (bf16[8,1040,128]{2,1,0:T(8,128)(2,1)}, bf16[8,1040,128]{2,1,0:T(8,128)(2,1)}) custom-call(s32[64,128]{1,0:T(8,128)} %bitcast.40, s32[64,128]{1,0:T(8,128)} %bitcast.48, bf16[8192,128]{1,0:T(8,128)(2,1)} %bitcast.26), custom_call_target="tpu_custom_call" | custom-call | tf_op jit(solution)/shard_map/pack_windows/pallas_call | solution.py:61
  37.4 9.0 %fine_gradients.7 = (bf16[2560,128]{1,0:T(8,128)(2,1)}, bf16[2560,128]{1,0:T(8,128)(2,1)}, f32[8,128,128]{2,1,0:T(8,128)}) custom-call(s32[11]{0:T(128)} %fusion.1.refs_0_, s32[2,32]{1,0:T(2,128)} %pad_add_fusion.refs_1_, s32[64,128]{1,0:T(8,128)} %bitcast.41, s32[64,128]{1,0:T(8,128)} %bitcast.49, bf16[8192,128]{1,0:T(8,128)(2,1)} %bitcast.27, ...), custom_call_target="tpu_custom_call" | custom-call | tf_op jit(solution)/shard_map/fine_gradients/pallas_call | solution.py:310
  46.4 0.0 collective-permute-done.4.refs_6_
  46.4 0.0 collective-permute-done.5.refs_7_
  46.4 0.0 copy-start.2
  46.4 4.8 %all-to-all-start.1 = ((bf16[8,1040,128]{2,1,0:T(8,128)(2,1)}), bf16[8,1040,128]{2,1,0:T(8,128)(2,1)S(1)}, u32[]{:S(2)}, u32[]{:S(2)}) async-start(bf16[8,1040,128]{2,1,0:T(8,128)(2,1)} %get-tuple-element.47), calls=%async_computation.1 | async-start | bytes 4259840 | tf_op jit(solution)/shard_map/all_to_all | solution.py:464
  51.3 2.1 %collective-permute-start.7 = (bf16[1024,128]{1,0:T(8,128)(2,1)S(1)}, bf16[1024,128]{1,0:T(8,128)(2,1)S(1)}, u32[]{:S(2)}, u32[]{:S(2)}) collective-permute-start(bf16[1024,128]{1,0:T(8,128)(2,1)S(1)} %slice.15), channel_id=1, source_target_pairs={{2,0},{4,2},{6,4},{7,6},{5,7},{3,5},{1,3},{0,1},{10,8},{12,10},{14... | collective-permute-start | bytes 786440 | tf_op jit(solution)/shard_map/ppermute | solution.py:472
  53.4 0.0 copy-done.1
  53.4 0.1 collective-permute-start.6
  53.5 9.7 %fine_gradients.8 = (bf16[2560,128]{1,0:T(8,128)(2,1)}, bf16[2560,128]{1,0:T(8,128)(2,1)}, f32[8,128,128]{2,1,0:T(8,128)}) custom-call(s32[11]{0:T(128)} %fusion.1.refs_0_, s32[2,32]{1,0:T(2,128)} %pad_add_fusion.refs_1_, s32[64,128]{1,0:T(8,128)} %bitcast.42, s32[64,128]{1,0:T(8,128)} %bitcast.50, bf16[8192,128]{1,0:T(8,128)(2,1)} %bitcast.28, ...), custom_call_target="tpu_custom_call" | custom-call | tf_op jit(solution)/shard_map/fine_gradients/pallas_call | solution.py:310
  63.2 19.7 %collective-permute-done.7.refs_7_ = bf16[1024,128]{1,0:T(8,128)(2,1)S(1)} collective-permute-done((bf16[1024,128]{1,0:T(8,128)(2,1)S(1)}, bf16[1024,128]{1,0:T(8,128)(2,1)S(1)}, u32[]{:S(2)}, u32[]{:S(2)}) %collective-permute-start.7) | collective-permute-done | bytes 262176 | tf_op jit(solution)/shard_map/ppermute | solution.py:472
  82.9 7.7 %collective-permute-done.6.refs_6_ = bf16[1024,128]{1,0:T(8,128)(2,1)S(1)} collective-permute-done((bf16[1024,128]{1,0:T(8,128)(2,1)S(1)}, bf16[1024,128]{1,0:T(8,128)(2,1)S(1)}, u32[]{:S(2)}, u32[]{:S(2)}) %collective-permute-start.6) | collective-permute-done | bytes 262176 | tf_op jit(solution)/shard_map/ppermute | solution.py:471
  90.5 11.1 %all-to-all-done.1.refs_0_ = bf16[8,1040,128]{2,1,0:T(8,128)(2,1)S(1)} async-done(((bf16[8,1040,128]{2,1,0:T(8,128)(2,1)}), bf16[8,1040,128]{2,1,0:T(8,128)(2,1)S(1)}, u32[]{:S(2)}, u32[]{:S(2)}) %all-to-all-start.1) | async-done | bytes 2129952 | tf_op jit(solution)/shard_map/all_to_all | solution.py:464
  101.6 0.0 copy-done.8
  101.6 6.8 %all-to-all-start = ((bf16[8,1040,128]{2,1,0:T(8,128)(2,1)}), bf16[8,1040,128]{2,1,0:T(8,128)(2,1)}, u32[]{:S(2)}, u32[]{:S(2)}) async-start(bf16[8,1040,128]{2,1,0:T(8,128)(2,1)} %get-tuple-element.45), calls=%async_computation | async-start | bytes 4259840 | tf_op jit(solution)/shard_map/all_to_all | solution.py:481
  108.4 7.5 %fine_gradients.9 = (bf16[2560,128]{1,0:T(8,128)(2,1)}, bf16[2560,128]{1,0:T(8,128)(2,1)}, f32[512,128]{1,0:T(8,128)}, f32[512,128]{1,0:T(8,128)}) custom-call(s32[11]{0:T(128)} %fusion.1.refs_0_, s32[2,32]{1,0:T(2,128)} %pad_add_fusion.refs_1_, s32[64,128]{1,0:T(8,128)} %bitcast.43, s32[64,128]{1,0:T(8,128)} %bitcast.51, bf16[8192,128]{1,0:T(8,128)(2,1)} %bitcast.29, ...), custom_call_target="tpu_custom_call" | custom-call | tf_op jit(solution)/shard_map/fine_gradients/pallas_call | solution.py:310
  116.0 0.1 collective-permute-start.8
  116.1 1.7 collective-permute-done.8
  117.8 1.0 add.64
  118.8 21.4 %place_children.2.refs_2_ = f32[2048,128]{1,0:T(8,128)} custom-call(bf16[8,1040,128]{2,1,0:T(8,128)(2,1)} %copy-done, bf16[1024,128]{1,0:T(8,128)(2,1)} %bitcast.36), custom_call_target="tpu_custom_call" | custom-call | tf_op jit(solution)/shard_map/place_children/pallas_call | solution.py:183
  140.2 4.7 %collective-permute-start.9 = (f32[256,128]{1,0:T(8,128)S(1)}, f32[256,128]{1,0:T(8,128)S(1)}, u32[]{:S(2)}, u32[]{:S(2)}) collective-permute-start(f32[256,128]{1,0:T(8,128)S(1)} %dynamic-slice_bitcast_fusion), channel_id=1, source_target_pairs={{0,16},{8,24},{16,0},{24,8},{1,17},{9,25},{17,1},{25,9},{2,18},{10... | collective-permute-start | bytes 393224 | tf_op jit(solution)/shard_map/ppermute | solution.py:362
  144.8 3.4 %collective-permute-done.9 = f32[256,128]{1,0:T(8,128)S(1)} collective-permute-done((f32[256,128]{1,0:T(8,128)S(1)}, f32[256,128]{1,0:T(8,128)S(1)}, u32[]{:S(2)}, u32[]{:S(2)}) %collective-permute-start.9) | collective-permute-done | bytes 131104 | tf_op jit(solution)/shard_map/ppermute | solution.py:362
  148.3 2.8 %collective-permute-start.10 = (f32[128,128]{1,0:T(8,128)S(1)}, f32[128,128]{1,0:T(8,128)S(1)}, u32[]{:S(2)}, u32[]{:S(2)}) collective-permute-start(f32[128,128]{1,0:T(8,128)S(1)} %dynamic-slice_bitcast_fusion.1), channel_id=1, source_target_pairs={{0,1},{1,0},{2,3},{3,2},{4,5},{5,4},{6,7},{7,6},{8,9},{9,8},{10,11... | collective-permute-start | bytes 196616 | tf_op jit(solution)/shard_map/ppermute | solution.py:362
  151.1 6.3 %merge_gradients.1 = bf16[8192,128]{1,0:T(8,128)(2,1)} custom-call(s32[11]{0:T(128)} %fusion.1.refs_0_, s32[64,128]{1,0:T(8,128)} %bitcast.44, bf16[2560,128]{1,0:T(8,128)(2,1)} %get-tuple-element.50.refs_2_, bf16[2560,128]{1,0:T(8,128)(2,1)} %get-tuple-element.51.refs_3_, bf16[2560,128]{1,0:T(8,128)(2,1)} %get-tuple-element.52.refs_4_, ...), custom_call_target="tpu_custom_call" | custom-call | tf_op jit(solution)/shard_map/merge_gradients/pallas_call | solution.py:344
  157.4 0.0 collective-permute-done.10
  157.4 2.5 %collective-permute-start.13 = (f32[128,128]{1,0:T(8,128)S(1)}, f32[128,128]{1,0:T(8,128)S(1)}, u32[]{:S(2)}, u32[]{:S(2)}) collective-permute-start(f32[128,128]{1,0:T(8,128)S(1)} %bitcast_add_fusion.1), channel_id=1, source_target_pairs={{0,6},{1,7},{2,4},{3,5},{4,2},{5,3},{6,0},{7,1},{8,14},{9,15},{10,... | collective-permute-start | bytes 196616 | tf_op jit(solution)/shard_map/ppermute | solution.py:362
  159.9 1.7 collective-permute-start.12
  161.5 0.3 collective-permute-start.11
  161.9 2.4 %collective-permute-done.13 = f32[128,128]{1,0:T(8,128)S(1)} collective-permute-done((f32[128,128]{1,0:T(8,128)S(1)}, f32[128,128]{1,0:T(8,128)S(1)}, u32[]{:S(2)}, u32[]{:S(2)}) %collective-permute-start.13) | collective-permute-done | bytes 65568 | tf_op jit(solution)/shard_map/ppermute | solution.py:362
  164.2 2.4 %collective-permute-done.12 = f32[128,128]{1,0:T(8,128)S(1)} collective-permute-done((f32[128,128]{1,0:T(8,128)S(1)}, f32[128,128]{1,0:T(8,128)S(1)}, u32[]{:S(2)}, u32[]{:S(2)}) %collective-permute-start.12) | collective-permute-done | bytes 65568 | tf_op jit(solution)/shard_map/ppermute | solution.py:362
  166.6 0.0 collective-permute-done.11
  166.6 1.4 collective-permute-start.16
  168.0 1.7 collective-permute-start.15
  169.7 0.5 collective-permute-start.14
  170.2 0.0 all-to-all-done.refs_0_
  170.2 11.8 %place_children.3 = bf16[2048,128]{1,0:T(8,128)(2,1)} custom-call(bf16[8,1040,128]{2,1,0:T(8,128)(2,1)} %all-to-all-done.refs_0_, bf16[1024,128]{1,0:T(8,128)(2,1)} %bitcast.37, f32[2048,128]{1,0:T(8,128)} %place_children.2.refs_2_), custom_call_target="tpu_custom_call" | custom-call | tf_op jit(solution)/shard_map/place_children/pallas_call | solution.py:183
  182.0 0.0 collective-permute-done.16
  182.0 0.0 collective-permute-done.15
  182.0 0.0 collective-permute-done.14
  182.1 0.1 collective-permute-start.17
  182.2 1.5 collective-permute-done.17
  183.7 0.8 fusion
  (23 shorter events, 0.2 us)
Async XLA Ops:
  0.6 15.2 %collective-permute-start.1 = (bf16[2048,128]{1,0:T(8,128)(2,1)}, bf16[2048,128]{1,0:T(8,128)(2,1)S(1)}, u32[]{:S(2)}, u32[]{:S(2)}) collective-permute-start(bf16[2048,128]{1,0:T(8,128)(2,1)} %bitcast.58), channel_id=1, source_target_pairs={{2,0},{4,2},{6,4},{7,6},{5,7},{3,5},{1,3},{0,1},{10,8},{12,10},{14... | collective-permute-start | bytes 1572872 | tf_op jit(solution)/shard_map/ppermute | solution.py:472
  3.6 13.6 %collective-permute-start = (bf16[2048,128]{1,0:T(8,128)(2,1)}, bf16[2048,128]{1,0:T(8,128)(2,1)S(1)}, u32[]{:S(2)}, u32[]{:S(2)}) collective-permute-start(bf16[2048,128]{1,0:T(8,128)(2,1)} %bitcast.59), channel_id=1, source_target_pairs={{0,2},{2,4},{4,6},{6,7},{7,5},{5,3},{3,1},{1,0},{8,10},{10,12},{12... | collective-permute-start | bytes 1572872 | tf_op jit(solution)/shard_map/ppermute | solution.py:471
  15.8 3.4 %copy-start.3 = (bf16[2048,128]{1,0:T(8,128)(2,1)}, bf16[2048,128]{1,0:T(8,128)(2,1)S(1)}, u32[]{:S(2)}) copy-start(bf16[2048,128]{1,0:T(8,128)(2,1)S(1)} %collective-permute-done.1.refs_7_) | copy-start | bytes 1572868
  17.2 2.0 %copy-start.4 = (bf16[2048,128]{1,0:T(8,128)(2,1)}, bf16[2048,128]{1,0:T(8,128)(2,1)S(1)}, u32[]{:S(2)}) copy-start(bf16[2048,128]{1,0:T(8,128)(2,1)S(1)} %collective-permute-done.refs_6_) | copy-start | bytes 1572868
  17.2 12.5 %collective-permute-start.2 = (bf16[2048,128]{1,0:T(8,128)(2,1)S(1)}, bf16[2048,128]{1,0:T(8,128)(2,1)S(1)}, u32[]{:S(2)}, u32[]{:S(2)}) collective-permute-start(bf16[2048,128]{1,0:T(8,128)(2,1)S(1)} %collective-permute-done.refs_6_), channel_id=1, source_target_pairs={{0,2},{2,4},{4,6},{6,7},{7,5},{5,3},{3,1},{1,0},{8,10},{10,12},{12... | collective-permute-start | bytes 1572872 | tf_op jit(solution)/shard_map/ppermute | solution.py:471
  17.6 13.3 %collective-permute-start.3 = (bf16[2048,128]{1,0:T(8,128)(2,1)S(1)}, bf16[2048,128]{1,0:T(8,128)(2,1)S(1)}, u32[]{:S(2)}, u32[]{:S(2)}) collective-permute-start(bf16[2048,128]{1,0:T(8,128)(2,1)S(1)} %collective-permute-done.1.refs_7_), channel_id=1, source_target_pairs={{2,0},{4,2},{6,4},{7,6},{5,7},{3,5},{1,3},{0,1},{10,8},{12,10},{14... | collective-permute-start | bytes 1572872 | tf_op jit(solution)/shard_map/ppermute | solution.py:472
  29.7 7.7 %copy-start.5 = (bf16[2048,128]{1,0:T(8,128)(2,1)}, bf16[2048,128]{1,0:T(8,128)(2,1)S(1)}, u32[]{:S(2)}) copy-start(bf16[2048,128]{1,0:T(8,128)(2,1)S(1)} %collective-permute-done.2.refs_6_) | copy-start | bytes 1572868
  31.0 6.4 %copy-start.6 = (bf16[2048,128]{1,0:T(8,128)(2,1)}, bf16[2048,128]{1,0:T(8,128)(2,1)S(1)}, u32[]{:S(2)}) copy-start(bf16[2048,128]{1,0:T(8,128)(2,1)S(1)} %collective-permute-done.3.refs_7_) | copy-start | bytes 1572868
  31.0 15.4 %collective-permute-start.4 = (bf16[2048,128]{1,0:T(8,128)(2,1)S(1)}, bf16[2048,128]{1,0:T(8,128)(2,1)S(1)}, u32[]{:S(2)}, u32[]{:S(2)}) collective-permute-start(bf16[2048,128]{1,0:T(8,128)(2,1)S(1)} %collective-permute-done.2.refs_6_), channel_id=1, source_target_pairs={{0,2},{2,4},{4,6},{6,7},{7,5},{5,3},{3,1},{1,0},{8,10},{10,12},{12... | collective-permute-start | bytes 1572872 | tf_op jit(solution)/shard_map/ppermute | solution.py:471
  32.4 14.0 %collective-permute-start.5 = (bf16[2048,128]{1,0:T(8,128)(2,1)S(1)}, bf16[2048,128]{1,0:T(8,128)(2,1)S(1)}, u32[]{:S(2)}, u32[]{:S(2)}) collective-permute-start(bf16[2048,128]{1,0:T(8,128)(2,1)S(1)} %collective-permute-done.3.refs_7_), channel_id=1, source_target_pairs={{2,0},{4,2},{6,4},{7,6},{5,7},{3,5},{1,3},{0,1},{10,8},{12,10},{14... | collective-permute-start | bytes 1572872 | tf_op jit(solution)/shard_map/ppermute | solution.py:472
  46.4 6.9 %copy-start.1 = (bf16[2048,128]{1,0:T(8,128)(2,1)}, bf16[2048,128]{1,0:T(8,128)(2,1)S(1)}, u32[]{:S(2)}) copy-start(bf16[2048,128]{1,0:T(8,128)(2,1)S(1)} %collective-permute-done.4.refs_6_) | copy-start | bytes 1572868
  46.4 4.8 %copy-start.2 = (bf16[2048,128]{1,0:T(8,128)(2,1)}, bf16[2048,128]{1,0:T(8,128)(2,1)S(1)}, u32[]{:S(2)}) copy-start(bf16[2048,128]{1,0:T(8,128)(2,1)S(1)} %collective-permute-done.5.refs_7_) | copy-start | bytes 1572868
  46.4 55.2 %all-to-all-start.1 = ((bf16[8,1040,128]{2,1,0:T(8,128)(2,1)}), bf16[8,1040,128]{2,1,0:T(8,128)(2,1)S(1)}, u32[]{:S(2)}, u32[]{:S(2)}) async-start(bf16[8,1040,128]{2,1,0:T(8,128)(2,1)} %get-tuple-element.47), calls=%async_computation.1 | async-start | bytes 4259840 | tf_op jit(solution)/shard_map/all_to_all | solution.py:464
  51.3 31.6 %collective-permute-start.7 = (bf16[1024,128]{1,0:T(8,128)(2,1)S(1)}, bf16[1024,128]{1,0:T(8,128)(2,1)S(1)}, u32[]{:S(2)}, u32[]{:S(2)}) collective-permute-start(bf16[1024,128]{1,0:T(8,128)(2,1)S(1)} %slice.15), channel_id=1, source_target_pairs={{2,0},{4,2},{6,4},{7,6},{5,7},{3,5},{1,3},{0,1},{10,8},{12,10},{14... | collective-permute-start | bytes 786440 | tf_op jit(solution)/shard_map/ppermute | solution.py:472
  53.4 37.2 %collective-permute-start.6 = (bf16[1024,128]{1,0:T(8,128)(2,1)S(1)}, bf16[1024,128]{1,0:T(8,128)(2,1)S(1)}, u32[]{:S(2)}, u32[]{:S(2)}) collective-permute-start(bf16[1024,128]{1,0:T(8,128)(2,1)S(1)} %slice.14), channel_id=1, source_target_pairs={{0,2},{2,4},{4,6},{6,7},{7,5},{5,3},{3,1},{1,0},{8,10},{10,12},{12... | collective-permute-start | bytes 786440 | tf_op jit(solution)/shard_map/ppermute | solution.py:471
  82.9 18.8 %copy-start.7 = (bf16[1024,128]{1,0:T(8,128)(2,1)}, bf16[1024,128]{1,0:T(8,128)(2,1)S(1)}, u32[]{:S(2)}) copy-start(bf16[1024,128]{1,0:T(8,128)(2,1)S(1)} %collective-permute-done.7.refs_7_) | copy-start | bytes 786436
  90.5 11.1 %copy-start.8 = (bf16[1024,128]{1,0:T(8,128)(2,1)}, bf16[1024,128]{1,0:T(8,128)(2,1)S(1)}, u32[]{:S(2)}) copy-start(bf16[1024,128]{1,0:T(8,128)(2,1)S(1)} %collective-permute-done.6.refs_6_) | copy-start | bytes 786436
  101.6 14.4 %copy-start = (bf16[8,1040,128]{2,1,0:T(8,128)(2,1)}, bf16[8,1040,128]{2,1,0:T(8,128)(2,1)S(1)}, u32[]{:S(2)}) copy-start(bf16[8,1040,128]{2,1,0:T(8,128)(2,1)S(1)} %all-to-all-done.1.refs_0_) | copy-start | bytes 6389764
  101.6 68.6 %all-to-all-start = ((bf16[8,1040,128]{2,1,0:T(8,128)(2,1)}), bf16[8,1040,128]{2,1,0:T(8,128)(2,1)}, u32[]{:S(2)}, u32[]{:S(2)}) async-start(bf16[8,1040,128]{2,1,0:T(8,128)(2,1)} %get-tuple-element.45), calls=%async_computation | async-start | bytes 4259840 | tf_op jit(solution)/shard_map/all_to_all | solution.py:481
  116.0 1.8 collective-permute-start.8
  140.2 8.1 %collective-permute-start.9 = (f32[256,128]{1,0:T(8,128)S(1)}, f32[256,128]{1,0:T(8,128)S(1)}, u32[]{:S(2)}, u32[]{:S(2)}) collective-permute-start(f32[256,128]{1,0:T(8,128)S(1)} %dynamic-slice_bitcast_fusion), channel_id=1, source_target_pairs={{0,16},{8,24},{16,0},{24,8},{1,17},{9,25},{17,1},{25,9},{2,18},{10... | collective-permute-start | bytes 393224 | tf_op jit(solution)/shard_map/ppermute | solution.py:362
  148.3 9.1 %collective-permute-start.10 = (f32[128,128]{1,0:T(8,128)S(1)}, f32[128,128]{1,0:T(8,128)S(1)}, u32[]{:S(2)}, u32[]{:S(2)}) collective-permute-start(f32[128,128]{1,0:T(8,128)S(1)} %dynamic-slice_bitcast_fusion.1), channel_id=1, source_target_pairs={{0,1},{1,0},{2,3},{3,2},{4,5},{5,4},{6,7},{7,6},{8,9},{9,8},{10,11... | collective-permute-start | bytes 196616 | tf_op jit(solution)/shard_map/ppermute | solution.py:362
  157.4 6.8 %collective-permute-start.13 = (f32[128,128]{1,0:T(8,128)S(1)}, f32[128,128]{1,0:T(8,128)S(1)}, u32[]{:S(2)}, u32[]{:S(2)}) collective-permute-start(f32[128,128]{1,0:T(8,128)S(1)} %bitcast_add_fusion.1), channel_id=1, source_target_pairs={{0,6},{1,7},{2,4},{3,5},{4,2},{5,3},{6,0},{7,1},{8,14},{9,15},{10,... | collective-permute-start | bytes 196616 | tf_op jit(solution)/shard_map/ppermute | solution.py:362
  159.9 6.7 %collective-permute-start.12 = (f32[128,128]{1,0:T(8,128)S(1)}, f32[128,128]{1,0:T(8,128)S(1)}, u32[]{:S(2)}, u32[]{:S(2)}) collective-permute-start(f32[128,128]{1,0:T(8,128)S(1)} %bitcast_add_fusion.1), channel_id=1, source_target_pairs={{0,4},{1,5},{2,6},{3,7},{4,0},{5,1},{6,2},{7,3},{8,12},{9,13},{10,... | collective-permute-start | bytes 196616 | tf_op jit(solution)/shard_map/ppermute | solution.py:362
  161.5 5.1 %collective-permute-start.11 = (f32[128,128]{1,0:T(8,128)S(1)}, f32[128,128]{1,0:T(8,128)S(1)}, u32[]{:S(2)}, u32[]{:S(2)}) collective-permute-start(f32[128,128]{1,0:T(8,128)S(1)} %bitcast_add_fusion.1), channel_id=1, source_target_pairs={{0,2},{1,3},{2,0},{3,1},{4,6},{5,7},{6,4},{7,5},{8,10},{9,11},{10,... | collective-permute-start | bytes 196616 | tf_op jit(solution)/shard_map/ppermute | solution.py:362
  166.6 15.3 %collective-permute-start.16 = (f32[128,128]{1,0:T(8,128)S(1)}, f32[128,128]{1,0:T(8,128)S(1)}, u32[]{:S(2)}, u32[]{:S(2)}) collective-permute-start(f32[128,128]{1,0:T(8,128)S(1)} %add_add_fusion), channel_id=1, source_target_pairs={{0,1},{1,0},{2,3},{3,2},{4,5},{5,4},{6,7},{7,6},{8,9},{9,8},{10,11... | collective-permute-start | bytes 196616 | tf_op jit(solution)/shard_map/ppermute | solution.py:362
  168.0 14.0 %collective-permute-start.15 = (f32[128,128]{1,0:T(8,128)S(1)}, f32[128,128]{1,0:T(8,128)S(1)}, u32[]{:S(2)}, u32[]{:S(2)}) collective-permute-start(f32[128,128]{1,0:T(8,128)S(1)} %add_add_fusion), channel_id=1, source_target_pairs={{0,16},{8,24},{16,0},{24,8},{1,17},{9,25},{17,1},{25,9},{2,18},{10... | collective-permute-start | bytes 196616 | tf_op jit(solution)/shard_map/ppermute | solution.py:362
  169.7 12.3 %collective-permute-start.14 = (f32[128,128]{1,0:T(8,128)S(1)}, f32[128,128]{1,0:T(8,128)S(1)}, u32[]{:S(2)}, u32[]{:S(2)}) collective-permute-start(f32[128,128]{1,0:T(8,128)S(1)} %add_add_fusion), channel_id=1, source_target_pairs={{0,17},{1,16},{2,19},{3,18},{4,21},{5,20},{6,23},{7,22},{8,25},{9,... | collective-permute-start | bytes 196616 | tf_op jit(solution)/shard_map/ppermute | solution.py:393
  182.1 1.6 collective-permute-start.17

commit v3 on v2

--- a/solution.py
+++ b/solution.py
@@ -95,7 +95,7 @@
     size = min(2 * TILE, half)
     parts = size // TILE
     per = TILE // LANES
-    window = min(5 * TILE // 2, par_rows)
+    window = min((5 if first else 3) * TILE // 2, par_rows)
     meta = payload_ref[:, half : half + ALIGN, :].astype(jnp.float32).astype(jnp.int32)
     rel = meta[:, 0:8] * 16 + (meta[:, 8:16] >> 3)
     line = lax.broadcasted_iota(jnp.int32, rel.shape, 1)
@@ -104,8 +104,17 @@
     code_ref[...] = (meta[:, 8:16] & 7).reshape(8 * sources, LANES)
     least = jnp.min(jnp.maximum(rel, 0), axis=1, keepdims=True)
     most = jnp.max(jnp.where(rel < par_rows, rel, -1), axis=1, keepdims=True)
-    ends_vmem[0] = jnp.broadcast_to(least, rel.shape)
-    ends_vmem[1] = jnp.broadcast_to(most, rel.shape)
+    for side, value in enumerate((least, most)):
+        value = jnp.broadcast_to(value.astype(jnp.float32), rel.shape)
+        if value.shape[0] % LANES:
+            value = jnp.concatenate([value] * (LANES // value.shape[0]), axis=0)
+        for i in range(value.shape[0] // LANES):
+            turned = jnp.transpose(value[i * LANES : (i + 1) * LANES])
+            ends_vmem[side, i] = turned[0:8].astype(jnp.int32)
+
+    def end_of(side, line):
+        return ends_ref[side, line // LANES, 0, line % LANES]
+
     copy = pltpu.make_async_copy(ends_vmem, ends_ref, sem)
     copy.start()
     total_ref[...] = jnp.zeros(total_ref.shape, jnp.float32)
@@ -119,11 +128,11 @@
         c = step % chunks
         line0 = 8 * s + c * (size // LANES)
         mosts = [
-            jnp.maximum(ends_ref[1, line0 + per * p, 0], ends_ref[1, line0 + per * p + per - 1, 0])
+            jnp.maximum(end_of(1, line0 + per * p), end_of(1, line0 + per * p + per - 1))
             for p in range(parts)
         ]
         starts = [
-            pl.multiple_of(jnp.minimum(ends_ref[0, line0 + per * p, 0] // 8 * 8, par_rows - window), 8)
+            pl.multiple_of(jnp.minimum(end_of(0, line0 + per * p) // 8 * 8, par_rows - window), 8)
             for p in range(parts)
         ]
         slow = mosts[0] >= starts[0] + window
@@ -189,8 +198,8 @@
             pltpu.VMEM((par_rows, 2 * chan_out), jnp.float32),
             pltpu.VMEM((8 * sources, LANES), jnp.int32),
             pltpu.VMEM((8 * sources, LANES), jnp.int32),
-            pltpu.VMEM((2, 8 * sources, LANES), jnp.int32),
-            pltpu.SMEM((2, 8 * sources, LANES), jnp.int32),
+            pltpu.VMEM((2, -(-8 * sources // LANES), 8, LANES), jnp.int32),
+            pltpu.SMEM((2, -(-8 * sources // LANES), 8, LANES), jnp.int32),
             pltpu.SemaphoreType.DMA(()),
         ],
         compiler_params=pltpu.CompilerParams(vmem_limit_bytes=VMEM_LIMIT),
@@ -351,6 +360,7 @@
     )(table, parents, *parts)
 
 GATE_EARLY = 3
+LAST = ("up", "dp", 1)
 
 
 def after(value, *marks):
@@ -487,7 +497,7 @@
     def mark(name, value):
         if name == ("down", "dp", 2):
             return after(value, placed)
-        if name == ("up", "dp", 1):
+        if name == LAST:
             return after(value, acc)
         return after(value, feature_grad) if name == "across" else value
 

time: 186 us -> 183 us (0.984)
  Pallas kernels: 85.7 us -> 82.9 us
  waiting for transfers between devices: 53.6 us -> 56.4 us
  starting transfers between devices: 36.6 us -> 34.5 us
    ppermute x9, starting transfers between devices: 15.2 us -> 9.21 us  [swap(): return lax.ppermute(value, axis, [(i, i ^ mask) for i in range(size)])]
    ppermute x1, starting transfers between devices: 0.49 us -> 2.84 us  [sum_terms(): lax.ppermute(total, ('dp', 'space'), pairs)]
  transfers between devices with their start and end apart: 20 -> 20, of which waited for: 12 -> 12; matrix products, arithmetic and copies ran while one was open for 4% -> 4% of each run, Pallas kernels for 46% -> 45%
where the time goes in v3:
time: 183 us
  Pallas kernels  82.9 us (45%)
  waiting for transfers between devices  56.4 us (31%)
  starting transfers between devices  34.5 us (19%)
  other arithmetic  3.94 us (2%)
  local copies, waits for them, and re-layouts  3.91 us (2%)
    pallas_call x5, Pallas kernels, stage(): pl.pallas_call(lambda *refs: stage_kernel(blocks, len(priors), shares, of...  40.6 us
    pallas_call x2, Pallas kernels, place_children(): pl.pallas_call(lambda *refs: place_children_kernel(payload.shape[1] - ALI...  31.7 us
    ppermute x4, waiting for transfers between devices, per_device(): left = lax.ppermute(left, 'space', behind)  22.7 us
    ppermute x9, waiting for transfers between devices, swap(): return lax.ppermute(value, axis, [(i, i ^ mask) for i in range(size)])  12.6 us
    all_to_all x1, waiting for transfers between devices, exchange(): return lax.all_to_all(after(windows, mark), 'space', 0, 0, tiled=True)  11.6 us
    ppermute x4, waiting for transfers between devices, per_device(): right = lax.ppermute(right, 'space', ahead)  9.48 us
    ppermute x9, starting transfers between devices, swap(): return lax.ppermute(value, axis, [(i, i ^ mask) for i in range(size)])  9.21 us
    ppermute x4, starting transfers between devices, per_device(): left = lax.ppermute(left, 'space', behind)  6.71 us
  transfers between devices with their start and end apart: 20, of which 12 were waited for; matrix products, arithmetic and copies ran while one was open for 4% of the time, Pallas kernels for 45%

profile of v3, /device:TPU:0, one launch (start us, length us, event | category | flops | bytes accessed | tf_op | source)
XLA Modules:
  0.0 182.6 jit_solution(935095067196105197)
XLA Ops:
  0.6 3.0 %collective-permute-start.1 = (bf16[2048,128]{1,0:T(8,128)(2,1)}, bf16[2048,128]{1,0:T(8,128)(2,1)S(1)}, u32[]{:S(2)}, u32[]{:S(2)}) collective-permute-start(bf16[2048,128]{1,0:T(8,128)(2,1)} %bitcast.58), channel_id=1, source_target_pairs={{2,0},{4,2},{6,4},{7,6},{5,7},{3,5},{1,3},{0,1},{10,8},{12,10},{14... | collective-permute-start | bytes 1572872 | tf_op jit(solution)/shard_map/ppermute | solution.py:482
  3.6 0.1 collective-permute-start
  3.8 0.5 broadcast.17
  4.3 1.5 reduce.3
  5.8 0.1 fusion.2
  5.9 0.1 copy.12
  5.9 0.1 copy.13
  6.0 1.8 copy.11
  7.8 1.3 fusion.1.refs_0_
  9.1 0.5 pad_add_fusion.refs_1_
  9.6 5.1 %fine_gradients.5 = (bf16[2560,128]{1,0:T(8,128)(2,1)}, f32[8,128,128]{2,1,0:T(8,128)}) custom-call(s32[11]{0:T(128)} %fusion.1.refs_0_, s32[2,32]{1,0:T(2,128)} %pad_add_fusion.refs_1_, s32[64,128]{1,0:T(8,128)} %bitcast.38, s32[64,128]{1,0:T(8,128)} %bitcast.46, bf16[8192,128]{1,0:T(8,128)(2,1)} %bitcast.24, bf16[1024,128]{1,0:T(8,128)(2,1)} %bitcast.30, ...), custom_call_target="tpu_custom_call" | custom-call | tf_op jit(solution)/shard_map/fine_gradients/pallas_call | solution.py:319
  14.7 1.1 collective-permute-done.1.refs_7_
  15.8 1.4 collective-permute-done.refs_6_
  17.2 0.4 collective-permute-start.2
  17.6 1.6 collective-permute-start.3
  19.3 0.0 copy-done.3
  19.3 9.8 %fine_gradients.6 = (bf16[2560,128]{1,0:T(8,128)(2,1)}, bf16[2560,128]{1,0:T(8,128)(2,1)}, f32[8,128,128]{2,1,0:T(8,128)}) custom-call(s32[11]{0:T(128)} %fusion.1.refs_0_, s32[2,32]{1,0:T(2,128)} %pad_add_fusion.refs_1_, s32[64,128]{1,0:T(8,128)} %bitcast.39, s32[64,128]{1,0:T(8,128)} %bitcast.47, bf16[8192,128]{1,0:T(8,128)(2,1)} %bitcast.25, ...), custom_call_target="tpu_custom_call" | custom-call | tf_op jit(solution)/shard_map/fine_gradients/pallas_call | solution.py:319
  29.1 0.7 collective-permute-done.2.refs_6_
  29.7 0.4 collective-permute-done.3.refs_7_
  30.2 3.1 %collective-permute-start.4 = (bf16[2048,128]{1,0:T(8,128)(2,1)S(1)}, bf16[2048,128]{1,0:T(8,128)(2,1)S(1)}, u32[]{:S(2)}, u32[]{:S(2)}) collective-permute-start(bf16[2048,128]{1,0:T(8,128)(2,1)S(1)} %collective-permute-done.2.refs_6_), channel_id=1, source_target_pairs={{0,2},{2,4},{4,6},{6,7},{7,5},{5,3},{3,1},{1,0},{8,10},{10,12},{12... | collective-permute-start | bytes 1572872 | tf_op jit(solution)/shard_map/ppermute | solution.py:481
  33.3 0.0 collective-permute-start.5
  33.3 4.4 %pack_windows.1 = (bf16[8,1040,128]{2,1,0:T(8,128)(2,1)}, bf16[8,1040,128]{2,1,0:T(8,128)(2,1)}) custom-call(s32[64,128]{1,0:T(8,128)} %bitcast.40, s32[64,128]{1,0:T(8,128)} %bitcast.48, bf16[8192,128]{1,0:T(8,128)(2,1)} %bitcast.26), custom_call_target="tpu_custom_call" | custom-call | tf_op jit(solution)/shard_map/pack_windows/pallas_call | solution.py:61
  37.7 0.0 copy-done.5
  37.7 0.0 copy-done.6
  37.7 9.0 %fine_gradients.7 = (bf16[2560,128]{1,0:T(8,128)(2,1)}, bf16[2560,128]{1,0:T(8,128)(2,1)}, f32[8,128,128]{2,1,0:T(8,128)}) custom-call(s32[11]{0:T(128)} %fusion.1.refs_0_, s32[2,32]{1,0:T(2,128)} %pad_add_fusion.refs_1_, s32[64,128]{1,0:T(8,128)} %bitcast.41, s32[64,128]{1,0:T(8,128)} %bitcast.49, bf16[8192,128]{1,0:T(8,128)(2,1)} %bitcast.27, ...), custom_call_target="tpu_custom_call" | custom-call | tf_op jit(solution)/shard_map/fine_gradients/pallas_call | solution.py:319
  46.7 0.0 collective-permute-done.4.refs_6_
  46.7 0.0 collective-permute-done.5.refs_7_
  46.7 0.0 copy-start.2
  46.7 5.7 %all-to-all-start.1 = ((bf16[8,1040,128]{2,1,0:T(8,128)(2,1)}), bf16[8,1040,128]{2,1,0:T(8,128)(2,1)S(1)}, u32[]{:S(2)}, u32[]{:S(2)}) async-start(bf16[8,1040,128]{2,1,0:T(8,128)(2,1)} %get-tuple-element.47), calls=%async_computation.1 | async-start | bytes 4259840 | tf_op jit(solution)/shard_map/all_to_all | solution.py:474
  52.4 0.0 copy-done.2
  52.5 2.1 %collective-permute-start.7 = (bf16[1024,128]{1,0:T(8,128)(2,1)S(1)}, bf16[1024,128]{1,0:T(8,128)(2,1)S(1)}, u32[]{:S(2)}, u32[]{:S(2)}) collective-permute-start(bf16[1024,128]{1,0:T(8,128)(2,1)S(1)} %slice.15), channel_id=1, source_target_pairs={{2,0},{4,2},{6,4},{7,6},{5,7},{3,5},{1,3},{0,1},{10,8},{12,10},{14... | collective-permute-start | bytes 786440 | tf_op jit(solution)/shard_map/ppermute | solution.py:482
  54.5 0.1 collective-permute-start.6
  54.6 8.0 %fine_gradients.8 = (bf16[2560,128]{1,0:T(8,128)(2,1)}, bf16[2560,128]{1,0:T(8,128)(2,1)}, f32[8,128,128]{2,1,0:T(8,128)}) custom-call(s32[11]{0:T(128)} %fusion.1.refs_0_, s32[2,32]{1,0:T(2,128)} %pad_add_fusion.refs_1_, s32[64,128]{1,0:T(8,128)} %bitcast.42, s32[64,128]{1,0:T(8,128)} %bitcast.50, bf16[8192,128]{1,0:T(8,128)(2,1)} %bitcast.28, ...), custom_call_target="tpu_custom_call" | custom-call | tf_op jit(solution)/shard_map/fine_gradients/pallas_call | solution.py:319
  62.6 21.1 %collective-permute-done.7.refs_7_ = bf16[1024,128]{1,0:T(8,128)(2,1)S(1)} collective-permute-done((bf16[1024,128]{1,0:T(8,128)(2,1)S(1)}, bf16[1024,128]{1,0:T(8,128)(2,1)S(1)}, u32[]{:S(2)}, u32[]{:S(2)}) %collective-permute-start.7) | collective-permute-done | bytes 262176 | tf_op jit(solution)/shard_map/ppermute | solution.py:482
  83.7 7.4 %collective-permute-done.6.refs_6_ = bf16[1024,128]{1,0:T(8,128)(2,1)S(1)} collective-permute-done((bf16[1024,128]{1,0:T(8,128)(2,1)S(1)}, bf16[1024,128]{1,0:T(8,128)(2,1)S(1)}, u32[]{:S(2)}, u32[]{:S(2)}) %collective-permute-start.6) | collective-permute-done | bytes 262176 | tf_op jit(solution)/shard_map/ppermute | solution.py:481
  91.2 11.6 %all-to-all-done.1.refs_0_ = bf16[8,1040,128]{2,1,0:T(8,128)(2,1)S(1)} async-done(((bf16[8,1040,128]{2,1,0:T(8,128)(2,1)}), bf16[8,1040,128]{2,1,0:T(8,128)(2,1)S(1)}, u32[]{:S(2)}, u32[]{:S(2)}) %all-to-all-start.1) | async-done | bytes 2129952 | tf_op jit(solution)/shard_map/all_to_all | solution.py:474
  102.8 6.4 %all-to-all-start = ((bf16[8,1040,128]{2,1,0:T(8,128)(2,1)}), bf16[8,1040,128]{2,1,0:T(8,128)(2,1)}, u32[]{:S(2)}, u32[]{:S(2)}) async-start(bf16[8,1040,128]{2,1,0:T(8,128)(2,1)} %get-tuple-element.45), calls=%async_computation | async-start | bytes 4259840 | tf_op jit(solution)/shard_map/all_to_all | solution.py:491
  109.1 8.7 %fine_gradients.9 = (bf16[2560,128]{1,0:T(8,128)(2,1)}, bf16[2560,128]{1,0:T(8,128)(2,1)}, f32[512,128]{1,0:T(8,128)}, f32[512,128]{1,0:T(8,128)}) custom-call(s32[11]{0:T(128)} %fusion.1.refs_0_, s32[2,32]{1,0:T(2,128)} %pad_add_fusion.refs_1_, s32[64,128]{1,0:T(8,128)} %bitcast.43, s32[64,128]{1,0:T(8,128)} %bitcast.51, bf16[8192,128]{1,0:T(8,128)(2,1)} %bitcast.29, ...), custom_call_target="tpu_custom_call" | custom-call | tf_op jit(solution)/shard_map/fine_gradients/pallas_call | solution.py:319
  117.9 0.1 collective-permute-start.8
  118.0 1.7 collective-permute-done.8
  119.7 1.0 add.64
  120.7 22.2 %place_children.2.refs_2_ = f32[2048,128]{1,0:T(8,128)} custom-call(bf16[8,1040,128]{2,1,0:T(8,128)(2,1)} %copy-done, bf16[1024,128]{1,0:T(8,128)(2,1)} %bitcast.36), custom_call_target="tpu_custom_call" | custom-call | tf_op jit(solution)/shard_map/place_children/pallas_call | solution.py:192
  142.9 0.5 collective-permute-start.9
  143.5 4.5 %collective-permute-done.9 = f32[256,128]{1,0:T(8,128)S(1)} collective-permute-done((f32[256,128]{1,0:T(8,128)S(1)}, f32[256,128]{1,0:T(8,128)S(1)}, u32[]{:S(2)}, u32[]{:S(2)}) %collective-permute-start.9) | collective-permute-done | bytes 131104 | tf_op jit(solution)/shard_map/ppermute | solution.py:372
  148.0 3.1 %collective-permute-start.10 = (f32[128,128]{1,0:T(8,128)S(1)}, f32[128,128]{1,0:T(8,128)S(1)}, u32[]{:S(2)}, u32[]{:S(2)}) collective-permute-start(f32[128,128]{1,0:T(8,128)S(1)} %dynamic-slice_bitcast_fusion.1), channel_id=1, source_target_pairs={{0,1},{1,0},{2,3},{3,2},{4,5},{5,4},{6,7},{7,6},{8,9},{9,8},{10,11... | collective-permute-start | bytes 196616 | tf_op jit(solution)/shard_map/ppermute | solution.py:372
  151.2 6.3 %merge_gradients.1 = bf16[8192,128]{1,0:T(8,128)(2,1)} custom-call(s32[11]{0:T(128)} %fusion.1.refs_0_, s32[64,128]{1,0:T(8,128)} %bitcast.44, bf16[2560,128]{1,0:T(8,128)(2,1)} %get-tuple-element.50.refs_2_, bf16[2560,128]{1,0:T(8,128)(2,1)} %get-tuple-element.51.refs_3_, bf16[2560,128]{1,0:T(8,128)(2,1)} %get-tuple-element.52.refs_4_, ...), custom_call_target="tpu_custom_call" | custom-call | tf_op jit(solution)/shard_map/merge_gradients/pallas_call | solution.py:353
  157.4 0.0 collective-permute-done.10
  157.4 2.7 %collective-permute-start.13 = (f32[128,128]{1,0:T(8,128)S(1)}, f32[128,128]{1,0:T(8,128)S(1)}, u32[]{:S(2)}, u32[]{:S(2)}) collective-permute-start(f32[128,128]{1,0:T(8,128)S(1)} %bitcast_add_fusion.1), channel_id=1, source_target_pairs={{0,6},{1,7},{2,4},{3,5},{4,2},{5,3},{6,0},{7,1},{8,14},{9,15},{10,... | collective-permute-start | bytes 196616 | tf_op jit(solution)/shard_map/ppermute | solution.py:372
  160.1 1.5 collective-permute-start.12
  161.7 0.5 collective-permute-start.11
  162.1 1.5 collective-permute-done.13
  163.7 3.3 %collective-permute-done.12 = f32[128,128]{1,0:T(8,128)S(1)} collective-permute-done((f32[128,128]{1,0:T(8,128)S(1)}, f32[128,128]{1,0:T(8,128)S(1)}, u32[]{:S(2)}, u32[]{:S(2)}) %collective-permute-start.12) | collective-permute-done | bytes 65568 | tf_op jit(solution)/shard_map/ppermute | solution.py:372
  167.0 0.0 collective-permute-done.11
  167.0 0.4 collective-permute-start.16
  167.4 0.3 collective-permute-start.15
  167.8 2.8 %collective-permute-start.14 = (f32[128,128]{1,0:T(8,128)S(1)}, f32[128,128]{1,0:T(8,128)S(1)}, u32[]{:S(2)}, u32[]{:S(2)}) collective-permute-start(f32[128,128]{1,0:T(8,128)S(1)} %add_add_fusion), channel_id=1, source_target_pairs={{0,17},{1,16},{2,19},{3,18},{4,21},{5,20},{6,23},{7,22},{8,25},{9,... | collective-permute-start | bytes 196616 | tf_op jit(solution)/shard_map/ppermute | solution.py:403
  170.6 0.0 all-to-all-done.refs_0_
  170.6 9.4 %place_children.3 = bf16[2048,128]{1,0:T(8,128)(2,1)} custom-call(bf16[8,1040,128]{2,1,0:T(8,128)(2,1)} %all-to-all-done.refs_0_, bf16[1024,128]{1,0:T(8,128)(2,1)} %bitcast.37, f32[2048,128]{1,0:T(8,128)} %place_children.2.refs_2_), custom_call_target="tpu_custom_call" | custom-call | tf_op jit(solution)/shard_map/place_children/pallas_call | solution.py:192
  180.1 0.0 collective-permute-done.16
  180.1 0.0 collective-permute-done.15
  180.1 0.0 collective-permute-done.14
  180.2 0.1 collective-permute-start.17
  180.2 1.5 collective-permute-done.17
  181.8 0.8 fusion
  (23 shorter events, 0.2 us)
Async XLA Ops:
  0.6 15.2 %collective-permute-start.1 = (bf16[2048,128]{1,0:T(8,128)(2,1)}, bf16[2048,128]{1,0:T(8,128)(2,1)S(1)}, u32[]{:S(2)}, u32[]{:S(2)}) collective-permute-start(bf16[2048,128]{1,0:T(8,128)(2,1)} %bitcast.58), channel_id=1, source_target_pairs={{2,0},{4,2},{6,4},{7,6},{5,7},{3,5},{1,3},{0,1},{10,8},{12,10},{14... | collective-permute-start | bytes 1572872 | tf_op jit(solution)/shard_map/ppermute | solution.py:482
  3.6 13.6 %collective-permute-start = (bf16[2048,128]{1,0:T(8,128)(2,1)}, bf16[2048,128]{1,0:T(8,128)(2,1)S(1)}, u32[]{:S(2)}, u32[]{:S(2)}) collective-permute-start(bf16[2048,128]{1,0:T(8,128)(2,1)} %bitcast.59), channel_id=1, source_target_pairs={{0,2},{2,4},{4,6},{6,7},{7,5},{5,3},{3,1},{1,0},{8,10},{10,12},{12... | collective-permute-start | bytes 1572872 | tf_op jit(solution)/shard_map/ppermute | solution.py:481
  15.8 3.4 %copy-start.3 = (bf16[2048,128]{1,0:T(8,128)(2,1)}, bf16[2048,128]{1,0:T(8,128)(2,1)S(1)}, u32[]{:S(2)}) copy-start(bf16[2048,128]{1,0:T(8,128)(2,1)S(1)} %collective-permute-done.1.refs_7_) | copy-start | bytes 1572868
  17.2 2.0 %copy-start.4 = (bf16[2048,128]{1,0:T(8,128)(2,1)}, bf16[2048,128]{1,0:T(8,128)(2,1)S(1)}, u32[]{:S(2)}) copy-start(bf16[2048,128]{1,0:T(8,128)(2,1)S(1)} %collective-permute-done.refs_6_) | copy-start | bytes 1572868
  17.2 12.5 %collective-permute-start.2 = (bf16[2048,128]{1,0:T(8,128)(2,1)S(1)}, bf16[2048,128]{1,0:T(8,128)(2,1)S(1)}, u32[]{:S(2)}, u32[]{:S(2)}) collective-permute-start(bf16[2048,128]{1,0:T(8,128)(2,1)S(1)} %collective-permute-done.refs_6_), channel_id=1, source_target_pairs={{0,2},{2,4},{4,6},{6,7},{7,5},{5,3},{3,1},{1,0},{8,10},{10,12},{12... | collective-permute-start | bytes 1572872 | tf_op jit(solution)/shard_map/ppermute | solution.py:481
  17.6 12.5 %collective-permute-start.3 = (bf16[2048,128]{1,0:T(8,128)(2,1)S(1)}, bf16[2048,128]{1,0:T(8,128)(2,1)S(1)}, u32[]{:S(2)}, u32[]{:S(2)}) collective-permute-start(bf16[2048,128]{1,0:T(8,128)(2,1)S(1)} %collective-permute-done.1.refs_7_), channel_id=1, source_target_pairs={{2,0},{4,2},{6,4},{7,6},{5,7},{3,5},{1,3},{0,1},{10,8},{12,10},{14... | collective-permute-start | bytes 1572872 | tf_op jit(solution)/shard_map/ppermute | solution.py:482
  29.7 7.9 %copy-start.5 = (bf16[2048,128]{1,0:T(8,128)(2,1)}, bf16[2048,128]{1,0:T(8,128)(2,1)S(1)}, u32[]{:S(2)}) copy-start(bf16[2048,128]{1,0:T(8,128)(2,1)S(1)} %collective-permute-done.2.refs_6_) | copy-start | bytes 1572868
  30.2 7.5 %copy-start.6 = (bf16[2048,128]{1,0:T(8,128)(2,1)}, bf16[2048,128]{1,0:T(8,128)(2,1)S(1)}, u32[]{:S(2)}) copy-start(bf16[2048,128]{1,0:T(8,128)(2,1)S(1)} %collective-permute-done.3.refs_7_) | copy-start | bytes 1572868
  30.2 16.5 %collective-permute-start.4 = (bf16[2048,128]{1,0:T(8,128)(2,1)S(1)}, bf16[2048,128]{1,0:T(8,128)(2,1)S(1)}, u32[]{:S(2)}, u32[]{:S(2)}) collective-permute-start(bf16[2048,128]{1,0:T(8,128)(2,1)S(1)} %collective-permute-done.2.refs_6_), channel_id=1, source_target_pairs={{0,2},{2,4},{4,6},{6,7},{7,5},{5,3},{3,1},{1,0},{8,10},{10,12},{12... | collective-permute-start | bytes 1572872 | tf_op jit(solution)/shard_map/ppermute | solution.py:481
  33.3 13.4 %collective-permute-start.5 = (bf16[2048,128]{1,0:T(8,128)(2,1)S(1)}, bf16[2048,128]{1,0:T(8,128)(2,1)S(1)}, u32[]{:S(2)}, u32[]{:S(2)}) collective-permute-start(bf16[2048,128]{1,0:T(8,128)(2,1)S(1)} %collective-permute-done.3.refs_7_), channel_id=1, source_target_pairs={{2,0},{4,2},{6,4},{7,6},{5,7},{3,5},{1,3},{0,1},{10,8},{12,10},{14... | collective-permute-start | bytes 1572872 | tf_op jit(solution)/shard_map/ppermute | solution.py:482
  46.7 7.8 %copy-start.1 = (bf16[2048,128]{1,0:T(8,128)(2,1)}, bf16[2048,128]{1,0:T(8,128)(2,1)S(1)}, u32[]{:S(2)}) copy-start(bf16[2048,128]{1,0:T(8,128)(2,1)S(1)} %collective-permute-done.4.refs_6_) | copy-start | bytes 1572868
  46.7 5.7 %copy-start.2 = (bf16[2048,128]{1,0:T(8,128)(2,1)}, bf16[2048,128]{1,0:T(8,128)(2,1)S(1)}, u32[]{:S(2)}) copy-start(bf16[2048,128]{1,0:T(8,128)(2,1)S(1)} %collective-permute-done.5.refs_7_) | copy-start | bytes 1572868
  46.7 56.1 %all-to-all-start.1 = ((bf16[8,1040,128]{2,1,0:T(8,128)(2,1)}), bf16[8,1040,128]{2,1,0:T(8,128)(2,1)S(1)}, u32[]{:S(2)}, u32[]{:S(2)}) async-start(bf16[8,1040,128]{2,1,0:T(8,128)(2,1)} %get-tuple-element.47), calls=%async_computation.1 | async-start | bytes 4259840 | tf_op jit(solution)/shard_map/all_to_all | solution.py:474
  52.5 31.3 %collective-permute-start.7 = (bf16[1024,128]{1,0:T(8,128)(2,1)S(1)}, bf16[1024,128]{1,0:T(8,128)(2,1)S(1)}, u32[]{:S(2)}, u32[]{:S(2)}) collective-permute-start(bf16[1024,128]{1,0:T(8,128)(2,1)S(1)} %slice.15), channel_id=1, source_target_pairs={{2,0},{4,2},{6,4},{7,6},{5,7},{3,5},{1,3},{0,1},{10,8},{12,10},{14... | collective-permute-start | bytes 786440 | tf_op jit(solution)/shard_map/ppermute | solution.py:482
  54.5 36.6 %collective-permute-start.6 = (bf16[1024,128]{1,0:T(8,128)(2,1)S(1)}, bf16[1024,128]{1,0:T(8,128)(2,1)S(1)}, u32[]{:S(2)}, u32[]{:S(2)}) collective-permute-start(bf16[1024,128]{1,0:T(8,128)(2,1)S(1)} %slice.14), channel_id=1, source_target_pairs={{0,2},{2,4},{4,6},{6,7},{7,5},{5,3},{3,1},{1,0},{8,10},{10,12},{12... | collective-permute-start | bytes 786440 | tf_op jit(solution)/shard_map/ppermute | solution.py:481
  83.7 19.1 %copy-start.7 = (bf16[1024,128]{1,0:T(8,128)(2,1)}, bf16[1024,128]{1,0:T(8,128)(2,1)S(1)}, u32[]{:S(2)}) copy-start(bf16[1024,128]{1,0:T(8,128)(2,1)S(1)} %collective-permute-done.7.refs_7_) | copy-start | bytes 786436
  91.2 11.6 %copy-start.8 = (bf16[1024,128]{1,0:T(8,128)(2,1)}, bf16[1024,128]{1,0:T(8,128)(2,1)S(1)}, u32[]{:S(2)}) copy-start(bf16[1024,128]{1,0:T(8,128)(2,1)S(1)} %collective-permute-done.6.refs_6_) | copy-start | bytes 786436
  102.8 15.1 %copy-start = (bf16[8,1040,128]{2,1,0:T(8,128)(2,1)}, bf16[8,1040,128]{2,1,0:T(8,128)(2,1)S(1)}, u32[]{:S(2)}) copy-start(bf16[8,1040,128]{2,1,0:T(8,128)(2,1)S(1)} %all-to-all-done.1.refs_0_) | copy-start | bytes 6389764
  102.8 67.8 %all-to-all-start = ((bf16[8,1040,128]{2,1,0:T(8,128)(2,1)}), bf16[8,1040,128]{2,1,0:T(8,128)(2,1)}, u32[]{:S(2)}, u32[]{:S(2)}) async-start(bf16[8,1040,128]{2,1,0:T(8,128)(2,1)} %get-tuple-element.45), calls=%async_computation | async-start | bytes 4259840 | tf_op jit(solution)/shard_map/all_to_all | solution.py:491
  117.9 1.8 collective-permute-start.8
  142.9 5.0 %collective-permute-start.9 = (f32[256,128]{1,0:T(8,128)S(1)}, f32[256,128]{1,0:T(8,128)S(1)}, u32[]{:S(2)}, u32[]{:S(2)}) collective-permute-start(f32[256,128]{1,0:T(8,128)S(1)} %dynamic-slice_bitcast_fusion), channel_id=1, source_target_pairs={{0,16},{8,24},{16,0},{24,8},{1,17},{9,25},{17,1},{25,9},{2,18},{10... | collective-permute-start | bytes 393224 | tf_op jit(solution)/shard_map/ppermute | solution.py:372
  148.0 9.4 %collective-permute-start.10 = (f32[128,128]{1,0:T(8,128)S(1)}, f32[128,128]{1,0:T(8,128)S(1)}, u32[]{:S(2)}, u32[]{:S(2)}) collective-permute-start(f32[128,128]{1,0:T(8,128)S(1)} %dynamic-slice_bitcast_fusion.1), channel_id=1, source_target_pairs={{0,1},{1,0},{2,3},{3,2},{4,5},{5,4},{6,7},{7,6},{8,9},{9,8},{10,11... | collective-permute-start | bytes 196616 | tf_op jit(solution)/shard_map/ppermute | solution.py:372
  157.4 6.2 %collective-permute-start.13 = (f32[128,128]{1,0:T(8,128)S(1)}, f32[128,128]{1,0:T(8,128)S(1)}, u32[]{:S(2)}, u32[]{:S(2)}) collective-permute-start(f32[128,128]{1,0:T(8,128)S(1)} %bitcast_add_fusion.1), channel_id=1, source_target_pairs={{0,6},{1,7},{2,4},{3,5},{4,2},{5,3},{6,0},{7,1},{8,14},{9,15},{10,... | collective-permute-start | bytes 196616 | tf_op jit(solution)/shard_map/ppermute | solution.py:372
  160.1 6.9 %collective-permute-start.12 = (f32[128,128]{1,0:T(8,128)S(1)}, f32[128,128]{1,0:T(8,128)S(1)}, u32[]{:S(2)}, u32[]{:S(2)}) collective-permute-start(f32[128,128]{1,0:T(8,128)S(1)} %bitcast_add_fusion.1), channel_id=1, source_target_pairs={{0,4},{1,5},{2,6},{3,7},{4,0},{5,1},{6,2},{7,3},{8,12},{9,13},{10,... | collective-permute-start | bytes 196616 | tf_op jit(solution)/shard_map/ppermute | solution.py:372
  161.7 5.4 %collective-permute-start.11 = (f32[128,128]{1,0:T(8,128)S(1)}, f32[128,128]{1,0:T(8,128)S(1)}, u32[]{:S(2)}, u32[]{:S(2)}) collective-permute-start(f32[128,128]{1,0:T(8,128)S(1)} %bitcast_add_fusion.1), channel_id=1, source_target_pairs={{0,2},{1,3},{2,0},{3,1},{4,6},{5,7},{6,4},{7,5},{8,10},{9,11},{10,... | collective-permute-start | bytes 196616 | tf_op jit(solution)/shard_map/ppermute | solution.py:372
  167.0 13.0 %collective-permute-start.16 = (f32[128,128]{1,0:T(8,128)S(1)}, f32[128,128]{1,0:T(8,128)S(1)}, u32[]{:S(2)}, u32[]{:S(2)}) collective-permute-start(f32[128,128]{1,0:T(8,128)S(1)} %add_add_fusion), channel_id=1, source_target_pairs={{0,1},{1,0},{2,3},{3,2},{4,5},{5,4},{6,7},{7,6},{8,9},{9,8},{10,11... | collective-permute-start | bytes 196616 | tf_op jit(solution)/shard_map/ppermute | solution.py:372
  167.4 12.7 %collective-permute-start.15 = (f32[128,128]{1,0:T(8,128)S(1)}, f32[128,128]{1,0:T(8,128)S(1)}, u32[]{:S(2)}, u32[]{:S(2)}) collective-permute-start(f32[128,128]{1,0:T(8,128)S(1)} %add_add_fusion), channel_id=1, source_target_pairs={{0,16},{8,24},{16,0},{24,8},{1,17},{9,25},{17,1},{25,9},{2,18},{10... | collective-permute-start | bytes 196616 | tf_op jit(solution)/shard_map/ppermute | solution.py:372
  167.8 12.3 %collective-permute-start.14 = (f32[128,128]{1,0:T(8,128)S(1)}, f32[128,128]{1,0:T(8,128)S(1)}, u32[]{:S(2)}, u32[]{:S(2)}) collective-permute-start(f32[128,128]{1,0:T(8,128)S(1)} %add_add_fusion), channel_id=1, source_target_pairs={{0,17},{1,16},{2,19},{3,18},{4,21},{5,20},{6,23},{7,22},{8,25},{9,... | collective-permute-start | bytes 196616 | tf_op jit(solution)/shard_map/ppermute | solution.py:403
  180.2 1.6 collective-permute-start.17

commit v4 on v3

--- a/solution.py
+++ b/solution.py
@@ -8,6 +8,7 @@
 LANES = 128
 ALIGN = 16
 TILE = 256
+GROUP = 4
 VMEM_LIMIT = 60 * 1024 * 1024
 
 
@@ -85,15 +86,13 @@
 
 def place_children_kernel(half, first, payload_ref, weight_ref, *rest):
     if first:
-        out_ref, total_ref, rel_ref, code_ref, ends_vmem, ends_ref, sem = rest
+        out_ref, total_ref, rel_ref, code_ref, ends_vmem, ends_ref, list_ref, sem = rest
     else:
-        prior_ref, out_ref, total_ref, rel_ref, code_ref, ends_vmem, ends_ref, sem = rest
+        prior_ref, out_ref, total_ref, rel_ref, code_ref, ends_vmem, ends_ref, list_ref, sem = rest
     par_rows, chan_out = out_ref.shape
     sources = payload_ref.shape[0]
     kinds_total = weight_ref.shape[0] // payload_ref.shape[2]
     lines = half // LANES
-    size = min(2 * TILE, half)
-    parts = size // TILE
     per = TILE // LANES
     window = min((5 if first else 3) * TILE // 2, par_rows)
     meta = payload_ref[:, half : half + ALIGN, :].astype(jnp.float32).astype(jnp.int32)
@@ -121,38 +120,50 @@
     if not first:
         total_ref[:, 0:chan_out] = prior_ref[...]
     copy.wait()
-    chunks = half // size
-
-    def chunk(step, carry):
-        s = step // chunks
-        c = step % chunks
-        line0 = 8 * s + c * (size // LANES)
-        mosts = [
-            jnp.maximum(end_of(1, line0 + per * p), end_of(1, line0 + per * p + per - 1))
-            for p in range(parts)
-        ]
-        starts = [
-            pl.multiple_of(jnp.minimum(end_of(0, line0 + per * p) // 8 * 8, par_rows - window), 8)
-            for p in range(parts)
-        ]
-        slow = mosts[0] >= starts[0] + window
-        live = mosts[0] >= 0
-        for p in range(1, parts):
-            slow = slow | (mosts[p] >= starts[p] + window)
-            live = live | (mosts[p] >= 0)
+    tiles = half // TILE
+
+    def collect(tile, found):
+        line = 8 * (tile // tiles) + per * (tile % tiles)
+        live = jnp.maximum(end_of(1, line), end_of(1, line + per - 1)) >= 0
+
+        @pl.when(live)
+        def _():
+            list_ref[found] = line
+
+        return found + live.astype(jnp.int32)
+
+    found = lax.fori_loop(0, sources * tiles, collect, 0)
+
+    def group(step, carry):
+        held, mosts, starts, spare = [], [], [], []
+        slow = False
+        for p in range(GROUP):
+            index = step * GROUP + p
+            line = list_ref[jnp.minimum(index, found - 1)]
+            most = jnp.maximum(end_of(1, line), end_of(1, line + per - 1))
+            start = pl.multiple_of(jnp.minimum(end_of(0, line) // 8 * 8, par_rows - window), 8)
+            held.append(line)
+            starts.append(start)
+            mosts.append(jnp.where(index < found, most, -1))
+            spare.append(jnp.where(index < found, 0, 1 << 20))
+            slow = slow | (mosts[p] >= start + window)
 
         def work(extra):
-            feats = payload_ref[s, pl.ds(pl.multiple_of(c * size, size), size), :]
-            kinds = [column(code_ref[pl.ds(line0 + i, 1), :]) for i in range(size // LANES)]
-            spread = spread_kinds(jnp.concatenate(kinds, axis=0), feats, kinds_total)
+            feats, kinds = [], []
+            for line in held:
+                row0 = pl.multiple_of(line % 8 * LANES, TILE)
+                feats.append(payload_ref[line // 8, pl.ds(row0, TILE), :])
+                kinds += [column(code_ref[pl.ds(line + i, 1), :]) for i in range(per)]
+            spread = spread_kinds(
+                jnp.concatenate(kinds, axis=0), jnp.concatenate(feats, axis=0), kinds_total
+            )
             product = jnp.dot(spread, weight_ref[...], preferred_element_type=jnp.float32)
             upper = product.astype(jnp.bfloat16)
             lower = (product - upper.astype(jnp.float32)).astype(jnp.bfloat16)
             both = jnp.concatenate([upper, lower], axis=1)
-            for p in range(parts):
-                count = TILE // LANES
-                spots = [rel_ref[pl.ds(line0 + p * count + i, 1), :] for i in range(count)]
-                spot = jnp.concatenate(spots, axis=1)
+            for p in range(GROUP):
+                spots = [rel_ref[pl.ds(held[p] + i, 1), :] for i in range(per)]
+                spot = jnp.concatenate(spots, axis=1) + spare[p]
                 mine = both[p * TILE : (p + 1) * TILE]
 
                 def add(start, width, floor):
@@ -176,11 +187,11 @@
 
                     lax.fori_loop(0, (mosts[p] + TILE - starts[p] - window) // TILE, body, 0)
 
-        pl.when(live & slow)(lambda: work(True))
-        pl.when(live & jnp.logical_not(slow))(lambda: work(False))
+        pl.when(slow)(lambda: work(True))
+        pl.when(jnp.logical_not(slow))(lambda: work(False))
         return carry
 
-    lax.fori_loop(0, sources * chunks, chunk, 0)
+    lax.fori_loop(0, (found + GROUP - 1) // GROUP, group, 0)
     out_ref[...] = (total_ref[:, 0:chan_out] + total_ref[:, chan_out : 2 * chan_out]).astype(out_ref.dtype)
 
 
@@ -200,6 +211,7 @@
             pltpu.VMEM((8 * sources, LANES), jnp.int32),
             pltpu.VMEM((2, -(-8 * sources // LANES), 8, LANES), jnp.int32),
             pltpu.SMEM((2, -(-8 * sources // LANES), 8, LANES), jnp.int32),
+            pltpu.SMEM((4 * sources,), jnp.int32),
             pltpu.SemaphoreType.DMA(()),
         ],
         compiler_params=pltpu.CompilerParams(vmem_limit_bytes=VMEM_LIMIT),

time: 183 us -> 180 us (0.984)
  waiting for transfers between devices: 56.4 us -> 60.3 us
  starting transfers between devices: 34.5 us -> 31.2 us
  Pallas kernels: 82.9 us -> 80 us
    ppermute x4, starting transfers between devices: 3.71 us -> 0.95 us  [per_device(): right = lax.ppermute(right, 'space', ahead)]
    pallas_call x2, Pallas kernels: 31.7 us -> 29.4 us  [place_children(): pl.pallas_call(lambda *refs: place_children_kernel(payload.shape[1] - ALI...]
    ppermute x4, waiting for transfers between devices: 22.7 us -> 24.9 us  [per_device(): left = lax.ppermute(left, 'space', behind)]
  transfers between devices with their start and end apart: 20 -> 20, of which waited for: 12 -> 12; matrix products, arithmetic and copies ran while one was open for 4% -> 4% of each run, Pallas kernels for 45% -> 44%
where the time goes in v4:
time: 180 us
  Pallas kernels  80 us (44%)
  waiting for transfers between devices  60.3 us (34%)
  starting transfers between devices  31.2 us (17%)
  other arithmetic  3.94 us (2%)
  local copies, waits for them, and re-layouts  3.91 us (2%)
    pallas_call x5, Pallas kernels, stage(): pl.pallas_call(lambda *refs: stage_kernel(blocks, len(priors), shares, of...  39.9 us
    pallas_call x2, Pallas kernels, place_children(): pl.pallas_call(lambda *refs: place_children_kernel(payload.shape[1] - ALI...  29.4 us
    ppermute x4, waiting for transfers between devices, per_device(): left = lax.ppermute(left, 'space', behind)  24.9 us
    ppermute x9, waiting for transfers between devices, swap(): return lax.ppermute(value, axis, [(i, i ^ mask) for i in range(size)])  13.9 us
    ppermute x4, waiting for transfers between devices, per_device(): right = lax.ppermute(right, 'space', ahead)  11.1 us
    all_to_all x1, waiting for transfers between devices, exchange(): return lax.all_to_all(after(windows, mark), 'space', 0, 0, tiled=True)  10.5 us
    ppermute x4, starting transfers between devices, per_device(): left = lax.ppermute(left, 'space', behind)  8.39 us
    ppermute x9, starting transfers between devices, swap(): return lax.ppermute(value, axis, [(i, i ^ mask) for i in range(size)])  8.34 us
  transfers between devices with their start and end apart: 20, of which 12 were waited for; matrix products, arithmetic and copies ran while one was open for 4% of the time, Pallas kernels for 44%

profile of v4, /device:TPU:0, one launch (start us, length us, event | category | flops | bytes accessed | tf_op | source)
XLA Modules:
  0.0 180.2 jit_solution(12923712437442325682)
XLA Ops:
  0.6 3.0 %collective-permute-start.1 = (bf16[2048,128]{1,0:T(8,128)(2,1)}, bf16[2048,128]{1,0:T(8,128)(2,1)S(1)}, u32[]{:S(2)}, u32[]{:S(2)}) collective-permute-start(bf16[2048,128]{1,0:T(8,128)(2,1)} %bitcast.58), channel_id=1, source_target_pairs={{2,0},{4,2},{6,4},{7,6},{5,7},{3,5},{1,3},{0,1},{10,8},{12,10},{14... | collective-permute-start | bytes 1572872 | tf_op jit(solution)/shard_map/ppermute | solution.py:494
  3.6 0.1 collective-permute-start
  3.8 0.5 broadcast.17
  4.3 1.5 reduce.3
  5.8 0.1 fusion.2
  5.9 0.1 copy.12
  5.9 0.1 copy.13
  6.0 1.8 copy.11
  7.8 1.3 fusion.1.refs_0_
  9.1 0.5 pad_add_fusion.refs_1_
  9.6 5.5 %fine_gradients.5 = (bf16[2560,128]{1,0:T(8,128)(2,1)}, f32[8,128,128]{2,1,0:T(8,128)}) custom-call(s32[11]{0:T(128)} %fusion.1.refs_0_, s32[2,32]{1,0:T(2,128)} %pad_add_fusion.refs_1_, s32[64,128]{1,0:T(8,128)} %bitcast.38, s32[64,128]{1,0:T(8,128)} %bitcast.46, bf16[8192,128]{1,0:T(8,128)(2,1)} %bitcast.24, bf16[1024,128]{1,0:T(8,128)(2,1)} %bitcast.30, ...), custom_call_target="tpu_custom_call" | custom-call | tf_op jit(solution)/shard_map/fine_gradients/pallas_call | solution.py:331
  15.1 0.8 collective-permute-done.1.refs_7_
  15.8 1.4 collective-permute-done.refs_6_
  17.2 0.4 collective-permute-start.2
  17.6 1.6 collective-permute-start.3
  19.3 0.0 copy-done.3
  19.3 8.9 %fine_gradients.6 = (bf16[2560,128]{1,0:T(8,128)(2,1)}, bf16[2560,128]{1,0:T(8,128)(2,1)}, f32[8,128,128]{2,1,0:T(8,128)}) custom-call(s32[11]{0:T(128)} %fusion.1.refs_0_, s32[2,32]{1,0:T(2,128)} %pad_add_fusion.refs_1_, s32[64,128]{1,0:T(8,128)} %bitcast.39, s32[64,128]{1,0:T(8,128)} %bitcast.47, bf16[8192,128]{1,0:T(8,128)(2,1)} %bitcast.25, ...), custom_call_target="tpu_custom_call" | custom-call | tf_op jit(solution)/shard_map/fine_gradients/pallas_call | solution.py:331
  28.1 1.6 collective-permute-done.2.refs_6_
  29.7 2.1 %collective-permute-done.3.refs_7_ = bf16[2048,128]{1,0:T(8,128)(2,1)S(1)} collective-permute-done((bf16[2048,128]{1,0:T(8,128)(2,1)S(1)}, bf16[2048,128]{1,0:T(8,128)(2,1)S(1)}, u32[]{:S(2)}, u32[]{:S(2)}) %collective-permute-start.3) | collective-permute-done | bytes 524320 | tf_op jit(solution)/shard_map/ppermute | solution.py:494
  31.9 0.3 collective-permute-start.4
  32.2 1.7 collective-permute-start.5
  33.9 4.4 %pack_windows.1 = (bf16[8,1040,128]{2,1,0:T(8,128)(2,1)}, bf16[8,1040,128]{2,1,0:T(8,128)(2,1)}) custom-call(s32[64,128]{1,0:T(8,128)} %bitcast.40, s32[64,128]{1,0:T(8,128)} %bitcast.48, bf16[8192,128]{1,0:T(8,128)(2,1)} %bitcast.26), custom_call_target="tpu_custom_call" | custom-call | tf_op jit(solution)/shard_map/pack_windows/pallas_call | solution.py:62
  38.3 0.0 copy-done.5
  38.3 0.0 copy-done.6
  38.3 9.5 %fine_gradients.7 = (bf16[2560,128]{1,0:T(8,128)(2,1)}, bf16[2560,128]{1,0:T(8,128)(2,1)}, f32[8,128,128]{2,1,0:T(8,128)}) custom-call(s32[11]{0:T(128)} %fusion.1.refs_0_, s32[2,32]{1,0:T(2,128)} %pad_add_fusion.refs_1_, s32[64,128]{1,0:T(8,128)} %bitcast.41, s32[64,128]{1,0:T(8,128)} %bitcast.49, bf16[8192,128]{1,0:T(8,128)(2,1)} %bitcast.27, ...), custom_call_target="tpu_custom_call" | custom-call | tf_op jit(solution)/shard_map/fine_gradients/pallas_call | solution.py:331
  47.8 0.0 collective-permute-done.4.refs_6_
  47.8 0.0 collective-permute-done.5.refs_7_
  47.9 0.0 copy-start.2
  47.9 4.2 %all-to-all-start.1 = ((bf16[8,1040,128]{2,1,0:T(8,128)(2,1)}), bf16[8,1040,128]{2,1,0:T(8,128)(2,1)S(1)}, u32[]{:S(2)}, u32[]{:S(2)}) async-start(bf16[8,1040,128]{2,1,0:T(8,128)(2,1)} %get-tuple-element.47), calls=%async_computation.1 | async-start | bytes 4259840 | tf_op jit(solution)/shard_map/all_to_all | solution.py:486
  52.1 2.1 %collective-permute-start.7 = (bf16[1024,128]{1,0:T(8,128)(2,1)S(1)}, bf16[1024,128]{1,0:T(8,128)(2,1)S(1)}, u32[]{:S(2)}, u32[]{:S(2)}) collective-permute-start(bf16[1024,128]{1,0:T(8,128)(2,1)S(1)} %slice.15), channel_id=1, source_target_pairs={{2,0},{4,2},{6,4},{7,6},{5,7},{3,5},{1,3},{0,1},{10,8},{12,10},{14... | collective-permute-start | bytes 786440 | tf_op jit(solution)/shard_map/ppermute | solution.py:494
  54.2 0.1 collective-permute-start.6
  54.3 7.6 %fine_gradients.8 = (bf16[2560,128]{1,0:T(8,128)(2,1)}, bf16[2560,128]{1,0:T(8,128)(2,1)}, f32[8,128,128]{2,1,0:T(8,128)}) custom-call(s32[11]{0:T(128)} %fusion.1.refs_0_, s32[2,32]{1,0:T(2,128)} %pad_add_fusion.refs_1_, s32[64,128]{1,0:T(8,128)} %bitcast.42, s32[64,128]{1,0:T(8,128)} %bitcast.50, bf16[8192,128]{1,0:T(8,128)(2,1)} %bitcast.28, ...), custom_call_target="tpu_custom_call" | custom-call | tf_op jit(solution)/shard_map/fine_gradients/pallas_call | solution.py:331
  61.9 22.0 %collective-permute-done.7.refs_7_ = bf16[1024,128]{1,0:T(8,128)(2,1)S(1)} collective-permute-done((bf16[1024,128]{1,0:T(8,128)(2,1)S(1)}, bf16[1024,128]{1,0:T(8,128)(2,1)S(1)}, u32[]{:S(2)}, u32[]{:S(2)}) %collective-permute-start.7) | collective-permute-done | bytes 262176 | tf_op jit(solution)/shard_map/ppermute | solution.py:494
  83.9 8.1 %collective-permute-done.6.refs_6_ = bf16[1024,128]{1,0:T(8,128)(2,1)S(1)} collective-permute-done((bf16[1024,128]{1,0:T(8,128)(2,1)S(1)}, bf16[1024,128]{1,0:T(8,128)(2,1)S(1)}, u32[]{:S(2)}, u32[]{:S(2)}) %collective-permute-start.6) | collective-permute-done | bytes 262176 | tf_op jit(solution)/shard_map/ppermute | solution.py:493
  92.0 10.5 %all-to-all-done.1.refs_0_ = bf16[8,1040,128]{2,1,0:T(8,128)(2,1)S(1)} async-done(((bf16[8,1040,128]{2,1,0:T(8,128)(2,1)}), bf16[8,1040,128]{2,1,0:T(8,128)(2,1)S(1)}, u32[]{:S(2)}, u32[]{:S(2)}) %all-to-all-start.1) | async-done | bytes 2129952 | tf_op jit(solution)/shard_map/all_to_all | solution.py:486
  102.5 0.0 copy-done.7
  102.5 7.1 %all-to-all-start = ((bf16[8,1040,128]{2,1,0:T(8,128)(2,1)}), bf16[8,1040,128]{2,1,0:T(8,128)(2,1)}, u32[]{:S(2)}, u32[]{:S(2)}) async-start(bf16[8,1040,128]{2,1,0:T(8,128)(2,1)} %get-tuple-element.45), calls=%async_computation | async-start | bytes 4259840 | tf_op jit(solution)/shard_map/all_to_all | solution.py:503
  109.6 8.5 %fine_gradients.9 = (bf16[2560,128]{1,0:T(8,128)(2,1)}, bf16[2560,128]{1,0:T(8,128)(2,1)}, f32[512,128]{1,0:T(8,128)}, f32[512,128]{1,0:T(8,128)}) custom-call(s32[11]{0:T(128)} %fusion.1.refs_0_, s32[2,32]{1,0:T(2,128)} %pad_add_fusion.refs_1_, s32[64,128]{1,0:T(8,128)} %bitcast.43, s32[64,128]{1,0:T(8,128)} %bitcast.51, bf16[8192,128]{1,0:T(8,128)(2,1)} %bitcast.29, ...), custom_call_target="tpu_custom_call" | custom-call | tf_op jit(solution)/shard_map/fine_gradients/pallas_call | solution.py:331
  118.1 0.1 collective-permute-start.8
  118.2 1.7 collective-permute-done.8
  119.9 1.0 add.64
  120.9 19.8 %place_children.2.refs_2_ = f32[2048,128]{1,0:T(8,128)} custom-call(bf16[8,1040,128]{2,1,0:T(8,128)(2,1)} %copy-done, bf16[1024,128]{1,0:T(8,128)(2,1)} %bitcast.36), custom_call_target="tpu_custom_call" | custom-call | tf_op jit(solution)/shard_map/place_children/pallas_call | solution.py:203
  140.7 0.1 collective-permute-start.9
  140.8 5.9 %collective-permute-done.9 = f32[256,128]{1,0:T(8,128)S(1)} collective-permute-done((f32[256,128]{1,0:T(8,128)S(1)}, f32[256,128]{1,0:T(8,128)S(1)}, u32[]{:S(2)}, u32[]{:S(2)}) %collective-permute-start.9) | collective-permute-done | bytes 131104 | tf_op jit(solution)/shard_map/ppermute | solution.py:384
  146.7 2.3 %collective-permute-start.10 = (f32[128,128]{1,0:T(8,128)S(1)}, f32[128,128]{1,0:T(8,128)S(1)}, u32[]{:S(2)}, u32[]{:S(2)}) collective-permute-start(f32[128,128]{1,0:T(8,128)S(1)} %dynamic-slice_bitcast_fusion.1), channel_id=1, source_target_pairs={{0,1},{1,0},{2,3},{3,2},{4,5},{5,4},{6,7},{7,6},{8,9},{9,8},{10,11... | collective-permute-start | bytes 196616 | tf_op jit(solution)/shard_map/ppermute | solution.py:384
  149.0 6.3 %merge_gradients.1 = bf16[8192,128]{1,0:T(8,128)(2,1)} custom-call(s32[11]{0:T(128)} %fusion.1.refs_0_, s32[64,128]{1,0:T(8,128)} %bitcast.44, bf16[2560,128]{1,0:T(8,128)(2,1)} %get-tuple-element.50.refs_2_, bf16[2560,128]{1,0:T(8,128)(2,1)} %get-tuple-element.51.refs_3_, bf16[2560,128]{1,0:T(8,128)(2,1)} %get-tuple-element.52.refs_4_, ...), custom_call_target="tpu_custom_call" | custom-call | tf_op jit(solution)/shard_map/merge_gradients/pallas_call | solution.py:365
  155.3 0.0 collective-permute-done.10
  155.3 1.7 collective-permute-start.13
  157.0 0.0 collective-permute-start.12
  157.0 2.8 %collective-permute-start.11 = (f32[128,128]{1,0:T(8,128)S(1)}, f32[128,128]{1,0:T(8,128)S(1)}, u32[]{:S(2)}, u32[]{:S(2)}) collective-permute-start(f32[128,128]{1,0:T(8,128)S(1)} %bitcast_add_fusion.1), channel_id=1, source_target_pairs={{0,2},{1,3},{2,0},{3,1},{4,6},{5,7},{6,4},{7,5},{8,10},{9,11},{10,... | collective-permute-start | bytes 196616 | tf_op jit(solution)/shard_map/ppermute | solution.py:384
  159.7 2.4 %collective-permute-done.13 = f32[128,128]{1,0:T(8,128)S(1)} collective-permute-done((f32[128,128]{1,0:T(8,128)S(1)}, f32[128,128]{1,0:T(8,128)S(1)}, u32[]{:S(2)}, u32[]{:S(2)}) %collective-permute-start.13) | collective-permute-done | bytes 65568 | tf_op jit(solution)/shard_map/ppermute | solution.py:384
  162.1 2.4 %collective-permute-done.12 = f32[128,128]{1,0:T(8,128)S(1)} collective-permute-done((f32[128,128]{1,0:T(8,128)S(1)}, f32[128,128]{1,0:T(8,128)S(1)}, u32[]{:S(2)}, u32[]{:S(2)}) %collective-permute-start.12) | collective-permute-done | bytes 65568 | tf_op jit(solution)/shard_map/ppermute | solution.py:384
  164.5 0.0 collective-permute-done.11
  164.5 1.4 collective-permute-start.16
  165.9 0.0 collective-permute-start.15
  165.9 2.2 %collective-permute-start.14 = (f32[128,128]{1,0:T(8,128)S(1)}, f32[128,128]{1,0:T(8,128)S(1)}, u32[]{:S(2)}, u32[]{:S(2)}) collective-permute-start(f32[128,128]{1,0:T(8,128)S(1)} %add_add_fusion), channel_id=1, source_target_pairs={{0,17},{1,16},{2,19},{3,18},{4,21},{5,20},{6,23},{7,22},{8,25},{9,... | collective-permute-start | bytes 196616 | tf_op jit(solution)/shard_map/ppermute | solution.py:415
  168.1 0.0 all-to-all-done.refs_0_
  168.1 9.6 %place_children.3 = bf16[2048,128]{1,0:T(8,128)(2,1)} custom-call(bf16[8,1040,128]{2,1,0:T(8,128)(2,1)} %all-to-all-done.refs_0_, bf16[1024,128]{1,0:T(8,128)(2,1)} %bitcast.37, f32[2048,128]{1,0:T(8,128)} %place_children.2.refs_2_), custom_call_target="tpu_custom_call" | custom-call | tf_op jit(solution)/shard_map/place_children/pallas_call | solution.py:203
  177.7 0.0 collective-permute-done.16
  177.7 0.0 collective-permute-done.15
  177.7 0.0 collective-permute-done.14
  177.8 0.1 collective-permute-start.17
  177.9 1.5 collective-permute-done.17
  179.4 0.8 fusion
  (23 shorter events, 0.2 us)
Async XLA Ops:
  0.6 15.2 %collective-permute-start.1 = (bf16[2048,128]{1,0:T(8,128)(2,1)}, bf16[2048,128]{1,0:T(8,128)(2,1)S(1)}, u32[]{:S(2)}, u32[]{:S(2)}) collective-permute-start(bf16[2048,128]{1,0:T(8,128)(2,1)} %bitcast.58), channel_id=1, source_target_pairs={{2,0},{4,2},{6,4},{7,6},{5,7},{3,5},{1,3},{0,1},{10,8},{12,10},{14... | collective-permute-start | bytes 1572872 | tf_op jit(solution)/shard_map/ppermute | solution.py:494
  3.6 13.6 %collective-permute-start = (bf16[2048,128]{1,0:T(8,128)(2,1)}, bf16[2048,128]{1,0:T(8,128)(2,1)S(1)}, u32[]{:S(2)}, u32[]{:S(2)}) collective-permute-start(bf16[2048,128]{1,0:T(8,128)(2,1)} %bitcast.59), channel_id=1, source_target_pairs={{0,2},{2,4},{4,6},{6,7},{7,5},{5,3},{3,1},{1,0},{8,10},{10,12},{12... | collective-permute-start | bytes 1572872 | tf_op jit(solution)/shard_map/ppermute | solution.py:493
  15.8 3.4 %copy-start.3 = (bf16[2048,128]{1,0:T(8,128)(2,1)}, bf16[2048,128]{1,0:T(8,128)(2,1)S(1)}, u32[]{:S(2)}) copy-start(bf16[2048,128]{1,0:T(8,128)(2,1)S(1)} %collective-permute-done.1.refs_7_) | copy-start | bytes 1572868
  17.2 2.0 %copy-start.4 = (bf16[2048,128]{1,0:T(8,128)(2,1)}, bf16[2048,128]{1,0:T(8,128)(2,1)S(1)}, u32[]{:S(2)}) copy-start(bf16[2048,128]{1,0:T(8,128)(2,1)S(1)} %collective-permute-done.refs_6_) | copy-start | bytes 1572868
  17.2 12.5 %collective-permute-start.2 = (bf16[2048,128]{1,0:T(8,128)(2,1)S(1)}, bf16[2048,128]{1,0:T(8,128)(2,1)S(1)}, u32[]{:S(2)}, u32[]{:S(2)}) collective-permute-start(bf16[2048,128]{1,0:T(8,128)(2,1)S(1)} %collective-permute-done.refs_6_), channel_id=1, source_target_pairs={{0,2},{2,4},{4,6},{6,7},{7,5},{5,3},{3,1},{1,0},{8,10},{10,12},{12... | collective-permute-start | bytes 1572872 | tf_op jit(solution)/shard_map/ppermute | solution.py:493
  17.6 14.2 %collective-permute-start.3 = (bf16[2048,128]{1,0:T(8,128)(2,1)S(1)}, bf16[2048,128]{1,0:T(8,128)(2,1)S(1)}, u32[]{:S(2)}, u32[]{:S(2)}) collective-permute-start(bf16[2048,128]{1,0:T(8,128)(2,1)S(1)} %collective-permute-done.1.refs_7_), channel_id=1, source_target_pairs={{2,0},{4,2},{6,4},{7,6},{5,7},{3,5},{1,3},{0,1},{10,8},{12,10},{14... | collective-permute-start | bytes 1572872 | tf_op jit(solution)/shard_map/ppermute | solution.py:494
  29.7 8.6 %copy-start.5 = (bf16[2048,128]{1,0:T(8,128)(2,1)}, bf16[2048,128]{1,0:T(8,128)(2,1)S(1)}, u32[]{:S(2)}) copy-start(bf16[2048,128]{1,0:T(8,128)(2,1)S(1)} %collective-permute-done.2.refs_6_) | copy-start | bytes 1572868
  31.8 6.4 %copy-start.6 = (bf16[2048,128]{1,0:T(8,128)(2,1)}, bf16[2048,128]{1,0:T(8,128)(2,1)S(1)}, u32[]{:S(2)}) copy-start(bf16[2048,128]{1,0:T(8,128)(2,1)S(1)} %collective-permute-done.3.refs_7_) | copy-start | bytes 1572868
  31.9 16.0 %collective-permute-start.4 = (bf16[2048,128]{1,0:T(8,128)(2,1)S(1)}, bf16[2048,128]{1,0:T(8,128)(2,1)S(1)}, u32[]{:S(2)}, u32[]{:S(2)}) collective-permute-start(bf16[2048,128]{1,0:T(8,128)(2,1)S(1)} %collective-permute-done.2.refs_6_), channel_id=1, source_target_pairs={{0,2},{2,4},{4,6},{6,7},{7,5},{5,3},{3,1},{1,0},{8,10},{10,12},{12... | collective-permute-start | bytes 1572872 | tf_op jit(solution)/shard_map/ppermute | solution.py:493
  32.2 15.6 %collective-permute-start.5 = (bf16[2048,128]{1,0:T(8,128)(2,1)S(1)}, bf16[2048,128]{1,0:T(8,128)(2,1)S(1)}, u32[]{:S(2)}, u32[]{:S(2)}) collective-permute-start(bf16[2048,128]{1,0:T(8,128)(2,1)S(1)} %collective-permute-done.3.refs_7_), channel_id=1, source_target_pairs={{2,0},{4,2},{6,4},{7,6},{5,7},{3,5},{1,3},{0,1},{10,8},{12,10},{14... | collective-permute-start | bytes 1572872 | tf_op jit(solution)/shard_map/ppermute | solution.py:494
  47.8 6.4 %copy-start.1 = (bf16[2048,128]{1,0:T(8,128)(2,1)}, bf16[2048,128]{1,0:T(8,128)(2,1)S(1)}, u32[]{:S(2)}) copy-start(bf16[2048,128]{1,0:T(8,128)(2,1)S(1)} %collective-permute-done.4.refs_6_) | copy-start | bytes 1572868
  47.9 4.3 %copy-start.2 = (bf16[2048,128]{1,0:T(8,128)(2,1)}, bf16[2048,128]{1,0:T(8,128)(2,1)S(1)}, u32[]{:S(2)}) copy-start(bf16[2048,128]{1,0:T(8,128)(2,1)S(1)} %collective-permute-done.5.refs_7_) | copy-start | bytes 1572868
  47.9 54.6 %all-to-all-start.1 = ((bf16[8,1040,128]{2,1,0:T(8,128)(2,1)}), bf16[8,1040,128]{2,1,0:T(8,128)(2,1)S(1)}, u32[]{:S(2)}, u32[]{:S(2)}) async-start(bf16[8,1040,128]{2,1,0:T(8,128)(2,1)} %get-tuple-element.47), calls=%async_computation.1 | async-start | bytes 4259840 | tf_op jit(solution)/shard_map/all_to_all | solution.py:486
  52.1 31.7 %collective-permute-start.7 = (bf16[1024,128]{1,0:T(8,128)(2,1)S(1)}, bf16[1024,128]{1,0:T(8,128)(2,1)S(1)}, u32[]{:S(2)}, u32[]{:S(2)}) collective-permute-start(bf16[1024,128]{1,0:T(8,128)(2,1)S(1)} %slice.15), channel_id=1, source_target_pairs={{2,0},{4,2},{6,4},{7,6},{5,7},{3,5},{1,3},{0,1},{10,8},{12,10},{14... | collective-permute-start | bytes 786440 | tf_op jit(solution)/shard_map/ppermute | solution.py:494
  54.2 37.7 %collective-permute-start.6 = (bf16[1024,128]{1,0:T(8,128)(2,1)S(1)}, bf16[1024,128]{1,0:T(8,128)(2,1)S(1)}, u32[]{:S(2)}, u32[]{:S(2)}) collective-permute-start(bf16[1024,128]{1,0:T(8,128)(2,1)S(1)} %slice.14), channel_id=1, source_target_pairs={{0,2},{2,4},{4,6},{6,7},{7,5},{5,3},{3,1},{1,0},{8,10},{10,12},{12... | collective-permute-start | bytes 786440 | tf_op jit(solution)/shard_map/ppermute | solution.py:493
  83.9 18.6 %copy-start.7 = (bf16[1024,128]{1,0:T(8,128)(2,1)}, bf16[1024,128]{1,0:T(8,128)(2,1)S(1)}, u32[]{:S(2)}) copy-start(bf16[1024,128]{1,0:T(8,128)(2,1)S(1)} %collective-permute-done.7.refs_7_) | copy-start | bytes 786436
  92.0 10.5 %copy-start.8 = (bf16[1024,128]{1,0:T(8,128)(2,1)}, bf16[1024,128]{1,0:T(8,128)(2,1)S(1)}, u32[]{:S(2)}) copy-start(bf16[1024,128]{1,0:T(8,128)(2,1)S(1)} %collective-permute-done.6.refs_6_) | copy-start | bytes 786436
  102.5 15.6 %copy-start = (bf16[8,1040,128]{2,1,0:T(8,128)(2,1)}, bf16[8,1040,128]{2,1,0:T(8,128)(2,1)S(1)}, u32[]{:S(2)}) copy-start(bf16[8,1040,128]{2,1,0:T(8,128)(2,1)S(1)} %all-to-all-done.1.refs_0_) | copy-start | bytes 6389764
  102.5 65.6 %all-to-all-start = ((bf16[8,1040,128]{2,1,0:T(8,128)(2,1)}), bf16[8,1040,128]{2,1,0:T(8,128)(2,1)}, u32[]{:S(2)}, u32[]{:S(2)}) async-start(bf16[8,1040,128]{2,1,0:T(8,128)(2,1)} %get-tuple-element.45), calls=%async_computation | async-start | bytes 4259840 | tf_op jit(solution)/shard_map/all_to_all | solution.py:503
  118.1 1.8 %collective-permute-start.8 = (f32[512,128]{1,0:T(8,128)}, f32[512,128]{1,0:T(8,128)S(1)}, u32[]{:S(2)}, u32[]{:S(2)}) collective-permute-start(f32[512,128]{1,0:T(8,128)} %get-tuple-element.59), channel_id=1, source_target_pairs={{0,8},{8,0},{16,24},{24,16},{1,9},{9,1},{17,25},{25,17},{2,10},{10... | collective-permute-start | bytes 786440 | tf_op jit(solution)/shard_map/ppermute | solution.py:384
  140.7 6.0 %collective-permute-start.9 = (f32[256,128]{1,0:T(8,128)S(1)}, f32[256,128]{1,0:T(8,128)S(1)}, u32[]{:S(2)}, u32[]{:S(2)}) collective-permute-start(f32[256,128]{1,0:T(8,128)S(1)} %dynamic-slice_bitcast_fusion), channel_id=1, source_target_pairs={{0,16},{8,24},{16,0},{24,8},{1,17},{9,25},{17,1},{25,9},{2,18},{10... | collective-permute-start | bytes 393224 | tf_op jit(solution)/shard_map/ppermute | solution.py:384
  146.7 8.5 %collective-permute-start.10 = (f32[128,128]{1,0:T(8,128)S(1)}, f32[128,128]{1,0:T(8,128)S(1)}, u32[]{:S(2)}, u32[]{:S(2)}) collective-permute-start(f32[128,128]{1,0:T(8,128)S(1)} %dynamic-slice_bitcast_fusion.1), channel_id=1, source_target_pairs={{0,1},{1,0},{2,3},{3,2},{4,5},{5,4},{6,7},{7,6},{8,9},{9,8},{10,11... | collective-permute-start | bytes 196616 | tf_op jit(solution)/shard_map/ppermute | solution.py:384
  155.3 6.8 %collective-permute-start.13 = (f32[128,128]{1,0:T(8,128)S(1)}, f32[128,128]{1,0:T(8,128)S(1)}, u32[]{:S(2)}, u32[]{:S(2)}) collective-permute-start(f32[128,128]{1,0:T(8,128)S(1)} %bitcast_add_fusion.1), channel_id=1, source_target_pairs={{0,6},{1,7},{2,4},{3,5},{4,2},{5,3},{6,0},{7,1},{8,14},{9,15},{10,... | collective-permute-start | bytes 196616 | tf_op jit(solution)/shard_map/ppermute | solution.py:384
  157.0 7.5 %collective-permute-start.12 = (f32[128,128]{1,0:T(8,128)S(1)}, f32[128,128]{1,0:T(8,128)S(1)}, u32[]{:S(2)}, u32[]{:S(2)}) collective-permute-start(f32[128,128]{1,0:T(8,128)S(1)} %bitcast_add_fusion.1), channel_id=1, source_target_pairs={{0,4},{1,5},{2,6},{3,7},{4,0},{5,1},{6,2},{7,3},{8,12},{9,13},{10,... | collective-permute-start | bytes 196616 | tf_op jit(solution)/shard_map/ppermute | solution.py:384
  157.0 7.5 %collective-permute-start.11 = (f32[128,128]{1,0:T(8,128)S(1)}, f32[128,128]{1,0:T(8,128)S(1)}, u32[]{:S(2)}, u32[]{:S(2)}) collective-permute-start(f32[128,128]{1,0:T(8,128)S(1)} %bitcast_add_fusion.1), channel_id=1, source_target_pairs={{0,2},{1,3},{2,0},{3,1},{4,6},{5,7},{6,4},{7,5},{8,10},{9,11},{10,... | collective-permute-start | bytes 196616 | tf_op jit(solution)/shard_map/ppermute | solution.py:384
  164.5 13.1 %collective-permute-start.16 = (f32[128,128]{1,0:T(8,128)S(1)}, f32[128,128]{1,0:T(8,128)S(1)}, u32[]{:S(2)}, u32[]{:S(2)}) collective-permute-start(f32[128,128]{1,0:T(8,128)S(1)} %add_add_fusion), channel_id=1, source_target_pairs={{0,1},{1,0},{2,3},{3,2},{4,5},{5,4},{6,7},{7,6},{8,9},{9,8},{10,11... | collective-permute-start | bytes 196616 | tf_op jit(solution)/shard_map/ppermute | solution.py:384
  165.9 11.7 %collective-permute-start.15 = (f32[128,128]{1,0:T(8,128)S(1)}, f32[128,128]{1,0:T(8,128)S(1)}, u32[]{:S(2)}, u32[]{:S(2)}) collective-permute-start(f32[128,128]{1,0:T(8,128)S(1)} %add_add_fusion), channel_id=1, source_target_pairs={{0,16},{8,24},{16,0},{24,8},{1,17},{9,25},{17,1},{25,9},{2,18},{10... | collective-permute-start | bytes 196616 | tf_op jit(solution)/shard_map/ppermute | solution.py:384
  165.9 11.7 %collective-permute-start.14 = (f32[128,128]{1,0:T(8,128)S(1)}, f32[128,128]{1,0:T(8,128)S(1)}, u32[]{:S(2)}, u32[]{:S(2)}) collective-permute-start(f32[128,128]{1,0:T(8,128)S(1)} %add_add_fusion), channel_id=1, source_target_pairs={{0,17},{1,16},{2,19},{3,18},{4,21},{5,20},{6,23},{7,22},{8,25},{9,... | collective-permute-start | bytes 196616 | tf_op jit(solution)/shard_map/ppermute | solution.py:415
  177.8 1.6 collective-permute-start.17

commit v5 on v4

--- a/solution.py
+++ b/solution.py
@@ -8,7 +8,6 @@
 LANES = 128
 ALIGN = 16
 TILE = 256
-GROUP = 4
 VMEM_LIMIT = 60 * 1024 * 1024
 
 
@@ -116,11 +115,12 @@
 
     copy = pltpu.make_async_copy(ends_vmem, ends_ref, sem)
     copy.start()
-    total_ref[...] = jnp.zeros(total_ref.shape, jnp.float32)
-    if not first:
-        total_ref[:, 0:chan_out] = prior_ref[...]
+    blank = jnp.zeros((par_rows, chan_out), jnp.float32)
+    total_ref[:, 0:chan_out] = blank if first else prior_ref[...]
+    total_ref[:, chan_out : 2 * chan_out] = blank
     copy.wait()
     tiles = half // TILE
+    together = 4 if first else 6
 
     def collect(tile, found):
         line = 8 * (tile // tiles) + per * (tile % tiles)
@@ -137,8 +137,8 @@
     def group(step, carry):
         held, mosts, starts, spare = [], [], [], []
         slow = False
-        for p in range(GROUP):
-            index = step * GROUP + p
+        for p in range(together):
+            index = step * together + p
             line = list_ref[jnp.minimum(index, found - 1)]
             most = jnp.maximum(end_of(1, line), end_of(1, line + per - 1))
             start = pl.multiple_of(jnp.minimum(end_of(0, line) // 8 * 8, par_rows - window), 8)
@@ -161,7 +161,7 @@
             upper = product.astype(jnp.bfloat16)
             lower = (product - upper.astype(jnp.float32)).astype(jnp.bfloat16)
             both = jnp.concatenate([upper, lower], axis=1)
-            for p in range(GROUP):
+            for p in range(together):
                 spots = [rel_ref[pl.ds(held[p] + i, 1), :] for i in range(per)]
                 spot = jnp.concatenate(spots, axis=1) + spare[p]
                 mine = both[p * TILE : (p + 1) * TILE]
@@ -191,7 +191,7 @@
         pl.when(jnp.logical_not(slow))(lambda: work(False))
         return carry
 
-    lax.fori_loop(0, (found + GROUP - 1) // GROUP, group, 0)
+    lax.fori_loop(0, (found + together - 1) // together, group, 0)
     out_ref[...] = (total_ref[:, 0:chan_out] + total_ref[:, chan_out : 2 * chan_out]).astype(out_ref.dtype)
 
 

time: 180 us -> 179 us (level)
  waiting for transfers between devices: 60.3 us -> 53.2 us
  starting transfers between devices: 31.2 us -> 36.4 us
    ppermute x9, starting transfers between devices: 8.34 us -> 14.8 us  [swap(): return lax.ppermute(value, axis, [(i, i ^ mask) for i in range(size)])]
    ppermute x4, waiting for transfers between devices: 24.9 us -> 21.2 us  [per_device(): left = lax.ppermute(left, 'space', behind)]
    ppermute x9, waiting for transfers between devices: 13.9 us -> 11.6 us  [swap(): return lax.ppermute(value, axis, [(i, i ^ mask) for i in range(size)])]
    ppermute x4, waiting for transfers between devices: 11.1 us -> 8.89 us  [per_device(): right = lax.ppermute(right, 'space', ahead)]
    ppermute x1, starting transfers between devices: 2.16 us -> 0.13 us  [sum_terms(): lax.ppermute(total, ('dp', 'space'), pairs)]
  transfers between devices with their start and end apart: 20 -> 20, of which waited for: 12 -> 11; matrix products, arithmetic and copies ran while one was open for 4% -> 4% of each run, Pallas kernels for 44% -> 45%
where the time goes in v5:
time: 179 us; the launch traced here: 178 us
  Pallas kernels  80.2 us (45%)
  waiting for transfers between devices  53.2 us (30%)
  starting transfers between devices  36.4 us (20%)
  other arithmetic  3.94 us (2%)
  local copies, waits for them, and re-layouts  3.91 us (2%)
    pallas_call x5, Pallas kernels, stage(): pl.pallas_call(lambda *refs: stage_kernel(blocks, len(priors), shares, of...  40.9 us
    pallas_call x2, Pallas kernels, place_children(): pl.pallas_call(lambda *refs: place_children_kernel(payload.shape[1] - ALI...  28.6 us
    ppermute x4, waiting for transfers between devices, per_device(): left = lax.ppermute(left, 'space', behind)  21.2 us
    ppermute x9, starting transfers between devices, swap(): return lax.ppermute(value, axis, [(i, i ^ mask) for i in range(size)])  14.8 us
    ppermute x9, waiting for transfers between devices, swap(): return lax.ppermute(value, axis, [(i, i ^ mask) for i in range(size)])  11.6 us
    all_to_all x1, waiting for transfers between devices, exchange(): return lax.all_to_all(after(windows, mark), 'space', 0, 0, tiled=True)  11.5 us
    ppermute x4, waiting for transfers between devices, per_device(): right = lax.ppermute(right, 'space', ahead)  8.89 us
    ppermute x4, starting transfers between devices, per_device(): left = lax.ppermute(left, 'space', behind)  7.84 us
  transfers between devices with their start and end apart: 20, of which 11 were waited for; matrix products, arithmetic and copies ran while one was open for 4% of the time, Pallas kernels for 45%

profile of v5, /device:TPU:0, one launch (start us, length us, event | category | flops | bytes accessed | tf_op | source)
XLA Modules:
  0.0 178.4 jit_solution(14844482031826702209)
XLA Ops:
  0.6 3.0 %collective-permute-start.1 = (bf16[2048,128]{1,0:T(8,128)(2,1)}, bf16[2048,128]{1,0:T(8,128)(2,1)S(1)}, u32[]{:S(2)}, u32[]{:S(2)}) collective-permute-start(bf16[2048,128]{1,0:T(8,128)(2,1)} %bitcast.58), channel_id=1, source_target_pairs={{2,0},{4,2},{6,4},{7,6},{5,7},{3,5},{1,3},{0,1},{10,8},{12,10},{14... | collective-permute-start | bytes 1572872 | tf_op jit(solution)/shard_map/ppermute | solution.py:494
  3.6 0.1 collective-permute-start
  3.8 0.5 broadcast.17
  4.3 1.5 reduce.3
  5.8 0.1 fusion.2
  5.9 0.1 copy.12
  5.9 0.1 copy.13
  6.0 1.8 %copy.11 = bf16[8,128,128]{2,1,0:T(8,128)(2,1)} copy(bf16[8,128,128]{1,2,0:T(8,128)(2,1)} %bitcast.35) | data formatting | bytes 524288 | tf_op jit(solution)/shard_map/transpose | solution.py:457
  7.8 1.3 fusion.1.refs_0_
  9.1 0.5 pad_add_fusion.refs_1_
  9.6 4.7 %fine_gradients.5 = (bf16[2560,128]{1,0:T(8,128)(2,1)}, f32[8,128,128]{2,1,0:T(8,128)}) custom-call(s32[11]{0:T(128)} %fusion.1.refs_0_, s32[2,32]{1,0:T(2,128)} %pad_add_fusion.refs_1_, s32[64,128]{1,0:T(8,128)} %bitcast.38, s32[64,128]{1,0:T(8,128)} %bitcast.46, bf16[8192,128]{1,0:T(8,128)(2,1)} %bitcast.24, bf16[1024,128]{1,0:T(8,128)(2,1)} %bitcast.30, ...), custom_call_target="tpu_custom_call" | custom-call | tf_op jit(solution)/shard_map/fine_gradients/pallas_call | solution.py:331
  14.3 1.5 collective-permute-done.1.refs_7_
  15.8 1.4 collective-permute-done.refs_6_
  17.2 0.4 collective-permute-start.2
  17.6 1.6 collective-permute-start.3
  19.3 0.0 copy-done.3
  19.3 0.0 copy-done.4
  19.3 10.5 %fine_gradients.6 = (bf16[2560,128]{1,0:T(8,128)(2,1)}, bf16[2560,128]{1,0:T(8,128)(2,1)}, f32[8,128,128]{2,1,0:T(8,128)}) custom-call(s32[11]{0:T(128)} %fusion.1.refs_0_, s32[2,32]{1,0:T(2,128)} %pad_add_fusion.refs_1_, s32[64,128]{1,0:T(8,128)} %bitcast.39, s32[64,128]{1,0:T(8,128)} %bitcast.47, bf16[8192,128]{1,0:T(8,128)(2,1)} %bitcast.25, ...), custom_call_target="tpu_custom_call" | custom-call | tf_op jit(solution)/shard_map/fine_gradients/pallas_call | solution.py:331
  29.8 0.0 collective-permute-done.2.refs_6_
  29.8 1.0 collective-permute-done.3.refs_7_
  30.8 0.9 collective-permute-start.4
  31.7 1.1 collective-permute-start.5
  32.9 4.4 %pack_windows.1 = (bf16[8,1040,128]{2,1,0:T(8,128)(2,1)}, bf16[8,1040,128]{2,1,0:T(8,128)(2,1)}) custom-call(s32[64,128]{1,0:T(8,128)} %bitcast.40, s32[64,128]{1,0:T(8,128)} %bitcast.48, bf16[8192,128]{1,0:T(8,128)(2,1)} %bitcast.26), custom_call_target="tpu_custom_call" | custom-call | tf_op jit(solution)/shard_map/pack_windows/pallas_call | solution.py:61
  37.3 0.0 copy-done.5
  37.3 8.5 %fine_gradients.7 = (bf16[2560,128]{1,0:T(8,128)(2,1)}, bf16[2560,128]{1,0:T(8,128)(2,1)}, f32[8,128,128]{2,1,0:T(8,128)}) custom-call(s32[11]{0:T(128)} %fusion.1.refs_0_, s32[2,32]{1,0:T(2,128)} %pad_add_fusion.refs_1_, s32[64,128]{1,0:T(8,128)} %bitcast.41, s32[64,128]{1,0:T(8,128)} %bitcast.49, bf16[8192,128]{1,0:T(8,128)(2,1)} %bitcast.27, ...), custom_call_target="tpu_custom_call" | custom-call | tf_op jit(solution)/shard_map/fine_gradients/pallas_call | solution.py:331
  45.7 0.0 collective-permute-done.4.refs_6_
  45.7 0.0 collective-permute-done.5.refs_7_
  45.8 0.0 copy-start.2
  45.8 5.5 %all-to-all-start.1 = ((bf16[8,1040,128]{2,1,0:T(8,128)(2,1)}), bf16[8,1040,128]{2,1,0:T(8,128)(2,1)S(1)}, u32[]{:S(2)}, u32[]{:S(2)}) async-start(bf16[8,1040,128]{2,1,0:T(8,128)(2,1)} %get-tuple-element.47), calls=%async_computation.1 | async-start | bytes 4259840 | tf_op jit(solution)/shard_map/all_to_all | solution.py:486
  51.3 2.1 %collective-permute-start.7 = (bf16[1024,128]{1,0:T(8,128)(2,1)S(1)}, bf16[1024,128]{1,0:T(8,128)(2,1)S(1)}, u32[]{:S(2)}, u32[]{:S(2)}) collective-permute-start(bf16[1024,128]{1,0:T(8,128)(2,1)S(1)} %slice.15), channel_id=1, source_target_pairs={{2,0},{4,2},{6,4},{7,6},{5,7},{3,5},{1,3},{0,1},{10,8},{12,10},{14... | collective-permute-start | bytes 786440 | tf_op jit(solution)/shard_map/ppermute | solution.py:494
  53.4 0.1 collective-permute-start.6
  53.5 10.6 %fine_gradients.8 = (bf16[2560,128]{1,0:T(8,128)(2,1)}, bf16[2560,128]{1,0:T(8,128)(2,1)}, f32[8,128,128]{2,1,0:T(8,128)}) custom-call(s32[11]{0:T(128)} %fusion.1.refs_0_, s32[2,32]{1,0:T(2,128)} %pad_add_fusion.refs_1_, s32[64,128]{1,0:T(8,128)} %bitcast.42, s32[64,128]{1,0:T(8,128)} %bitcast.50, bf16[8192,128]{1,0:T(8,128)(2,1)} %bitcast.28, ...), custom_call_target="tpu_custom_call" | custom-call | tf_op jit(solution)/shard_map/fine_gradients/pallas_call | solution.py:331
  64.1 18.6 %collective-permute-done.7.refs_7_ = bf16[1024,128]{1,0:T(8,128)(2,1)S(1)} collective-permute-done((bf16[1024,128]{1,0:T(8,128)(2,1)S(1)}, bf16[1024,128]{1,0:T(8,128)(2,1)S(1)}, u32[]{:S(2)}, u32[]{:S(2)}) %collective-permute-start.7) | collective-permute-done | bytes 262176 | tf_op jit(solution)/shard_map/ppermute | solution.py:494
  82.7 7.5 %collective-permute-done.6.refs_6_ = bf16[1024,128]{1,0:T(8,128)(2,1)S(1)} collective-permute-done((bf16[1024,128]{1,0:T(8,128)(2,1)S(1)}, bf16[1024,128]{1,0:T(8,128)(2,1)S(1)}, u32[]{:S(2)}, u32[]{:S(2)}) %collective-permute-start.6) | collective-permute-done | bytes 262176 | tf_op jit(solution)/shard_map/ppermute | solution.py:493
  90.2 11.5 %all-to-all-done.1.refs_0_ = bf16[8,1040,128]{2,1,0:T(8,128)(2,1)S(1)} async-done(((bf16[8,1040,128]{2,1,0:T(8,128)(2,1)}), bf16[8,1040,128]{2,1,0:T(8,128)(2,1)S(1)}, u32[]{:S(2)}, u32[]{:S(2)}) %all-to-all-start.1) | async-done | bytes 2129952 | tf_op jit(solution)/shard_map/all_to_all | solution.py:486
  101.7 6.5 %all-to-all-start = ((bf16[8,1040,128]{2,1,0:T(8,128)(2,1)}), bf16[8,1040,128]{2,1,0:T(8,128)(2,1)}, u32[]{:S(2)}, u32[]{:S(2)}) async-start(bf16[8,1040,128]{2,1,0:T(8,128)(2,1)} %get-tuple-element.45), calls=%async_computation | async-start | bytes 4259840 | tf_op jit(solution)/shard_map/all_to_all | solution.py:503
  108.2 6.7 %fine_gradients.9 = (bf16[2560,128]{1,0:T(8,128)(2,1)}, bf16[2560,128]{1,0:T(8,128)(2,1)}, f32[512,128]{1,0:T(8,128)}, f32[512,128]{1,0:T(8,128)}) custom-call(s32[11]{0:T(128)} %fusion.1.refs_0_, s32[2,32]{1,0:T(2,128)} %pad_add_fusion.refs_1_, s32[64,128]{1,0:T(8,128)} %bitcast.43, s32[64,128]{1,0:T(8,128)} %bitcast.51, bf16[8192,128]{1,0:T(8,128)(2,1)} %bitcast.29, ...), custom_call_target="tpu_custom_call" | custom-call | tf_op jit(solution)/shard_map/fine_gradients/pallas_call | solution.py:331
  114.9 0.0 copy-done
  114.9 0.7 collective-permute-start.8
  115.6 1.4 collective-permute-done.8
  117.0 1.0 add.64
  117.9 19.8 %place_children.2.refs_2_ = f32[2048,128]{1,0:T(8,128)} custom-call(bf16[8,1040,128]{2,1,0:T(8,128)(2,1)} %copy-done, bf16[1024,128]{1,0:T(8,128)(2,1)} %bitcast.36), custom_call_target="tpu_custom_call" | custom-call | tf_op jit(solution)/shard_map/place_children/pallas_call | solution.py:203
  137.8 3.3 %collective-permute-start.9 = (f32[256,128]{1,0:T(8,128)S(1)}, f32[256,128]{1,0:T(8,128)S(1)}, u32[]{:S(2)}, u32[]{:S(2)}) collective-permute-start(f32[256,128]{1,0:T(8,128)S(1)} %dynamic-slice_bitcast_fusion), channel_id=1, source_target_pairs={{0,16},{8,24},{16,0},{24,8},{1,17},{9,25},{17,1},{25,9},{2,18},{10... | collective-permute-start | bytes 393224 | tf_op jit(solution)/shard_map/ppermute | solution.py:384
  141.1 3.4 %collective-permute-done.9 = f32[256,128]{1,0:T(8,128)S(1)} collective-permute-done((f32[256,128]{1,0:T(8,128)S(1)}, f32[256,128]{1,0:T(8,128)S(1)}, u32[]{:S(2)}, u32[]{:S(2)}) %collective-permute-start.9) | collective-permute-done | bytes 131104 | tf_op jit(solution)/shard_map/ppermute | solution.py:384
  144.5 2.3 %collective-permute-start.10 = (f32[128,128]{1,0:T(8,128)S(1)}, f32[128,128]{1,0:T(8,128)S(1)}, u32[]{:S(2)}, u32[]{:S(2)}) collective-permute-start(f32[128,128]{1,0:T(8,128)S(1)} %dynamic-slice_bitcast_fusion.1), channel_id=1, source_target_pairs={{0,1},{1,0},{2,3},{3,2},{4,5},{5,4},{6,7},{7,6},{8,9},{9,8},{10,11... | collective-permute-start | bytes 196616 | tf_op jit(solution)/shard_map/ppermute | solution.py:384
  146.8 6.3 %merge_gradients.1 = bf16[8192,128]{1,0:T(8,128)(2,1)} custom-call(s32[11]{0:T(128)} %fusion.1.refs_0_, s32[64,128]{1,0:T(8,128)} %bitcast.44, bf16[2560,128]{1,0:T(8,128)(2,1)} %get-tuple-element.50.refs_2_, bf16[2560,128]{1,0:T(8,128)(2,1)} %get-tuple-element.51.refs_3_, bf16[2560,128]{1,0:T(8,128)(2,1)} %get-tuple-element.52.refs_4_, ...), custom_call_target="tpu_custom_call" | custom-call | tf_op jit(solution)/shard_map/merge_gradients/pallas_call | solution.py:365
  153.1 0.0 collective-permute-done.10
  153.1 4.3 %collective-permute-start.13 = (f32[128,128]{1,0:T(8,128)S(1)}, f32[128,128]{1,0:T(8,128)S(1)}, u32[]{:S(2)}, u32[]{:S(2)}) collective-permute-start(f32[128,128]{1,0:T(8,128)S(1)} %bitcast_add_fusion.1), channel_id=1, source_target_pairs={{0,6},{1,7},{2,4},{3,5},{4,2},{5,3},{6,0},{7,1},{8,14},{9,15},{10,... | collective-permute-start | bytes 196616 | tf_op jit(solution)/shard_map/ppermute | solution.py:384
  157.4 0.3 collective-permute-start.12
  157.8 0.4 collective-permute-start.11
  158.2 1.8 %collective-permute-done.13 = f32[128,128]{1,0:T(8,128)S(1)} collective-permute-done((f32[128,128]{1,0:T(8,128)S(1)}, f32[128,128]{1,0:T(8,128)S(1)}, u32[]{:S(2)}, u32[]{:S(2)}) %collective-permute-start.13) | collective-permute-done | bytes 65568 | tf_op jit(solution)/shard_map/ppermute | solution.py:384
  159.9 3.6 %collective-permute-done.12 = f32[128,128]{1,0:T(8,128)S(1)} collective-permute-done((f32[128,128]{1,0:T(8,128)S(1)}, f32[128,128]{1,0:T(8,128)S(1)}, u32[]{:S(2)}, u32[]{:S(2)}) %collective-permute-start.12) | collective-permute-done | bytes 65568 | tf_op jit(solution)/shard_map/ppermute | solution.py:384
  163.5 0.0 collective-permute-done.11
  163.6 1.3 collective-permute-start.16
  164.8 2.2 %collective-permute-start.15 = (f32[128,128]{1,0:T(8,128)S(1)}, f32[128,128]{1,0:T(8,128)S(1)}, u32[]{:S(2)}, u32[]{:S(2)}) collective-permute-start(f32[128,128]{1,0:T(8,128)S(1)} %add_add_fusion), channel_id=1, source_target_pairs={{0,16},{8,24},{16,0},{24,8},{1,17},{9,25},{17,1},{25,9},{2,18},{10... | collective-permute-start | bytes 196616 | tf_op jit(solution)/shard_map/ppermute | solution.py:384
  167.0 0.1 collective-permute-start.14
  167.1 0.0 all-to-all-done.refs_0_
  167.1 8.8 %place_children.3 = bf16[2048,128]{1,0:T(8,128)(2,1)} custom-call(bf16[8,1040,128]{2,1,0:T(8,128)(2,1)} %all-to-all-done.refs_0_, bf16[1024,128]{1,0:T(8,128)(2,1)} %bitcast.37, f32[2048,128]{1,0:T(8,128)} %place_children.2.refs_2_), custom_call_target="tpu_custom_call" | custom-call | tf_op jit(solution)/shard_map/place_children/pallas_call | solution.py:203
  175.9 0.0 collective-permute-done.16
  175.9 0.0 collective-permute-done.15
  175.9 0.0 collective-permute-done.14
  176.0 0.1 collective-permute-start.17
  176.1 1.5 collective-permute-done.17
  177.6 0.8 fusion
  (23 shorter events, 0.2 us)
Async XLA Ops:
  0.6 15.2 %collective-permute-start.1 = (bf16[2048,128]{1,0:T(8,128)(2,1)}, bf16[2048,128]{1,0:T(8,128)(2,1)S(1)}, u32[]{:S(2)}, u32[]{:S(2)}) collective-permute-start(bf16[2048,128]{1,0:T(8,128)(2,1)} %bitcast.58), channel_id=1, source_target_pairs={{2,0},{4,2},{6,4},{7,6},{5,7},{3,5},{1,3},{0,1},{10,8},{12,10},{14... | collective-permute-start | bytes 1572872 | tf_op jit(solution)/shard_map/ppermute | solution.py:494
  3.6 13.6 %collective-permute-start = (bf16[2048,128]{1,0:T(8,128)(2,1)}, bf16[2048,128]{1,0:T(8,128)(2,1)S(1)}, u32[]{:S(2)}, u32[]{:S(2)}) collective-permute-start(bf16[2048,128]{1,0:T(8,128)(2,1)} %bitcast.59), channel_id=1, source_target_pairs={{0,2},{2,4},{4,6},{6,7},{7,5},{5,3},{3,1},{1,0},{8,10},{10,12},{12... | collective-permute-start | bytes 1572872 | tf_op jit(solution)/shard_map/ppermute | solution.py:493
  15.8 3.4 %copy-start.3 = (bf16[2048,128]{1,0:T(8,128)(2,1)}, bf16[2048,128]{1,0:T(8,128)(2,1)S(1)}, u32[]{:S(2)}) copy-start(bf16[2048,128]{1,0:T(8,128)(2,1)S(1)} %collective-permute-done.1.refs_7_) | copy-start | bytes 1572868
  17.2 2.0 %copy-start.4 = (bf16[2048,128]{1,0:T(8,128)(2,1)}, bf16[2048,128]{1,0:T(8,128)(2,1)S(1)}, u32[]{:S(2)}) copy-start(bf16[2048,128]{1,0:T(8,128)(2,1)S(1)} %collective-permute-done.refs_6_) | copy-start | bytes 1572868
  17.2 12.5 %collective-permute-start.2 = (bf16[2048,128]{1,0:T(8,128)(2,1)S(1)}, bf16[2048,128]{1,0:T(8,128)(2,1)S(1)}, u32[]{:S(2)}, u32[]{:S(2)}) collective-permute-start(bf16[2048,128]{1,0:T(8,128)(2,1)S(1)} %collective-permute-done.refs_6_), channel_id=1, source_target_pairs={{0,2},{2,4},{4,6},{6,7},{7,5},{5,3},{3,1},{1,0},{8,10},{10,12},{12... | collective-permute-start | bytes 1572872 | tf_op jit(solution)/shard_map/ppermute | solution.py:493
  17.6 13.2 %collective-permute-start.3 = (bf16[2048,128]{1,0:T(8,128)(2,1)S(1)}, bf16[2048,128]{1,0:T(8,128)(2,1)S(1)}, u32[]{:S(2)}, u32[]{:S(2)}) collective-permute-start(bf16[2048,128]{1,0:T(8,128)(2,1)S(1)} %collective-permute-done.1.refs_7_), channel_id=1, source_target_pairs={{2,0},{4,2},{6,4},{7,6},{5,7},{3,5},{1,3},{0,1},{10,8},{12,10},{14... | collective-permute-start | bytes 1572872 | tf_op jit(solution)/shard_map/ppermute | solution.py:494
  29.8 7.5 %copy-start.5 = (bf16[2048,128]{1,0:T(8,128)(2,1)}, bf16[2048,128]{1,0:T(8,128)(2,1)S(1)}, u32[]{:S(2)}) copy-start(bf16[2048,128]{1,0:T(8,128)(2,1)S(1)} %collective-permute-done.2.refs_6_) | copy-start | bytes 1572868
  30.8 6.4 %copy-start.6 = (bf16[2048,128]{1,0:T(8,128)(2,1)}, bf16[2048,128]{1,0:T(8,128)(2,1)S(1)}, u32[]{:S(2)}) copy-start(bf16[2048,128]{1,0:T(8,128)(2,1)S(1)} %collective-permute-done.3.refs_7_) | copy-start | bytes 1572868
  30.8 14.9 %collective-permute-start.4 = (bf16[2048,128]{1,0:T(8,128)(2,1)S(1)}, bf16[2048,128]{1,0:T(8,128)(2,1)S(1)}, u32[]{:S(2)}, u32[]{:S(2)}) collective-permute-start(bf16[2048,128]{1,0:T(8,128)(2,1)S(1)} %collective-permute-done.2.refs_6_), channel_id=1, source_target_pairs={{0,2},{2,4},{4,6},{6,7},{7,5},{5,3},{3,1},{1,0},{8,10},{10,12},{12... | collective-permute-start | bytes 1572872 | tf_op jit(solution)/shard_map/ppermute | solution.py:493
  31.7 14.0 %collective-permute-start.5 = (bf16[2048,128]{1,0:T(8,128)(2,1)S(1)}, bf16[2048,128]{1,0:T(8,128)(2,1)S(1)}, u32[]{:S(2)}, u32[]{:S(2)}) collective-permute-start(bf16[2048,128]{1,0:T(8,128)(2,1)S(1)} %collective-permute-done.3.refs_7_), channel_id=1, source_target_pairs={{2,0},{4,2},{6,4},{7,6},{5,7},{3,5},{1,3},{0,1},{10,8},{12,10},{14... | collective-permute-start | bytes 1572872 | tf_op jit(solution)/shard_map/ppermute | solution.py:494
  45.7 7.7 %copy-start.1 = (bf16[2048,128]{1,0:T(8,128)(2,1)}, bf16[2048,128]{1,0:T(8,128)(2,1)S(1)}, u32[]{:S(2)}) copy-start(bf16[2048,128]{1,0:T(8,128)(2,1)S(1)} %collective-permute-done.4.refs_6_) | copy-start | bytes 1572868
  45.8 5.6 %copy-start.2 = (bf16[2048,128]{1,0:T(8,128)(2,1)}, bf16[2048,128]{1,0:T(8,128)(2,1)S(1)}, u32[]{:S(2)}) copy-start(bf16[2048,128]{1,0:T(8,128)(2,1)S(1)} %collective-permute-done.5.refs_7_) | copy-start | bytes 1572868
  45.8 55.9 %all-to-all-start.1 = ((bf16[8,1040,128]{2,1,0:T(8,128)(2,1)}), bf16[8,1040,128]{2,1,0:T(8,128)(2,1)S(1)}, u32[]{:S(2)}, u32[]{:S(2)}) async-start(bf16[8,1040,128]{2,1,0:T(8,128)(2,1)} %get-tuple-element.47), calls=%async_computation.1 | async-start | bytes 4259840 | tf_op jit(solution)/shard_map/all_to_all | solution.py:486
  51.3 31.4 %collective-permute-start.7 = (bf16[1024,128]{1,0:T(8,128)(2,1)S(1)}, bf16[1024,128]{1,0:T(8,128)(2,1)S(1)}, u32[]{:S(2)}, u32[]{:S(2)}) collective-permute-start(bf16[1024,128]{1,0:T(8,128)(2,1)S(1)} %slice.15), channel_id=1, source_target_pairs={{2,0},{4,2},{6,4},{7,6},{5,7},{3,5},{1,3},{0,1},{10,8},{12,10},{14... | collective-permute-start | bytes 786440 | tf_op jit(solution)/shard_map/ppermute | solution.py:494
  53.4 36.8 %collective-permute-start.6 = (bf16[1024,128]{1,0:T(8,128)(2,1)S(1)}, bf16[1024,128]{1,0:T(8,128)(2,1)S(1)}, u32[]{:S(2)}, u32[]{:S(2)}) collective-permute-start(bf16[1024,128]{1,0:T(8,128)(2,1)S(1)} %slice.14), channel_id=1, source_target_pairs={{0,2},{2,4},{4,6},{6,7},{7,5},{5,3},{3,1},{1,0},{8,10},{10,12},{12... | collective-permute-start | bytes 786440 | tf_op jit(solution)/shard_map/ppermute | solution.py:493
  82.7 19.0 %copy-start.7 = (bf16[1024,128]{1,0:T(8,128)(2,1)}, bf16[1024,128]{1,0:T(8,128)(2,1)S(1)}, u32[]{:S(2)}) copy-start(bf16[1024,128]{1,0:T(8,128)(2,1)S(1)} %collective-permute-done.7.refs_7_) | copy-start | bytes 786436
  90.2 11.5 %copy-start.8 = (bf16[1024,128]{1,0:T(8,128)(2,1)}, bf16[1024,128]{1,0:T(8,128)(2,1)S(1)}, u32[]{:S(2)}) copy-start(bf16[1024,128]{1,0:T(8,128)(2,1)S(1)} %collective-permute-done.6.refs_6_) | copy-start | bytes 786436
  101.7 13.2 %copy-start = (bf16[8,1040,128]{2,1,0:T(8,128)(2,1)}, bf16[8,1040,128]{2,1,0:T(8,128)(2,1)S(1)}, u32[]{:S(2)}) copy-start(bf16[8,1040,128]{2,1,0:T(8,128)(2,1)S(1)} %all-to-all-done.1.refs_0_) | copy-start | bytes 6389764
  101.7 65.4 %all-to-all-start = ((bf16[8,1040,128]{2,1,0:T(8,128)(2,1)}), bf16[8,1040,128]{2,1,0:T(8,128)(2,1)}, u32[]{:S(2)}, u32[]{:S(2)}) async-start(bf16[8,1040,128]{2,1,0:T(8,128)(2,1)} %get-tuple-element.45), calls=%async_computation | async-start | bytes 4259840 | tf_op jit(solution)/shard_map/all_to_all | solution.py:503
  114.9 2.1 %collective-permute-start.8 = (f32[512,128]{1,0:T(8,128)}, f32[512,128]{1,0:T(8,128)S(1)}, u32[]{:S(2)}, u32[]{:S(2)}) collective-permute-start(f32[512,128]{1,0:T(8,128)} %get-tuple-element.59), channel_id=1, source_target_pairs={{0,8},{8,0},{16,24},{24,16},{1,9},{9,1},{17,25},{25,17},{2,10},{10... | collective-permute-start | bytes 786440 | tf_op jit(solution)/shard_map/ppermute | solution.py:384
  137.8 6.6 %collective-permute-start.9 = (f32[256,128]{1,0:T(8,128)S(1)}, f32[256,128]{1,0:T(8,128)S(1)}, u32[]{:S(2)}, u32[]{:S(2)}) collective-permute-start(f32[256,128]{1,0:T(8,128)S(1)} %dynamic-slice_bitcast_fusion), channel_id=1, source_target_pairs={{0,16},{8,24},{16,0},{24,8},{1,17},{9,25},{17,1},{25,9},{2,18},{10... | collective-permute-start | bytes 393224 | tf_op jit(solution)/shard_map/ppermute | solution.py:384
  144.5 8.6 %collective-permute-start.10 = (f32[128,128]{1,0:T(8,128)S(1)}, f32[128,128]{1,0:T(8,128)S(1)}, u32[]{:S(2)}, u32[]{:S(2)}) collective-permute-start(f32[128,128]{1,0:T(8,128)S(1)} %dynamic-slice_bitcast_fusion.1), channel_id=1, source_target_pairs={{0,1},{1,0},{2,3},{3,2},{4,5},{5,4},{6,7},{7,6},{8,9},{9,8},{10,11... | collective-permute-start | bytes 196616 | tf_op jit(solution)/shard_map/ppermute | solution.py:384
  153.1 6.8 %collective-permute-start.13 = (f32[128,128]{1,0:T(8,128)S(1)}, f32[128,128]{1,0:T(8,128)S(1)}, u32[]{:S(2)}, u32[]{:S(2)}) collective-permute-start(f32[128,128]{1,0:T(8,128)S(1)} %bitcast_add_fusion.1), channel_id=1, source_target_pairs={{0,6},{1,7},{2,4},{3,5},{4,2},{5,3},{6,0},{7,1},{8,14},{9,15},{10,... | collective-permute-start | bytes 196616 | tf_op jit(solution)/shard_map/ppermute | solution.py:384
  157.4 6.1 %collective-permute-start.12 = (f32[128,128]{1,0:T(8,128)S(1)}, f32[128,128]{1,0:T(8,128)S(1)}, u32[]{:S(2)}, u32[]{:S(2)}) collective-permute-start(f32[128,128]{1,0:T(8,128)S(1)} %bitcast_add_fusion.1), channel_id=1, source_target_pairs={{0,4},{1,5},{2,6},{3,7},{4,0},{5,1},{6,2},{7,3},{8,12},{9,13},{10,... | collective-permute-start | bytes 196616 | tf_op jit(solution)/shard_map/ppermute | solution.py:384
  157.8 5.8 %collective-permute-start.11 = (f32[128,128]{1,0:T(8,128)S(1)}, f32[128,128]{1,0:T(8,128)S(1)}, u32[]{:S(2)}, u32[]{:S(2)}) collective-permute-start(f32[128,128]{1,0:T(8,128)S(1)} %bitcast_add_fusion.1), channel_id=1, source_target_pairs={{0,2},{1,3},{2,0},{3,1},{4,6},{5,7},{6,4},{7,5},{8,10},{9,11},{10,... | collective-permute-start | bytes 196616 | tf_op jit(solution)/shard_map/ppermute | solution.py:384
  163.6 12.3 %collective-permute-start.16 = (f32[128,128]{1,0:T(8,128)S(1)}, f32[128,128]{1,0:T(8,128)S(1)}, u32[]{:S(2)}, u32[]{:S(2)}) collective-permute-start(f32[128,128]{1,0:T(8,128)S(1)} %add_add_fusion), channel_id=1, source_target_pairs={{0,1},{1,0},{2,3},{3,2},{4,5},{5,4},{6,7},{7,6},{8,9},{9,8},{10,11... | collective-permute-start | bytes 196616 | tf_op jit(solution)/shard_map/ppermute | solution.py:384
  164.8 11.1 %collective-permute-start.15 = (f32[128,128]{1,0:T(8,128)S(1)}, f32[128,128]{1,0:T(8,128)S(1)}, u32[]{:S(2)}, u32[]{:S(2)}) collective-permute-start(f32[128,128]{1,0:T(8,128)S(1)} %add_add_fusion), channel_id=1, source_target_pairs={{0,16},{8,24},{16,0},{24,8},{1,17},{9,25},{17,1},{25,9},{2,18},{10... | collective-permute-start | bytes 196616 | tf_op jit(solution)/shard_map/ppermute | solution.py:384
  167.0 8.9 %collective-permute-start.14 = (f32[128,128]{1,0:T(8,128)S(1)}, f32[128,128]{1,0:T(8,128)S(1)}, u32[]{:S(2)}, u32[]{:S(2)}) collective-permute-start(f32[128,128]{1,0:T(8,128)S(1)} %add_add_fusion), channel_id=1, source_target_pairs={{0,17},{1,16},{2,19},{3,18},{4,21},{5,20},{6,23},{7,22},{8,25},{9,... | collective-permute-start | bytes 196616 | tf_op jit(solution)/shard_map/ppermute | solution.py:415
  176.0 1.6 collective-permute-start.17
